TPU v7x, 256 devices: a whole 4x4x8 slice. The times are simulated.
256 devices in a mesh: rep: 16 (over y, z_lo), tp: 16 (over x, z_hi, core).
Axes of the slice: x: 4, y: 4, z: 8 (z_hi: 2, z_lo: 4; z = z_hi * 4 + z_lo), core: 2. Of those that a mesh axis runs over, the one named last changes fastest.
Arguments:
- replica_weights: bfloat16 [16, 7168, 3584], P('rep', 'tp'), may hold values from -6 to 6
- slow_weights: float32 [7168, 3584], P('tp', 'rep'), may hold values from -6 to 6
- momentum: float32 [7168, 3584], P('tp', 'rep'), may hold values from -2 to 2
- hidden: bfloat16 [16, 2, 256, 7168], P('rep', None, None, 'tp'), may hold values from -6 to 6
- residual: bfloat16 [16, 2, 3584, 256], P('rep', None, 'tp'), may hold values from -60 to 60
- target: bfloat16 [16, 2, 3584, 256], P('rep', None, 'tp'), may hold values from -6 to 6
- arrival: int32 [16], replicated, may hold values from 0 to 15, each once
- staleness: int32 [16], replicated, may hold values from 0 to 4, as said below
- live: int32 [16], replicated, may hold values from 1 to 256, 2048 in all
Outputs:
- returned: bfloat16 [16, 7168, 3584], P('rep', 'tp')
- slow_after: float32 [7168, 3584], P('tp', 'rep')
- momentum_after: float32 [7168, 3584], P('tp', 'rep')
Inputs may be any that keep to these rules, and one draw needn't show every extreme that they name: `staleness`: every value from 0 to 4 occurs. `arrival`: a permutation of the replicas. The live counts sum to 2048, and some replica has all 256 tokens live.
All inputs are finite; a program needn't handle non-finite values.
Results may differ from a plain program's by a relative error of at most 0.008.
Values may be sent and summed in bfloat16 or wider, within the bound.
No kernel may reach another device: no remote copies, remote signals or barrier semaphores. Data moves between devices by JAX's collectives and lax.ppermute only.
A program may use at most 128 MiB of HBM per device.

v0:
```python
import math

import jax
import jax.numpy as jnp
from jax import lax
from jax.sharding import PartitionSpec as P

D = 3584
FF = 7168
ITERS = 2


inner_rate = 2.0
outer_rate = 0.7
momentum_decay = 0.9
epsilon = 1e-06


def normal_grad(summed, target_now, sum_squares, sum_cross, token_mask):
    rms = jnp.sqrt(sum_squares / D + epsilon)
    along = sum_cross / D / rms
    return (token_mask * (target_now - summed / rms * along) / rms).astype(jnp.bfloat16)


def local(
    replica_weights, slow_weights, momentum, hidden, residual, target, arrival, staleness, live
):
    replicas = arrival.shape[0]
    tokens = residual.shape[3]
    inv_width = 1.0 / math.sqrt(FF)
    contract_first = (((0,), (1,)), ((), ()))
    replica_index = lax.axis_index("rep")
    slots = jnp.arange(replicas, dtype=jnp.int32)
    live_count = jnp.sum(jnp.where(slots == replica_index, live, 0))
    token_mask = (jnp.arange(tokens, dtype=jnp.int32) < live_count).astype(jnp.float32)
    start_weights = replica_weights[0]
    current = start_weights.astype(jnp.float32)
    for inner_step in range(ITERS):
        features = hidden[0, inner_step]
        narrow = current.astype(jnp.bfloat16)
        output = lax.psum_scatter(
            (
                lax.dot_general(
                    narrow, features, contract_first, preferred_element_type=jnp.float32
                )
                * inv_width
            ).astype(jnp.bfloat16),
            "tp",
            scatter_dimension=0,
            tiled=True,
        ).astype(jnp.float32)
        summed = residual[0, inner_step].astype(jnp.float32) + output
        target_now = target[0, inner_step].astype(jnp.float32)
        sum_squares, sum_cross = lax.psum(
            (jnp.sum(summed * summed, axis=0), jnp.sum(target_now * summed, axis=0)), "tp"
        )
        grad_rows = normal_grad(summed, target_now, sum_squares, sum_cross, token_mask)
        update = lax.dot_general(
            features,
            lax.all_gather(grad_rows, "tp", axis=0, tiled=True),
            contract_first,
            preferred_element_type=jnp.float32,
        )
        current = current - inner_rate * inv_width * update
    delta = (start_weights.astype(jnp.float32) - current).astype(jnp.bfloat16)
    incoming = lax.all_to_all(delta[None], "rep", split_axis=2, concat_axis=0, tiled=True)
    ordered = jnp.take(incoming, arrival, axis=0)
    factors = 1.0 / (1.0 + staleness.astype(jnp.float32))

    def advance(carry, inputs):
        slow_now, held = carry
        portion, factor = inputs
        outer_grad = portion.astype(jnp.float32) * factor
        held = momentum_decay * held + outer_grad
        slow_now = slow_now - outer_rate * (outer_grad + momentum_decay * held)
        return ((slow_now, held), slow_now.astype(jnp.bfloat16))

    (slow_after, momentum_after), results = lax.scan(
        advance, (slow_weights, momentum), (ordered, factors)
    )
    position = jnp.sum(jnp.where(arrival[None, :] == slots[:, None], slots[None, :], 0), axis=1)
    by_replica = jnp.take(results, position, axis=0)
    returned = lax.all_to_all(by_replica, "rep", split_axis=0, concat_axis=2, tiled=True)
    return (returned, slow_after, momentum_after)


def solution(mesh):
    return jax.shard_map(
        local,
        mesh=mesh,
        in_specs=(
            P("rep", "tp", None),
            P("tp", "rep"),
            P("tp", "rep"),
            P("rep", None, None, "tp"),
            P("rep", None, "tp", None),
            P("rep", None, "tp", None),
            P(),
            P(),
            P(),
        ),
        out_specs=(P("rep", "tp", None), P("tp", "rep"), P("tp", "rep")),
        check_vma=False,
    )
```

profile of v0, /device:TPU:1, one launch (start us, length us, event | category | flops | bytes accessed | tf_op | source)
XLA Modules:
  0.0 728.6 jit_solution(6059518821562816613)
XLA Ops:
  7.2 4.5 fusion.4
  12.5 0.6 compare_convert_fusion
  13.1 87.4 %reduce-scatter.3.cloned.1.call-done = bf16[224,256]{1,0:T(8,128)(2,1)} async-done(((bf16[3584,256]{1,0:T(8,128)(2,1)}), bf16[224,256]{1,0:T(8,128)(2,1)}) %reduce-scatter.3.cloned.1.call-update) | async-done | bytes 114704 | tf_op jit(solution)/shard_map/reduce_scatter | solution.py:41
  100.5 1.0 multiply_reduce_fusion.1
  101.6 44.3 %all-reduce.1 = (f32[256]{0:T(256)S(1)}, f32[256]{0:T(256)S(1)}) all-reduce(f32[256]{0:T(256)S(1)} %get-tuple-element.44, f32[256]{0:T(256)S(1)} %get-tuple-element.43), channel_id=1, replica_groups=mesh['rep'=16,'tp'=16] {'tp'}, use_global_device_ids=true, to_apply=%region_5.6 | all-reduce | flops 512 | bytes 4096 | tf_op jit(solution)/shard_map/psum | solution.py:54
  145.9 1.7 fusion.11
  147.6 57.3 %all-gather.3.cloned.1.call-done = bf16[3584,256]{1,0:T(8,128)(2,1)} async-done(((bf16[224,256]{1,0:T(8,128)(2,1)}), bf16[3584,256]{1,0:T(8,128)(2,1)}) %all-gather.3.cloned.1.call-update) | async-done | bytes 1835024 | tf_op jit(solution)/shard_map/all_gather | solution.py:60
  204.9 2.6 convert_subtract_fusion.1
  207.5 2.7 copy-done
  210.2 2.5 fusion.5
  212.8 79.3 %reduce-scatter.5.cloned.1.call-done = bf16[224,256]{1,0:T(8,128)(2,1)} async-done(((bf16[3584,256]{1,0:T(8,128)(2,1)}), bf16[224,256]{1,0:T(8,128)(2,1)}) %reduce-scatter.5.cloned.1.call-update) | async-done | bytes 114704 | tf_op jit(solution)/shard_map/reduce_scatter | solution.py:41
  292.0 1.0 multiply_reduce_fusion
  293.1 44.2 %all-reduce = (f32[256]{0:T(256)S(1)}, f32[256]{0:T(256)S(1)}) all-reduce(f32[256]{0:T(256)S(1)} %get-tuple-element.42, f32[256]{0:T(256)S(1)} %get-tuple-element.41), channel_id=1, replica_groups=mesh['rep'=16,'tp'=16] {'tp'}, use_global_device_ids=true, to_apply=%region_10.11 | all-reduce | flops 512 | bytes 4096 | tf_op jit(solution)/shard_map/psum | solution.py:54
  337.3 1.7 fusion.15
  339.0 57.3 %all-gather.5.cloned.1.call-done = bf16[3584,256]{1,0:T(8,128)(2,1)} async-done(((bf16[224,256]{1,0:T(8,128)(2,1)}), bf16[3584,256]{1,0:T(8,128)(2,1)}) %all-gather.5.cloned.1.call-update) | async-done | bytes 1835024 | tf_op jit(solution)/shard_map/all_gather | solution.py:60
  396.3 6.4 fusion.3
  402.7 16.3 %copy.21 = bf16[1,448,3584]{1,0,2:T(2,128)(2,1)} copy(bf16[1,448,3584]{2,1,0:T(8,128)(2,1)} %fusion.3) | data formatting | bytes 6422528 | tf_op jit(solution)/shard_map/broadcast_in_dim | solution.py:66
  419.5 25.4 %reduce = bf16[3584,448]{1,0:T(8,128)(2,1)} reduce(bf16[3584,1,448]{2,1,0:T(2,128)(2,1)} %bitcast.72, bf16[]{:T(256)} %broadcast.116), dimensions={1}, to_apply=%bitcast.62.reduce_sub_computation | reduce | bytes 6422530
  444.9 8.1 %reshape.59 = bf16[16,2,50176]{2,1,0:T(2,128)(2,1)} reshape(bf16[3584,448]{1,0:T(8,128)(2,1)} %reduce) | data formatting | bytes 6422528
  453.1 4.3 all-to-all-start
  457.6 76.0 %all-to-all-done = bf16[16,2,50176]{2,1,0:T(2,128)(2,1)S(1)} async-done(((bf16[16,2,50176]{2,1,0:T(2,128)(2,1)}), bf16[16,2,50176]{2,1,0:T(2,128)(2,1)S(1)}, u32[]{:S(2)}, u32[]{:S(2)}) %all-to-all-start) | async-done | bytes 3211296 | tf_op jit(solution)/shard_map/all_to_all | solution.py:66
  533.7 8.9 %reshape.60 = bf16[3584,1,448]{2,1,0:T(2,128)(2,1)} reshape(bf16[16,2,50176]{2,1,0:T(2,128)(2,1)S(1)} %all-to-all-done) | data formatting | bytes 6422528
  542.6 6.1 copy.27
  548.6 6.1 copy.23
  554.7 4.6 gather_fusion
  559.4 4.4 broadcast_select_fusion.1
  563.8 52.0 %while.14 = (s32[]{:T(128)}, f32[448,224]{1,0:T(8,128)S(1)}, f32[448,224]{1,0:T(8,128)S(1)}, bf16[16,448,224]{2,1,0:T(8,128)(2,1)}, bf16[16,448,224]{2,1,0:T(8,128)(2,1)}, /*index=5*/f32[16]{0:T(128)S(1)}, s32[]{:T(128)}) while((s32[]{:T(128)}, f32[448,224]{1,0:T(8,128)S(1)}, f32[448,224]{1,0:T(8,128)S(1)}, ...), condition=%wide.region_12.14_spmd, body=%wide.region_11.13_spmd.sunk | while | flops 903170 | bytes 2065497 | solution.py:78
  564.3 2.7 bitcast_dynamic-update-slice_fusion.2
  567.6 2.6 bitcast_dynamic-update-slice_fusion.2
  570.8 2.7 bitcast_dynamic-update-slice_fusion.2
  574.1 2.7 bitcast_dynamic-update-slice_fusion.2
  577.3 2.7 bitcast_dynamic-update-slice_fusion.2
  580.6 2.7 bitcast_dynamic-update-slice_fusion.2
  583.9 2.7 bitcast_dynamic-update-slice_fusion.2
  587.1 2.6 bitcast_dynamic-update-slice_fusion.2
  590.3 2.7 bitcast_dynamic-update-slice_fusion.2
  593.6 2.7 bitcast_dynamic-update-slice_fusion.2
  596.9 2.7 bitcast_dynamic-update-slice_fusion.2
  600.1 2.7 bitcast_dynamic-update-slice_fusion.2
  603.3 2.6 bitcast_dynamic-update-slice_fusion.2
  606.6 2.7 bitcast_dynamic-update-slice_fusion.2
  609.8 2.7 bitcast_dynamic-update-slice_fusion.2
  613.0 2.7 bitcast_dynamic-update-slice_fusion.2
  615.7 4.9 gather_fusion.1
  620.7 2.4 broadcast_select_fusion
  623.1 87.0 %all_to_all.36 = bf16[16,448,224]{2,1,0:T(8,128)(2,1)S(1)} all-to-all(bf16[16,448,224]{2,1,0:T(8,128)(2,1)S(1)} %broadcast_select_fusion), channel_id=1, replica_groups=mesh['rep'=16,'tp'=16] {'rep'}, dimensions={0} | all-to-all | bytes 6422528 | tf_op jit(solution)/shard_map/all_to_all | solution.py:83
  710.2 3.9 copy.24
  714.1 8.0 %all_to_all.33 = bf16[1,448,3584]{2,1,0:T(8,128)(2,1)} reshape(bf16[1,448,16,224]{3,2,1,0:T(8,128)(2,1)} %copy.24) | data formatting | bytes 6422528 | tf_op jit(solution)/shard_map/all_to_all | solution.py:83
  (58 shorter events, 10.9 us)
Async XLA Ops:
  7.2 93.4 %reduce-scatter.3.cloned.1.call-start = ((), (), s32[]{:S(2)}) async-start(), calls=%async_computation.4 | async-start | bytes 1949696 | tf_op jit(solution)/shard_map/reduce_scatter | solution.py:41
  7.2 4.6 copy-start.8
  7.2 93.3 %copy-start.7 = (bf16[1,2,224,256]{3,2,1,0:T(8,128)(2,1)S(1)}, bf16[1,2,224,256]{3,2,1,0:T(8,128)(2,1)}, u32[]{:S(2)}) copy-start(bf16[1,2,224,256]{3,2,1,0:T(8,128)(2,1)} %param.17) | copy-start | bytes 688132
  7.2 197.7 %copy-start.1 = (bf16[1,448,3584]{2,1,0:T(8,128)(2,1)S(1)}, bf16[1,448,3584]{2,1,0:T(8,128)(2,1)}, u32[]{:S(2)}) copy-start(bf16[1,448,3584]{2,1,0:T(8,128)(2,1)} %param.13) | copy-start | bytes 9633796
  11.8 193.1 %all-gather.3.cloned.1.call-start = ((), (), s32[]{:S(2)}) async-start(), calls=%async_computation.5 | async-start | bytes 1949696 | tf_op jit(solution)/shard_map/all_gather | solution.py:60
  147.6 144.5 %reduce-scatter.5.cloned.1.call-start = ((), (), s32[]{:S(2)}) async-start(), calls=%async_computation.6 | async-start | bytes 1949696 | tf_op jit(solution)/shard_map/reduce_scatter | solution.py:41
  204.9 5.3 copy-start.6
  207.5 2.7 copy-start
  212.7 183.6 %all-gather.5.cloned.1.call-start = ((), (), s32[]{:S(2)}) async-start(), calls=%async_computation.7 | async-start | bytes 1949696 | tf_op jit(solution)/shard_map/all_gather | solution.py:60
  453.1 4.3 copy-start.9
  453.1 4.5 copy-start.10
  453.1 80.6 %all-to-all-start = ((bf16[16,2,50176]{2,1,0:T(2,128)(2,1)}), bf16[16,2,50176]{2,1,0:T(2,128)(2,1)S(1)}, u32[]{:S(2)}, u32[]{:S(2)}) async-start(bf16[16,2,50176]{2,1,0:T(2,128)(2,1)} %reshape.59), calls=%async_computation.2 | async-start | bytes 6422528 | tf_op jit(solution)/shard_map/all_to_all | solution.py:66
  559.4 4.4 copy-start.3
  559.4 4.4 copy-start.5
  615.7 4.9 copy-start.2
  615.7 4.9 copy-start.4
Sparse Core Ops, SparseCore 0:
  12.8 87.7 reduce-scatter.2
  147.7 57.1 all-gather.2
  212.8 79.1 reduce-scatter.4
  339.1 57.1 all-gather.4
where the time goes:
time: 731 us; the launch traced here: 729 us
  waiting for transfers between devices  357 us (49%)
  blocking collectives  175 us (24%)
  other arithmetic  81.7 us (11%)
  local copies, waits for them, and re-layouts  79.6 us (11%)
  matrix products  15.9 us (2%)
  between operations  13.9 us (2%)
    reduce_scatter x2, waiting for transfers between devices, local(): lax.psum_scatter((lax.dot_general(narrow, features, contract_first, prefe...  167 us
    all_gather x2, waiting for transfers between devices, local(): lax.all_gather(grad_rows, 'tp', axis=0, tiled=True)  115 us
    psum x2, blocking collectives, local(): lax.psum((jnp.sum(summed * summed, axis=0), jnp.sum(target_now * summed,...  88.5 us
    all_to_all x1, blocking collectives, local(): lax.all_to_all(by_replica, 'rep', split_axis=0, concat_axis=2, tiled=True)  87 us
    all_to_all x1, waiting for transfers between devices, local(): lax.all_to_all(delta[None], 'rep', split_axis=2, concat_axis=0, tiled=True)  76 us
    dynamic_update_slice x16, other arithmetic, local(): lax.scan(advance, (slow_weights, momentum), (ordered, factors))  42.6 us
    unnamed x26, local copies, waits for them, and re-layouts  26.4 us
    unnamed x1, other arithmetic  25.4 us
  transfers between devices with their start and end apart: 5, of which 5 were waited for; matrix products, arithmetic and copies ran while one was open for 0% of the time, Pallas kernels for 0%

commit v1 on v0

v1 whole, which is shorter than its diff:
```python
import itertools
import math

import jax
import jax.numpy as jnp
from jax import lax
from jax.experimental import pallas as pl
from jax.experimental.pallas import tpu as pltpu
from jax.sharding import Mesh
from jax.sharding import PartitionSpec as P

D = 3584
FF = 7168
TOK = 256
ITERS = 2
REPLICAS = 16
ROWS = 448
COLS = 224
WIDE = 896
PACKED = 784

inner_rate = 2.0
outer_rate = 0.7
momentum_decay = 0.9
epsilon = 1e-06

AXES = ("y", "b", "a", "x", "h", "c")
SIZES = (4, 2, 2, 4, 2, 2)
F32 = jnp.float32
BF16 = jnp.bfloat16


def flat(*where):
    index = 0
    for size, place in zip(SIZES, where):
        index = index * size + place
    return index


def devices():
    return itertools.product(*map(range, SIZES))


def swap(value, axis):
    return lax.ppermute(value, axis, [(0, 1), (1, 0)])


def ring(value, axis, mask):
    return lax.ppermute(value, axis, [(i, i ^ mask) for i in range(4)])


def line(value, mask):
    return lax.ppermute(value, ("b", "a"), [(i, i ^ mask) for i in range(4)])


def pick(array, index, axis=0):
    return lax.dynamic_index_in_dim(array, index, axis, keepdims=False)


def forward_kernel(rows_ref, weights_ref, out_ref):
    out_ref[0] = (
        jnp.dot(rows_ref[...], weights_ref[...], preferred_element_type=F32)
        * (1.0 / math.sqrt(FF))
    ).astype(BF16)


def forward(rows, weights):
    count = rows.shape[0]
    return pl.pallas_call(
        forward_kernel,
        grid=(4,),
        in_specs=[
            pl.BlockSpec((count, ROWS), lambda i: (0, 0)),
            pl.BlockSpec((ROWS, WIDE), lambda i: (0, i)),
        ],
        out_specs=pl.BlockSpec((1, count, WIDE), lambda i: (i, 0, 0)),
        out_shape=jax.ShapeDtypeStruct((4, count, WIDE), BF16),
        cost_estimate=pl.CostEstimate(
            flops=2 * count * ROWS * D, bytes_accessed=2 * ROWS * D, transcendentals=0
        ),
        compiler_params=pltpu.CompilerParams(vmem_limit_bytes=32 << 20),
        name="forward",
    )(rows, weights)


def reduce_tokens(keep, send, extra_keep, extra_send, x, h):
    got = swap(send, "c")
    extra = None
    if extra_keep is not None:
        extra_got = swap(extra_send, "c")
        extra = extra_keep.astype(F32) + extra_got.astype(F32)

    def block(index, half):
        rows = slice(64 * half, 64 * half + 64)
        return pick(keep, index)[rows].astype(F32) + pick(got, index)[rows].astype(F32)

    ends = []
    for half, first, second in ((0, 1, 3), (1, 3, 1)):
        parts = [block(x ^ first, half), block(x ^ 2, half)]
        mine = [block(x, half), block(x ^ second, half)]
        if extra is not None:
            own = extra[64 * half : 64 * half + 64]
            parts.append(own)
            mine.append(own)
        step = ring(jnp.concatenate(parts, axis=1).astype(BF16), "x", first).astype(F32)
        total = jnp.concatenate(mine, axis=1) + step
        step = ring(total[:, WIDE:].astype(BF16), "x", second).astype(F32)
        own = total[:, :WIDE] + step[:, :WIDE]
        if extra is not None:
            own = jnp.concatenate([own, total[:, 2 * WIDE :] + step[:, WIDE:]], axis=1)
        ends.append(own)
    low = h == 0
    last = swap(jnp.where(low, ends[1], ends[0]).astype(BF16), "h").astype(F32)
    return jnp.where(low, ends[0], ends[1]) + last


def redistribute(residual, target, h, c):
    both = jnp.concatenate([residual, target], axis=0)
    both = jnp.swapaxes(both, 1, 2).reshape(4, 2, 2, 64, COLS)
    near = pick(both, h, 2)
    far = swap(pick(both, 1 - h, 2), "h")
    got = swap(jnp.stack([pick(near, 1 - c, 1), pick(far, 1 - c, 1)]), "c")
    near, far = pick(near, c, 1), pick(far, c, 1)
    first = c == 0
    near = [jnp.where(first, near, got[0]), jnp.where(first, got[0], near)]
    far = [jnp.where(first, far, got[1]), jnp.where(first, got[1], far)]
    low = h == 0
    return jnp.concatenate(
        [jnp.where(low, n, f) for n, f in zip(near, far)]
        + [jnp.where(low, f, n) for n, f in zip(near, far)],
        axis=-1,
    )


def over_ring(value):
    return value + ring(value, "x", 1) + ring(value, "x", 2) + ring(value, "x", 3)


def normal_grad(summed, target_now, token_mask):
    sums = over_ring(
        jnp.stack([jnp.sum(summed * summed, axis=1), jnp.sum(target_now * summed, axis=1)])
    )
    rms = jnp.sqrt(sums[0] / D + epsilon)
    along = sums[1] / D / rms
    rms, along = rms[:, None], along[:, None]
    return (token_mask * (target_now - summed / rms * along) / rms).astype(BF16)


def in_order(own, other, index, axis):
    first = index == 0
    return jnp.stack([jnp.where(first, own, other), jnp.where(first, other, own)], axis=axis)


def to_owners(chunks, b, h):
    parts = [[None, None], [None, None]]
    for m1, m2 in itertools.product(range(2), range(2)):
        pairs = [
            (flat(y, b_, a, x, h_, c), flat(x, b_ ^ m1, c, y, h_ ^ m2, a))
            for y, b_, a, x, h_, c in devices()
        ]
        parts[m1][m2] = lax.ppermute(pick(chunks, b ^ m1), AXES, pairs)
    held = jnp.stack(
        [in_order(p.reshape(2, 64, COLS), q.reshape(2, 64, COLS), h, 1).reshape(TOK, COLS) for p, q in parts]
    )
    near = [held] + [ring(held, "x", k) for k in (1, 2, 3)]
    return near + [swap(v, "c") for v in near]


def gather_rows(rows):
    return jnp.stack([rows] + [line(rows, k) for k in (1, 2, 3)])


def pack(block):
    top, rest = block[:, :128], block[:, 128:]
    last = rest[336:]
    groups = [
        jnp.concatenate([rest[112 * q : 112 * q + 112], last[:, 32 * q : 32 * q + 32]], axis=1)
        for q in range(3)
    ]
    return jnp.concatenate([top] + groups, axis=0)


def unpack(block):
    groups = [block[448 + 112 * q : 560 + 112 * q] for q in range(3)]
    last = jnp.concatenate([g[:, 96:] for g in groups], axis=1)
    rest = jnp.concatenate([g[:, :96] for g in groups] + [last], axis=0)
    return jnp.concatenate([block[:ROWS], rest], axis=1)


def outer_kernel(place, position, arrival, factors, slow_ref, held_ref, *refs):
    grads = refs[:16]
    rows = refs[16:24]
    out_ref, slow_out, held_out, g_ref, d_ref, s_ref, m_ref, sems = refs[24:]
    copies = [
        pltpu.make_async_copy(grads[8 * i + j], g_ref.at[j, :, i], sems.at[8 * i + j])
        for i in range(ITERS)
        for j in range(8)
    ]
    for copy in copies:
        copy.start()
    s_ref[...] = pack(slow_ref[...])
    m_ref[...] = pack(held_ref[...])
    for copy in copies:
        copy.wait()
    scale = inner_rate / math.sqrt(FF)
    y, b, a, x, c = (place[i] for i in range(5))
    for ky, slot in ((0, 0), (1, 1), (3, 2), (2, 3)):
        for kz in range(4):
            ry, rb, ra = y ^ ky, b ^ (kz // 2), a ^ (kz % 2)
            replica = ry * 4 + rb * 2 + ra
            buffer = (ra ^ c) * 4 + (ry ^ x)
            parts = []
            for half in range(2):
                block = rows[4 * half + slot]
                total = jnp.dot(
                    block[kz, :, :TOK], g_ref[buffer, rb ^ b, 0], preferred_element_type=F32
                ) + jnp.dot(
                    block[kz, :, TOK:], g_ref[buffer, rb ^ b, 1], preferred_element_type=F32
                )
                parts.append(total)
            d_ref[position[replica]] = pack(jnp.concatenate(parts, axis=0) * scale)

    def step(k, _):
        factor = factors[k]
        target = arrival[k]
        for at in range(0, PACKED, 112):
            here = pl.ds(at, 112)
            grad = d_ref[k, here] * factor
            held = momentum_decay * m_ref[here] + grad
            slow = s_ref[here] - outer_rate * (grad + momentum_decay * held)
            m_ref[here] = held
            s_ref[here] = slow
            out_ref[target, here] = slow.astype(BF16)
        return 0

    lax.fori_loop(0, REPLICAS, step, 0)
    slow_out[...] = unpack(s_ref[...])
    held_out[...] = unpack(m_ref[...])


def outer(place, position, arrival, factors, slow, held, grads, rows):
    smem = pl.BlockSpec(memory_space=pltpu.SMEM)
    vmem = pl.BlockSpec(memory_space=pltpu.VMEM)
    return pl.pallas_call(
        outer_kernel,
        in_specs=[smem] * 4 + [vmem] * 2 + [pl.BlockSpec(memory_space=pl.ANY)] * 16 + [vmem] * 8,
        out_specs=[vmem] * 3,
        out_shape=[
            jax.ShapeDtypeStruct((REPLICAS, PACKED, 128), BF16),
            jax.ShapeDtypeStruct((ROWS, COLS), F32),
            jax.ShapeDtypeStruct((ROWS, COLS), F32),
        ],
        scratch_shapes=[
            pltpu.VMEM((8, 2, ITERS, TOK, COLS), BF16),
            pltpu.VMEM((REPLICAS, PACKED, 128), F32),
            pltpu.VMEM((PACKED, 128), F32),
            pltpu.VMEM((PACKED, 128), F32),
            pltpu.SemaphoreType.DMA((16,)),
        ],
        compiler_params=pltpu.CompilerParams(vmem_limit_bytes=56 << 20),
        name="outer",
    )(place, position, arrival, factors, slow, held, *grads, *rows)


def assemble_kernel(in_ref, out_ref):
    blocks = [unpack(in_ref[i].astype(F32)) for i in range(4)]
    out_ref[...] = jnp.concatenate(blocks, axis=1).astype(BF16)


def assemble(blocks):
    return pl.pallas_call(
        assemble_kernel,
        grid=(4,),
        in_specs=[pl.BlockSpec((4, PACKED, 128), lambda i: (i, 0, 0))],
        out_specs=pl.BlockSpec((ROWS, WIDE), lambda i: (0, i)),
        out_shape=jax.ShapeDtypeStruct((ROWS, D), BF16),
        compiler_params=pltpu.CompilerParams(vmem_limit_bytes=32 << 20),
        name="assemble",
    )(blocks)


def local(
    replica_weights, slow_weights, momentum, hidden, residual, target, arrival, staleness, live
):
    y, b, a, x, h, c = (lax.axis_index(name) for name in AXES)
    weights, features = replica_weights[0], hidden[0]

    by_core = features.reshape(ITERS, 2, 128, ROWS)
    others, mine = pick(by_core, 1 - c, 1), pick(by_core, c, 1)
    send_first = forward(others[0], weights)
    keep_first = forward(mine[0], weights)
    first_output = reduce_tokens(keep_first, send_first, None, None, x, h)
    send_second = forward(others[1], weights)
    keep_second = forward(mine[1], weights)
    cross = [
        (
            lax.dot_general(
                rows[1], features[0], (((1,), (1,)), ((), ())), preferred_element_type=F32
            )
            * (inner_rate / FF)
        ).astype(BF16)
        for rows in (mine, others)
    ]
    second = reduce_tokens(keep_second, send_second, cross[0], cross[1], x, h)
    second_output, cross_rows = second[:, :WIDE], second[:, WIDE:].astype(BF16)

    turned = jnp.transpose(features, (2, 0, 1)).reshape(ROWS, ITERS * TOK)
    rows = []
    for half, (near, next_) in enumerate(((1, 3), (3, 1))):
        own = gather_rows(turned[COLS * half : COLS * half + COLS])
        one = ring(own, "y", near)
        two = ring(own, "y", next_)
        both = ring(one, "y", next_)
        rows += [own, one, two, both] if near == 1 else [own, two, one, both]

    streams = redistribute(residual[0], target[0], h, c).astype(F32)
    slots = jnp.arange(REPLICAS, dtype=jnp.int32)
    live_count = jnp.sum(jnp.where(slots == y * 4 + b * 2 + a, live, 0))
    token = c * 128 + h * 64 + jnp.arange(64, dtype=jnp.int32)
    token_mask = (token < live_count).astype(F32)[:, None]

    first_grad = normal_grad(streams[0] + first_output, streams[2], token_mask)
    by_h = in_order(first_grad, swap(first_grad, "h"), h, 0)
    all_first = in_order(by_h, swap(by_h, "c"), c, 0).reshape(TOK, WIDE)
    change = jnp.dot(cross_rows, all_first, preferred_element_type=F32)
    second_grad = normal_grad(streams[1] + (second_output - change), streams[3], token_mask)

    first_chunks = pick(
        pick(all_first.reshape(2, 2, 64, 2, 2, COLS), h, 1), c, 3
    )
    first_chunks = jnp.transpose(first_chunks, (2, 0, 1, 3)).reshape(2, 128, COLS)
    by_core = second_grad.reshape(64, 2, 2, COLS)
    second_chunks = in_order(pick(by_core, c, 2), swap(pick(by_core, 1 - c, 2), "c"), c, 0)
    second_chunks = jnp.transpose(second_chunks, (2, 0, 1, 3)).reshape(2, 128, COLS)
    grads = to_owners(first_chunks, b, h) + to_owners(second_chunks, b, h)

    position = jnp.sum(jnp.where(arrival[None, :] == slots[:, None], slots[None, :], 0), axis=1)
    factors = 1.0 / (1.0 + staleness.astype(F32))
    place = jnp.stack([y, b, a, x, c]).astype(jnp.int32)
    results, slow_after, momentum_after = outer(
        place, position.astype(jnp.int32), arrival, factors, slow_weights, momentum, grads, rows
    )
    back = lax.all_to_all(results, ("y", "b", "a"), 0, 0, tiled=True)
    return (assemble(back)[None], slow_after, momentum_after)


def solution(mesh):
    rep, tp = AXES[:3], AXES[3:]
    fine = Mesh(mesh.devices.reshape(SIZES), AXES)
    return jax.shard_map(
        local,
        mesh=fine,
        in_specs=(
            P(rep, tp, None),
            P(tp, rep),
            P(tp, rep),
            P(rep, None, None, tp),
            P(rep, None, tp, None),
            P(rep, None, tp, None),
            P(),
            P(),
            P(),
        ),
        out_specs=(P(rep, tp, None), P(tp, rep), P(tp, rep)),
        check_vma=False,
    )
```

time: 731 us -> 347 us (0.47)
  waiting for transfers between devices: 357 us -> 70 us
  starting transfers between devices: 4.48 us -> 129 us
  blocking collectives: 175 us -> 79 us
  other arithmetic: 81.7 us -> 8.84 us
  local copies, waits for them, and re-layouts: 79.6 us -> 29.5 us
  Pallas kernels: 0 us -> 20.9 us
  matrix products: 15.9 us -> 3.23 us
  between operations: 13.9 us -> 1.75 us
    reduce_scatter x2 -> x0, waiting for transfers between devices: 167 us -> none  [local(): lax.psum_scatter((lax.dot_general(narrow, features, contract_first, prefe...]
    ppermute x0 -> x58, starting transfers between devices: none -> 129 us  [the longest x26 61.3 us: ring(): return lax.ppermute(value, axis, [(i, i ^ mask) for i in range(4)])]
    all_gather x2 -> x0, waiting for transfers between devices: 115 us -> none  [local(): lax.all_gather(grad_rows, 'tp', axis=0, tiled=True)]
    psum x2 -> x0, blocking collectives: 88.5 us -> none  [local(): lax.psum((jnp.sum(summed * summed, axis=0), jnp.sum(target_now * summed,...]
    all_to_all x1 -> x0, waiting for transfers between devices: 76 us -> none  [local(): lax.all_to_all(delta[None], 'rep', split_axis=2, concat_axis=0, tiled=True)]
    ppermute x0 -> x58, waiting for transfers between devices: none -> 70 us  [the longest x26 34.7 us: ring(): return lax.ppermute(value, axis, [(i, i ^ mask) for i in range(4)])]
    dynamic_update_slice x16 -> x0, other arithmetic: 42.6 us -> none  [local(): lax.scan(advance, (slow_weights, momentum), (ordered, factors))]
    unnamed x1 -> x0, other arithmetic: 25.4 us -> none
  transfers between devices with their start and end apart: 5 -> 58, of which waited for: 5 -> 21; matrix products, arithmetic and copies ran while one was open for 0% -> 10% of each run, Pallas kernels for 0% -> 2%
where the time goes in v1:
time: 347 us; the launch traced here: 342 us
  starting transfers between devices  129 us (37%)
  blocking collectives  79 us (23%)
  waiting for transfers between devices  70 us (20%)
  local copies, waits for them, and re-layouts  29.5 us (9%)
  Pallas kernels  20.9 us (6%)
  other arithmetic  8.84 us (3%)
    all_to_all x1, blocking collectives, local(): back = lax.all_to_all(results, ('y', 'b', 'a'), 0, 0, tiled=True)  79 us
    ppermute x26, starting transfers between devices, ring(): return lax.ppermute(value, axis, [(i, i ^ mask) for i in range(4)])  61.3 us
    ppermute x18, starting transfers between devices, swap(): return lax.ppermute(value, axis, [(0, 1), (1, 0)])  42.8 us
    ppermute x26, waiting for transfers between devices, ring(): return lax.ppermute(value, axis, [(i, i ^ mask) for i in range(4)])  34.7 us
    ppermute x8, waiting for transfers between devices, to_owners(): parts[m1][m2] = lax.ppermute(pick(chunks, b ^ m1), AXES, pairs)  17.3 us
    ppermute x8, starting transfers between devices, to_owners(): parts[m1][m2] = lax.ppermute(pick(chunks, b ^ m1), AXES, pairs)  16 us
    pallas_call x1, Pallas kernels, outer(): pl.pallas_call(outer_kernel, in_specs=[smem] * 4 + [vmem] * 2 + [pl.Block...  11.8 us
    ppermute x6, waiting for transfers between devices, line(): return lax.ppermute(value, ('b', 'a'), [(i, i ^ mask) for i in range(4)])  11.4 us
  transfers between devices with their start and end apart: 58, of which 21 were waited for; matrix products, arithmetic and copies ran while one was open for 10% of the time, Pallas kernels for 2%

profile of v1, /device:TPU:1, one launch (start us, length us, event | category | flops | bytes accessed | tf_op | source)
XLA Modules:
  0.0 342.4 jit_solution(10539806022692180853)
XLA Ops:
  0.6 2.1 fusion.24
  3.4 5.2 %collective-permute-start.48 = (bf16[224,512]{1,0:T(8,128)(2,1)}, bf16[224,512]{1,0:T(8,128)(2,1)}, u32[]{:S(2)}, u32[]{:S(2)}) collective-permute-start(bf16[224,512]{1,0:T(8,128)(2,1)} %bitcast.94), channel_id=1, source_target_pairs={{0,48},{16,32},{32,16},{48,0},{1,49},{17,33},{33,17},{49,1},{2,50}... | collective-permute-start | bytes 688136 | tf_op jit(solution)/shard_map/ppermute | solution.py:53
  9.9 1.8 copy.47
  14.3 5.8 %collective-permute-start = (bf16[4,2,64,224]{3,2,1,0:T(8,128)(2,1)}, bf16[4,2,64,224]{3,2,1,0:T(8,128)(2,1)}, u32[]{:S(2)}, u32[]{:S(2)}) collective-permute-start(bf16[4,2,64,224]{3,2,1,0:T(8,128)(2,1)} %dynamic-slice_bitcast_fusion), channel_id=1, source_target_pairs={{0,2},{2,0},{1,3},{3,1},{4,6},{6,4},{5,7},{7,5},{8,10},{10,8},{9,1... | collective-permute-start | bytes 688136 | tf_op jit(solution)/shard_map/ppermute | solution.py:45
  20.1 2.0 copy.48
  22.1 1.8 dynamic-slice_bitcast_fusion.2
  23.9 1.7 fusion.1
  26.3 1.8 collective-permute-start.25
  29.0 1.6 forward.7
  31.5 1.6 forward.6
  35.0 1.8 stack.172
  36.8 1.7 copy.62
  38.4 1.9 copy.55
  40.3 1.8 stack.167
  46.8 1.6 forward.4
  48.8 1.8 collective-permute-start.54
  51.6 1.9 collective-permute-start.52
  57.4 2.3 collective-permute-start.24
  59.8 10.1 %collective-permute-done.53 = bf16[224,512]{1,0:T(8,128)(2,1)S(1)} collective-permute-done((bf16[224,512]{1,0:T(8,128)(2,1)S(1)}, bf16[224,512]{1,0:T(8,128)(2,1)S(1)}, u32[]{:S(2)}, u32[]{:S(2)}) %collective-permute-start.53) | collective-permute-done | bytes 229408 | tf_op jit(solution)/shard_map/ppermute | solution.py:53
  71.3 2.0 collective-permute-start.56
  76.1 2.1 collective-permute-start.5
  83.0 1.8 collective-permute-start.4
  84.8 3.5 %collective-permute-done.28 = bf16[64,2048]{1,0:T(8,128)(2,1)S(1)} collective-permute-done((bf16[64,2048]{1,0:T(8,128)(2,1)S(1)}, bf16[64,2048]{1,0:T(8,128)(2,1)S(1)}, u32[]{:S(2)}, u32[]{:S(2)}) %collective-permute-start.28) | collective-permute-done | bytes 262176 | tf_op jit(solution)/shard_map/ppermute | solution.py:49
  90.8 1.8 collective-permute-start.27
  94.0 2.0 collective-permute-done.27
  96.1 4.2 %collective-permute-done.7 = bf16[64,896]{1,0:T(8,128)(2,1)S(1)} collective-permute-done((bf16[64,896]{1,0:T(8,128)(2,1)S(1)}, bf16[64,896]{1,0:T(8,128)(2,1)S(1)}, u32[]{:S(2)}, u32[]{:S(2)}) %collective-permute-start.7) | collective-permute-done | bytes 114720 | tf_op jit(solution)/shard_map/ppermute | solution.py:45
  106.7 4.9 %collective-permute-start.30 = (bf16[64,1152]{1,0:T(8,128)(2,1)S(1)}, bf16[64,1152]{1,0:T(8,128)(2,1)S(1)}, u32[]{:S(2)}, u32[]{:S(2)}) collective-permute-start(bf16[64,1152]{1,0:T(8,128)(2,1)S(1)} %select_convert_fusion), channel_id=1, source_target_pairs={{0,2},{2,0},{1,3},{3,1},{4,6},{6,4},{5,7},{7,5},{8,10},{10,8},{9,1... | collective-permute-start | bytes 442376 | tf_op jit(solution)/shard_map/ppermute | solution.py:45
  111.5 2.1 collective-permute-done.11
  113.7 8.6 %collective-permute-start.12 = (bf16[2,64,896]{2,1,0:T(8,128)(2,1)S(1)}, bf16[2,64,896]{2,1,0:T(8,128)(2,1)S(1)}, u32[]{:S(2)}, u32[]{:S(2)}) collective-permute-start(bf16[2,64,896]{2,1,0:T(8,128)(2,1)S(1)} %pad_maximum_fusion.13), channel_id=1, source_target_pairs={{0,1},{1,0},{2,3},{3,2},{4,5},{5,4},{6,7},{7,6},{8,9},{9,8},{10,11... | collective-permute-start | bytes 688136 | tf_op jit(solution)/shard_map/ppermute | solution.py:45
  126.0 1.7 collective-permute-start.32
  132.0 13.0 %collective-permute-start.34 = (bf16[64,2,224]{2,0,1:T(8,128)(2,1)S(1)}, bf16[64,2,224]{2,0,1:T(8,128)(2,1)S(1)}, u32[]{:S(2)}, u32[]{:S(2)}) collective-permute-start(bf16[64,2,224]{2,0,1:T(8,128)(2,1)S(1)} %bitcast.250), channel_id=1, source_target_pairs={{0,1},{1,0},{2,3},{3,2},{4,5},{5,4},{6,7},{7,6},{8,9},{9,8},{10,11... | collective-permute-start | bytes 172040 | tf_op jit(solution)/shard_map/ppermute | solution.py:45
  145.8 4.8 %collective-permute-start.13 = (bf16[128,224]{1,0:T(8,128)(2,1)S(1)}, bf16[128,224]{1,0:T(8,128)(2,1)S(1)}, u32[]{:S(2)}, u32[]{:S(2)}) collective-permute-start(bf16[128,224]{1,0:T(8,128)(2,1)S(1)} %get-tuple-element.62), channel_id=1, source_target_pairs={{0,0},{1,16},{2,2},{3,18},{4,64},{5,80},{6,66},{7,82},{8,128},{9,1... | collective-permute-start | bytes 172040 | tf_op jit(solution)/shard_map/ppermute | solution.py:161
  152.0 1.9 collective-permute-start.15
  153.9 9.3 %collective-permute-start.50 = (bf16[4,224,512]{2,1,0:T(8,128)(2,1)S(1)}, bf16[4,224,512]{2,1,0:T(8,128)(2,1)S(1)}, u32[]{:S(2)}, u32[]{:S(2)}) collective-permute-start(bf16[4,224,512]{2,1,0:T(8,128)(2,1)S(1)} %pad_maximum_fusion.refs_16_), channel_id=1, source_target_pairs={{0,192},{64,128},{128,64},{192,0},{1,193},{65,129},{129,65},{193,1... | collective-permute-start | bytes 2752520 | tf_op jit(solution)/shard_map/ppermute | solution.py:49
  166.4 6.2 %collective-permute-done.36 = bf16[128,224]{1,0:T(8,128)(2,1)S(1)} collective-permute-done((bf16[128,224]{1,0:T(8,128)(2,1)S(1)}, bf16[128,224]{1,0:T(8,128)(2,1)S(1)}, u32[]{:S(2)}, u32[]{:S(2)}) %collective-permute-start.36) | collective-permute-done | bytes 57376 | tf_op jit(solution)/shard_map/ppermute | solution.py:161
  172.6 1.9 collective-permute-start.35
  174.5 4.2 %collective-permute-done.35 = bf16[128,224]{1,0:T(8,128)(2,1)S(1)} collective-permute-done((bf16[128,224]{1,0:T(8,128)(2,1)S(1)}, bf16[128,224]{1,0:T(8,128)(2,1)S(1)}, u32[]{:S(2)}, u32[]{:S(2)}) %collective-permute-start.35) | collective-permute-done | bytes 57376 | tf_op jit(solution)/shard_map/ppermute | solution.py:161
  178.7 2.1 collective-permute-start.38
  180.9 3.5 %collective-permute-done.38 = bf16[128,224]{1,0:T(8,128)(2,1)S(1)} collective-permute-done((bf16[128,224]{1,0:T(8,128)(2,1)S(1)}, bf16[128,224]{1,0:T(8,128)(2,1)S(1)}, u32[]{:S(2)}, u32[]{:S(2)}) %collective-permute-start.38) | collective-permute-done | bytes 57376 | tf_op jit(solution)/shard_map/ppermute | solution.py:161
  184.4 2.1 collective-permute-start.37
  186.5 3.4 %collective-permute-done.37 = bf16[128,224]{1,0:T(8,128)(2,1)S(1)} collective-permute-done((bf16[128,224]{1,0:T(8,128)(2,1)S(1)}, bf16[128,224]{1,0:T(8,128)(2,1)S(1)}, u32[]{:S(2)}, u32[]{:S(2)}) %collective-permute-start.37) | collective-permute-done | bytes 57376 | tf_op jit(solution)/shard_map/ppermute | solution.py:161
  190.0 26.5 %collective-permute-start.19 = (bf16[2,256,224]{2,1,0:T(8,128)(2,1)S(1)}, bf16[2,256,224]{2,1,0:T(8,128)(2,1)S(1)}, u32[]{:S(2)}, u32[]{:S(2)}) collective-permute-start(bf16[2,256,224]{2,1,0:T(8,128)(2,1)S(1)} %pad_maximum_fusion.7.refs_0_), channel_id=1, source_target_pairs={{0,12},{4,8},{8,4},{12,0},{1,13},{5,9},{9,5},{13,1},{2,14},{6,10},... | collective-permute-start | bytes 688136 | tf_op jit(solution)/shard_map/ppermute | solution.py:49
  217.3 11.5 %collective-permute-done.19.refs_3_ = bf16[2,256,224]{2,1,0:T(8,128)(2,1)S(1)} collective-permute-done((bf16[2,256,224]{2,1,0:T(8,128)(2,1)S(1)}, bf16[2,256,224]{2,1,0:T(8,128)(2,1)S(1)}, u32[]{:S(2)}, u32[]{:S(2)}) %collective-permute-start.19) | collective-permute-done | bytes 229408 | tf_op jit(solution)/shard_map/ppermute | solution.py:49
  229.4 2.7 collective-permute-start.41
  234.0 10.1 %collective-permute-done.41.refs_11_ = bf16[2,256,224]{2,1,0:T(8,128)(2,1)S(1)} collective-permute-done((bf16[2,256,224]{2,1,0:T(8,128)(2,1)S(1)}, bf16[2,256,224]{2,1,0:T(8,128)(2,1)S(1)}, u32[]{:S(2)}, u32[]{:S(2)}) %collective-permute-start.41) | collective-permute-done | bytes 229408 | tf_op jit(solution)/shard_map/ppermute | solution.py:49
  248.6 11.8 %outer.1 = (bf16[16,784,128]{2,1,0:T(8,128)(2,1)}, f32[448,224]{1,0:T(8,128)}, f32[448,224]{1,0:T(8,128)}) custom-call(s32[5]{0:T(128)} %stack.139.place, s32[16]{0:T(128)} %select_reduce_fusion.position, s32[16]{0:T(128)} %arrival.1, f32[16]{0:T(128)} %add_divide_fusion.factors, f32[448,224]{1,0:T(8,128)} %slow_ref.1, f32[448,224]{1,0:T(8,128)} %held_ref.1, ...), custom_call_target="tpu_custom_call" | custom-call | tf_op jit(solution)/shard_map/outer/pallas_call | solution.py:244
  260.3 79.0 %all_to_all.5.in_ref = bf16[16,784,128]{2,1,0:T(8,128)(2,1)S(1)} all-to-all(bf16[16,784,128]{2,1,0:T(8,128)(2,1)} %get-tuple-element.6), channel_id=1, replica_groups=mesh['y'=4,'b'=2,'a'=2,'x'=4,'h'=2,'c'=2] {'y','b','a'}, dimensions={0} | all-to-all | bytes 6422528 | tf_op jit(solution)/shard_map/all_to_all | solution.py:343
  339.4 2.8 assemble.1
  (229 shorter events, 59.2 us)
Async XLA Ops:
  3.4 48.0 %collective-permute-start.48 = (bf16[224,512]{1,0:T(8,128)(2,1)}, bf16[224,512]{1,0:T(8,128)(2,1)}, u32[]{:S(2)}, u32[]{:S(2)}) collective-permute-start(bf16[224,512]{1,0:T(8,128)(2,1)} %bitcast.94), channel_id=1, source_target_pairs={{0,48},{16,32},{32,16},{48,0},{1,49},{17,33},{33,17},{49,1},{2,50}... | collective-permute-start | bytes 688136 | tf_op jit(solution)/shard_map/ppermute | solution.py:53
  8.6 43.0 %collective-permute-start.47 = (bf16[224,512]{1,0:T(8,128)(2,1)}, bf16[224,512]{1,0:T(8,128)(2,1)}, u32[]{:S(2)}, u32[]{:S(2)}) collective-permute-start(bf16[224,512]{1,0:T(8,128)(2,1)} %bitcast.94), channel_id=1, source_target_pairs={{0,32},{16,48},{32,0},{48,16},{1,33},{17,49},{33,1},{49,17},{2,34}... | collective-permute-start | bytes 688136 | tf_op jit(solution)/shard_map/ppermute | solution.py:53
  8.6 44.9 %collective-permute-start.46 = (bf16[224,512]{1,0:T(8,128)(2,1)}, bf16[224,512]{1,0:T(8,128)(2,1)}, u32[]{:S(2)}, u32[]{:S(2)}) collective-permute-start(bf16[224,512]{1,0:T(8,128)(2,1)} %bitcast.94), channel_id=1, source_target_pairs={{0,16},{16,0},{32,48},{48,32},{1,17},{17,1},{33,49},{49,33},{2,18}... | collective-permute-start | bytes 688136 | tf_op jit(solution)/shard_map/ppermute | solution.py:53
  14.3 34.5 %collective-permute-start = (bf16[4,2,64,224]{3,2,1,0:T(8,128)(2,1)}, bf16[4,2,64,224]{3,2,1,0:T(8,128)(2,1)}, u32[]{:S(2)}, u32[]{:S(2)}) collective-permute-start(bf16[4,2,64,224]{3,2,1,0:T(8,128)(2,1)} %dynamic-slice_bitcast_fusion), channel_id=1, source_target_pairs={{0,2},{2,0},{1,3},{3,1},{4,6},{6,4},{5,7},{7,5},{8,10},{10,8},{9,1... | collective-permute-start | bytes 688136 | tf_op jit(solution)/shard_map/ppermute | solution.py:45
  26.3 22.1 %collective-permute-start.25 = (bf16[128,256]{1,0:T(8,128)(2,1)}, bf16[128,256]{1,0:T(8,128)(2,1)S(1)}, u32[]{:S(2)}, u32[]{:S(2)}) collective-permute-start(bf16[128,256]{1,0:T(8,128)(2,1)} %fusion.1), channel_id=1, source_target_pairs={{0,1},{1,0},{2,3},{3,2},{4,5},{5,4},{6,7},{7,6},{8,9},{9,8},{10,11... | collective-permute-start | bytes 196616 | tf_op jit(solution)/shard_map/ppermute | solution.py:45
  48.4 26.1 %collective-permute-start.2 = (bf16[4,128,896]{2,1,0:T(8,128)(2,1)S(1)}, bf16[4,128,896]{2,1,0:T(8,128)(2,1)S(1)}, u32[]{:S(2)}, u32[]{:S(2)}) collective-permute-start(bf16[4,128,896]{2,1,0:T(8,128)(2,1)S(1)} %forward.5), channel_id=1, source_target_pairs={{0,1},{1,0},{2,3},{3,2},{4,5},{5,4},{6,7},{7,6},{8,9},{9,8},{10,11... | collective-permute-start | bytes 2752520 | tf_op jit(solution)/shard_map/ppermute | solution.py:45
  48.8 8.7 %collective-permute-start.54 = (bf16[224,512]{1,0:T(8,128)(2,1)S(1)}, bf16[224,512]{1,0:T(8,128)(2,1)S(1)}, u32[]{:S(2)}, u32[]{:S(2)}) collective-permute-start(bf16[224,512]{1,0:T(8,128)(2,1)S(1)} %bitcast.247), channel_id=1, source_target_pairs={{0,48},{16,32},{32,16},{48,0},{1,49},{17,33},{33,17},{49,1},{2,50}... | collective-permute-start | bytes 688136 | tf_op jit(solution)/shard_map/ppermute | solution.py:53
  51.4 18.4 %collective-permute-start.53 = (bf16[224,512]{1,0:T(8,128)(2,1)S(1)}, bf16[224,512]{1,0:T(8,128)(2,1)S(1)}, u32[]{:S(2)}, u32[]{:S(2)}) collective-permute-start(bf16[224,512]{1,0:T(8,128)(2,1)S(1)} %bitcast.248), channel_id=1, source_target_pairs={{0,32},{16,48},{32,0},{48,16},{1,33},{17,49},{33,1},{49,17},{2,34}... | collective-permute-start | bytes 688136 | tf_op jit(solution)/shard_map/ppermute | solution.py:53
  51.6 19.6 %collective-permute-start.52 = (bf16[224,512]{1,0:T(8,128)(2,1)S(1)}, bf16[224,512]{1,0:T(8,128)(2,1)S(1)}, u32[]{:S(2)}, u32[]{:S(2)}) collective-permute-start(bf16[224,512]{1,0:T(8,128)(2,1)S(1)} %bitcast.249), channel_id=1, source_target_pairs={{0,16},{16,0},{32,48},{48,32},{1,17},{17,1},{33,49},{49,33},{2,18}... | collective-permute-start | bytes 688136 | tf_op jit(solution)/shard_map/ppermute | solution.py:53
  53.5 19.8 %collective-permute-start.1 = (bf16[2,4,64,224]{3,2,1,0:T(8,128)(2,1)S(1)}, bf16[2,4,64,224]{3,2,1,0:T(8,128)(2,1)S(1)}, u32[]{:S(2)}, u32[]{:S(2)}) collective-permute-start(bf16[2,4,64,224]{3,2,1,0:T(8,128)(2,1)S(1)} %pad_maximum_fusion.6), channel_id=1, source_target_pairs={{0,1},{1,0},{2,3},{3,2},{4,5},{5,4},{6,7},{7,6},{8,9},{9,8},{10,11... | collective-permute-start | bytes 688136 | tf_op jit(solution)/shard_map/ppermute | solution.py:45
  57.4 20.8 %collective-permute-start.24 = (bf16[4,128,896]{2,1,0:T(8,128)(2,1)S(1)}, bf16[4,128,896]{2,1,0:T(8,128)(2,1)S(1)}, u32[]{:S(2)}, u32[]{:S(2)}) collective-permute-start(bf16[4,128,896]{2,1,0:T(8,128)(2,1)S(1)} %copy-done.4), channel_id=1, source_target_pairs={{0,1},{1,0},{2,3},{3,2},{4,5},{5,4},{6,7},{7,6},{8,9},{9,8},{10,11... | collective-permute-start | bytes 2752520 | tf_op jit(solution)/shard_map/ppermute | solution.py:45
  69.9 82.1 %collective-permute-start.49 = (bf16[4,224,512]{2,1,0:T(8,128)(2,1)S(1)}, bf16[4,224,512]{2,1,0:T(8,128)(2,1)}, u32[]{:S(2)}, u32[]{:S(2)}) collective-permute-start(bf16[4,224,512]{2,1,0:T(8,128)(2,1)S(1)} %pad_maximum_fusion.refs_16_), channel_id=1, source_target_pairs={{0,64},{64,0},{128,192},{192,128},{1,65},{65,1},{129,193},{193,129... | collective-permute-start | bytes 2752520 | tf_op jit(solution)/shard_map/ppermute | solution.py:49
  71.3 82.5 %collective-permute-start.56 = (bf16[4,224,512]{2,1,0:T(8,128)(2,1)S(1)}, bf16[4,224,512]{2,1,0:T(8,128)(2,1)}, u32[]{:S(2)}, u32[]{:S(2)}) collective-permute-start(bf16[4,224,512]{2,1,0:T(8,128)(2,1)S(1)} %pad_maximum_fusion.1.refs_20_), channel_id=1, source_target_pairs={{0,192},{64,128},{128,64},{192,0},{1,193},{65,129},{129,65},{193,1... | collective-permute-start | bytes 2752520 | tf_op jit(solution)/shard_map/ppermute | solution.py:49
  74.8 5.4 %collective-permute-start.3 = (bf16[64,1792]{1,0:T(8,128)(2,1)S(1)}, bf16[64,1792]{1,0:T(8,128)(2,1)S(1)}, u32[]{:S(2)}, u32[]{:S(2)}) collective-permute-start(bf16[64,1792]{1,0:T(8,128)(2,1)S(1)} %pad_maximum_fusion.11), channel_id=1, source_target_pairs={{0,4},{4,0},{8,12},{12,8},{1,5},{5,1},{9,13},{13,9},{2,6},{6,2},{1... | collective-permute-start | bytes 688136 | tf_op jit(solution)/shard_map/ppermute | solution.py:49
  76.1 6.8 %collective-permute-start.5 = (bf16[64,1792]{1,0:T(8,128)(2,1)S(1)}, bf16[64,1792]{1,0:T(8,128)(2,1)S(1)}, u32[]{:S(2)}, u32[]{:S(2)}) collective-permute-start(bf16[64,1792]{1,0:T(8,128)(2,1)S(1)} %pad_maximum_fusion.12), channel_id=1, source_target_pairs={{0,12},{4,8},{8,4},{12,0},{1,13},{5,9},{9,5},{13,1},{2,14},{6,10},... | collective-permute-start | bytes 688136 | tf_op jit(solution)/shard_map/ppermute | solution.py:49
  78.5 9.8 %collective-permute-start.28 = (bf16[64,2048]{1,0:T(8,128)(2,1)S(1)}, bf16[64,2048]{1,0:T(8,128)(2,1)S(1)}, u32[]{:S(2)}, u32[]{:S(2)}) collective-permute-start(bf16[64,2048]{1,0:T(8,128)(2,1)S(1)} %pad_maximum_fusion.9), channel_id=1, source_target_pairs={{0,12},{4,8},{8,4},{12,0},{1,13},{5,9},{9,5},{13,1},{2,14},{6,10},... | collective-permute-start | bytes 786440 | tf_op jit(solution)/shard_map/ppermute | solution.py:49
  80.2 8.2 %collective-permute-start.26 = (bf16[64,2048]{1,0:T(8,128)(2,1)S(1)}, bf16[64,2048]{1,0:T(8,128)(2,1)S(1)}, u32[]{:S(2)}, u32[]{:S(2)}) collective-permute-start(bf16[64,2048]{1,0:T(8,128)(2,1)S(1)} %pad_maximum_fusion.8), channel_id=1, source_target_pairs={{0,4},{4,0},{8,12},{12,8},{1,5},{5,1},{9,13},{13,9},{2,6},{6,2},{1... | collective-permute-start | bytes 786440 | tf_op jit(solution)/shard_map/ppermute | solution.py:49
  83.0 7.8 %collective-permute-start.4 = (bf16[64,896]{1,0:T(8,128)(2,1)S(1)}, bf16[64,896]{1,0:T(8,128)(2,1)S(1)}, u32[]{:S(2)}, u32[]{:S(2)}) collective-permute-start(bf16[64,896]{1,0:T(8,128)(2,1)S(1)} %slice.449), channel_id=1, source_target_pairs={{0,12},{4,8},{8,4},{12,0},{1,13},{5,9},{9,5},{13,1},{2,14},{6,10},... | collective-permute-start | bytes 344072 | tf_op jit(solution)/shard_map/ppermute | solution.py:49
  88.4 5.5 %collective-permute-start.29 = (bf16[64,1152]{1,0:T(8,128)(2,1)S(1)}, bf16[64,1152]{1,0:T(8,128)(2,1)S(1)}, u32[]{:S(2)}, u32[]{:S(2)}) collective-permute-start(bf16[64,1152]{1,0:T(8,128)(2,1)S(1)} %slice.446), channel_id=1, source_target_pairs={{0,4},{4,0},{8,12},{12,8},{1,5},{5,1},{9,13},{13,9},{2,6},{6,2},{1... | collective-permute-start | bytes 442376 | tf_op jit(solution)/shard_map/ppermute | solution.py:49
  90.8 5.2 %collective-permute-start.27 = (bf16[64,1152]{1,0:T(8,128)(2,1)S(1)}, bf16[64,1152]{1,0:T(8,128)(2,1)S(1)}, u32[]{:S(2)}, u32[]{:S(2)}) collective-permute-start(bf16[64,1152]{1,0:T(8,128)(2,1)S(1)} %slice.447), channel_id=1, source_target_pairs={{0,12},{4,8},{8,4},{12,0},{1,13},{5,9},{9,5},{13,1},{2,14},{6,10},... | collective-permute-start | bytes 442376 | tf_op jit(solution)/shard_map/ppermute | solution.py:49
  92.6 7.6 %collective-permute-start.7 = (bf16[64,896]{1,0:T(8,128)(2,1)S(1)}, bf16[64,896]{1,0:T(8,128)(2,1)S(1)}, u32[]{:S(2)}, u32[]{:S(2)}) collective-permute-start(bf16[64,896]{1,0:T(8,128)(2,1)S(1)} %select_convert_fusion.1), channel_id=1, source_target_pairs={{0,2},{2,0},{1,3},{3,1},{4,6},{6,4},{5,7},{7,5},{8,10},{10,8},{9,1... | collective-permute-start | bytes 344072 | tf_op jit(solution)/shard_map/ppermute | solution.py:45
  105.9 7.6 %collective-permute-start.11 = (bf16[64,896]{1,0:T(8,128)(2,1)S(1)}, bf16[64,896]{1,0:T(8,128)(2,1)S(1)}, u32[]{:S(2)}, u32[]{:S(2)}) collective-permute-start(bf16[64,896]{1,0:T(8,128)(2,1)S(1)} %divide_convert_fusion.1), channel_id=1, source_target_pairs={{0,2},{2,0},{1,3},{3,1},{4,6},{6,4},{5,7},{7,5},{8,10},{10,8},{9,1... | collective-permute-start | bytes 344072 | tf_op jit(solution)/shard_map/ppermute | solution.py:45
  106.7 15.6 %collective-permute-start.30 = (bf16[64,1152]{1,0:T(8,128)(2,1)S(1)}, bf16[64,1152]{1,0:T(8,128)(2,1)S(1)}, u32[]{:S(2)}, u32[]{:S(2)}) collective-permute-start(bf16[64,1152]{1,0:T(8,128)(2,1)S(1)} %select_convert_fusion), channel_id=1, source_target_pairs={{0,2},{2,0},{1,3},{3,1},{4,6},{6,4},{5,7},{7,5},{8,10},{10,8},{9,1... | collective-permute-start | bytes 442376 | tf_op jit(solution)/shard_map/ppermute | solution.py:45
  113.7 9.7 %collective-permute-start.12 = (bf16[2,64,896]{2,1,0:T(8,128)(2,1)S(1)}, bf16[2,64,896]{2,1,0:T(8,128)(2,1)S(1)}, u32[]{:S(2)}, u32[]{:S(2)}) collective-permute-start(bf16[2,64,896]{2,1,0:T(8,128)(2,1)S(1)} %pad_maximum_fusion.13), channel_id=1, source_target_pairs={{0,1},{1,0},{2,3},{3,2},{4,5},{5,4},{6,7},{7,6},{8,9},{9,8},{10,11... | collective-permute-start | bytes 688136 | tf_op jit(solution)/shard_map/ppermute | solution.py:45
  132.0 18.5 %collective-permute-start.34 = (bf16[64,2,224]{2,0,1:T(8,128)(2,1)S(1)}, bf16[64,2,224]{2,0,1:T(8,128)(2,1)S(1)}, u32[]{:S(2)}, u32[]{:S(2)}) collective-permute-start(bf16[64,2,224]{2,0,1:T(8,128)(2,1)S(1)} %bitcast.250), channel_id=1, source_target_pairs={{0,1},{1,0},{2,3},{3,2},{4,5},{5,4},{6,7},{7,6},{8,9},{9,8},{10,11... | collective-permute-start | bytes 172040 | tf_op jit(solution)/shard_map/ppermute | solution.py:45
  145.1 18.1 %collective-permute-start.14 = (bf16[128,224]{1,0:T(8,128)(2,1)S(1)}, bf16[128,224]{1,0:T(8,128)(2,1)S(1)}, u32[]{:S(2)}, u32[]{:S(2)}) collective-permute-start(bf16[128,224]{1,0:T(8,128)(2,1)S(1)} %get-tuple-element.62), channel_id=1, source_target_pairs={{0,2},{1,18},{2,0},{3,16},{4,66},{5,82},{6,64},{7,80},{8,130},{9,1... | collective-permute-start | bytes 172040 | tf_op jit(solution)/shard_map/ppermute | solution.py:161
  145.8 18.7 %collective-permute-start.13 = (bf16[128,224]{1,0:T(8,128)(2,1)S(1)}, bf16[128,224]{1,0:T(8,128)(2,1)S(1)}, u32[]{:S(2)}, u32[]{:S(2)}) collective-permute-start(bf16[128,224]{1,0:T(8,128)(2,1)S(1)} %get-tuple-element.62), channel_id=1, source_target_pairs={{0,0},{1,16},{2,2},{3,18},{4,64},{5,80},{6,66},{7,82},{8,128},{9,1... | collective-permute-start | bytes 172040 | tf_op jit(solution)/shard_map/ppermute | solution.py:161
  150.6 14.6 %collective-permute-start.16 = (bf16[128,224]{1,0:T(8,128)(2,1)S(1)}, bf16[128,224]{1,0:T(8,128)(2,1)S(1)}, u32[]{:S(2)}, u32[]{:S(2)}) collective-permute-start(bf16[128,224]{1,0:T(8,128)(2,1)S(1)} %get-tuple-element.63), channel_id=1, source_target_pairs={{0,34},{1,50},{2,32},{3,48},{4,98},{5,114},{6,96},{7,112},{8,162},... | collective-permute-start | bytes 172040 | tf_op jit(solution)/shard_map/ppermute | solution.py:161
  152.0 13.2 %collective-permute-start.15 = (bf16[128,224]{1,0:T(8,128)(2,1)S(1)}, bf16[128,224]{1,0:T(8,128)(2,1)S(1)}, u32[]{:S(2)}, u32[]{:S(2)}) collective-permute-start(bf16[128,224]{1,0:T(8,128)(2,1)S(1)} %get-tuple-element.63), channel_id=1, source_target_pairs={{0,32},{1,48},{2,34},{3,50},{4,96},{5,112},{6,98},{7,114},{8,160},... | collective-permute-start | bytes 172040 | tf_op jit(solution)/shard_map/ppermute | solution.py:161
  153.9 36.2 %collective-permute-start.50 = (bf16[4,224,512]{2,1,0:T(8,128)(2,1)S(1)}, bf16[4,224,512]{2,1,0:T(8,128)(2,1)S(1)}, u32[]{:S(2)}, u32[]{:S(2)}) collective-permute-start(bf16[4,224,512]{2,1,0:T(8,128)(2,1)S(1)} %pad_maximum_fusion.refs_16_), channel_id=1, source_target_pairs={{0,192},{64,128},{128,64},{192,0},{1,193},{65,129},{129,65},{193,1... | collective-permute-start | bytes 2752520 | tf_op jit(solution)/shard_map/ppermute | solution.py:49
  163.2 53.4 %collective-permute-start.55 = (bf16[4,224,512]{2,1,0:T(8,128)(2,1)S(1)}, bf16[4,224,512]{2,1,0:T(8,128)(2,1)S(1)}, u32[]{:S(2)}, u32[]{:S(2)}) collective-permute-start(bf16[4,224,512]{2,1,0:T(8,128)(2,1)S(1)} %pad_maximum_fusion.1.refs_20_), channel_id=1, source_target_pairs={{0,64},{64,0},{128,192},{192,128},{1,65},{65,1},{129,193},{193,129... | collective-permute-start | bytes 2752520 | tf_op jit(solution)/shard_map/ppermute | solution.py:49
  164.5 67.6 %collective-permute-start.51 = (bf16[4,224,512]{2,1,0:T(8,128)(2,1)}, bf16[4,224,512]{2,1,0:T(8,128)(2,1)S(1)}, u32[]{:S(2)}, u32[]{:S(2)}) collective-permute-start(bf16[4,224,512]{2,1,0:T(8,128)(2,1)} %collective-permute-done.49.refs_17_), channel_id=1, source_target_pairs={{0,192},{64,128},{128,64},{192,0},{1,193},{65,129},{129,65},{193,1... | collective-permute-start | bytes 2752520 | tf_op jit(solution)/shard_map/ppermute | solution.py:49
  165.2 67.6 %collective-permute-start.57 = (bf16[4,224,512]{2,1,0:T(8,128)(2,1)}, bf16[4,224,512]{2,1,0:T(8,128)(2,1)S(1)}, u32[]{:S(2)}, u32[]{:S(2)}) collective-permute-start(bf16[4,224,512]{2,1,0:T(8,128)(2,1)} %collective-permute-done.56.refs_22_), channel_id=1, source_target_pairs={{0,64},{64,0},{128,192},{192,128},{1,65},{65,1},{129,193},{193,129... | collective-permute-start | bytes 2752520 | tf_op jit(solution)/shard_map/ppermute | solution.py:49
  165.2 7.4 %collective-permute-start.36 = (bf16[128,224]{1,0:T(8,128)(2,1)S(1)}, bf16[128,224]{1,0:T(8,128)(2,1)S(1)}, u32[]{:S(2)}, u32[]{:S(2)}) collective-permute-start(bf16[128,224]{1,0:T(8,128)(2,1)S(1)} %get-tuple-element.50), channel_id=1, source_target_pairs={{0,2},{1,18},{2,0},{3,16},{4,66},{5,82},{6,64},{7,80},{8,130},{9,1... | collective-permute-start | bytes 172040 | tf_op jit(solution)/shard_map/ppermute | solution.py:161
  172.6 6.1 %collective-permute-start.35 = (bf16[128,224]{1,0:T(8,128)(2,1)S(1)}, bf16[128,224]{1,0:T(8,128)(2,1)S(1)}, u32[]{:S(2)}, u32[]{:S(2)}) collective-permute-start(bf16[128,224]{1,0:T(8,128)(2,1)S(1)} %get-tuple-element.50), channel_id=1, source_target_pairs={{0,0},{1,16},{2,2},{3,18},{4,64},{5,80},{6,66},{7,82},{8,128},{9,1... | collective-permute-start | bytes 172040 | tf_op jit(solution)/shard_map/ppermute | solution.py:161
  178.7 5.7 %collective-permute-start.38 = (bf16[128,224]{1,0:T(8,128)(2,1)S(1)}, bf16[128,224]{1,0:T(8,128)(2,1)S(1)}, u32[]{:S(2)}, u32[]{:S(2)}) collective-permute-start(bf16[128,224]{1,0:T(8,128)(2,1)S(1)} %get-tuple-element.51), channel_id=1, source_target_pairs={{0,34},{1,50},{2,32},{3,48},{4,98},{5,114},{6,96},{7,112},{8,162},... | collective-permute-start | bytes 172040 | tf_op jit(solution)/shard_map/ppermute | solution.py:161
  184.4 5.6 %collective-permute-start.37 = (bf16[128,224]{1,0:T(8,128)(2,1)S(1)}, bf16[128,224]{1,0:T(8,128)(2,1)S(1)}, u32[]{:S(2)}, u32[]{:S(2)}) collective-permute-start(bf16[128,224]{1,0:T(8,128)(2,1)S(1)} %get-tuple-element.51), channel_id=1, source_target_pairs={{0,32},{1,48},{2,34},{3,50},{4,96},{5,112},{6,98},{7,114},{8,160},... | collective-permute-start | bytes 172040 | tf_op jit(solution)/shard_map/ppermute | solution.py:161
  190.0 26.6 %collective-permute-start.20 = (bf16[2,256,224]{2,1,0:T(8,128)(2,1)S(1)}, bf16[2,256,224]{2,1,0:T(8,128)(2,1)S(1)}, u32[]{:S(2)}, u32[]{:S(2)}) collective-permute-start(bf16[2,256,224]{2,1,0:T(8,128)(2,1)S(1)} %pad_maximum_fusion.7.refs_0_), channel_id=1, source_target_pairs={{0,1},{1,0},{2,3},{3,2},{4,5},{5,4},{6,7},{7,6},{8,9},{9,8},{10,11... | collective-permute-start | bytes 688136 | tf_op jit(solution)/shard_map/ppermute | solution.py:45
  190.0 38.8 %collective-permute-start.19 = (bf16[2,256,224]{2,1,0:T(8,128)(2,1)S(1)}, bf16[2,256,224]{2,1,0:T(8,128)(2,1)S(1)}, u32[]{:S(2)}, u32[]{:S(2)}) collective-permute-start(bf16[2,256,224]{2,1,0:T(8,128)(2,1)S(1)} %pad_maximum_fusion.7.refs_0_), channel_id=1, source_target_pairs={{0,12},{4,8},{8,4},{12,0},{1,13},{5,9},{9,5},{13,1},{2,14},{6,10},... | collective-permute-start | bytes 688136 | tf_op jit(solution)/shard_map/ppermute | solution.py:49
  216.5 12.9 %collective-permute-start.18 = (bf16[2,256,224]{2,1,0:T(8,128)(2,1)S(1)}, bf16[2,256,224]{2,1,0:T(8,128)(2,1)S(1)}, u32[]{:S(2)}, u32[]{:S(2)}) collective-permute-start(bf16[2,256,224]{2,1,0:T(8,128)(2,1)S(1)} %pad_maximum_fusion.7.refs_0_), channel_id=1, source_target_pairs={{0,8},{4,12},{8,0},{12,4},{1,9},{5,13},{9,1},{13,5},{2,10},{6,14},... | collective-permute-start | bytes 688136 | tf_op jit(solution)/shard_map/ppermute | solution.py:49
  216.6 15.5 %collective-permute-start.17 = (bf16[2,256,224]{2,1,0:T(8,128)(2,1)S(1)}, bf16[2,256,224]{2,1,0:T(8,128)(2,1)S(1)}, u32[]{:S(2)}, u32[]{:S(2)}) collective-permute-start(bf16[2,256,224]{2,1,0:T(8,128)(2,1)S(1)} %pad_maximum_fusion.7.refs_0_), channel_id=1, source_target_pairs={{0,4},{4,0},{8,12},{12,8},{1,5},{5,1},{9,13},{13,9},{2,6},{6,2},{1... | collective-permute-start | bytes 688136 | tf_op jit(solution)/shard_map/ppermute | solution.py:49
  228.8 5.0 %collective-permute-start.42 = (bf16[2,256,224]{2,1,0:T(8,128)(2,1)S(1)}, bf16[2,256,224]{2,1,0:T(8,128)(2,1)S(1)}, u32[]{:S(2)}, u32[]{:S(2)}) collective-permute-start(bf16[2,256,224]{2,1,0:T(8,128)(2,1)S(1)} %pad_maximum_fusion.10.refs_8_), channel_id=1, source_target_pairs={{0,1},{1,0},{2,3},{3,2},{4,5},{5,4},{6,7},{7,6},{8,9},{9,8},{10,11... | collective-permute-start | bytes 688136 | tf_op jit(solution)/shard_map/ppermute | solution.py:45
  229.4 14.7 %collective-permute-start.41 = (bf16[2,256,224]{2,1,0:T(8,128)(2,1)S(1)}, bf16[2,256,224]{2,1,0:T(8,128)(2,1)S(1)}, u32[]{:S(2)}, u32[]{:S(2)}) collective-permute-start(bf16[2,256,224]{2,1,0:T(8,128)(2,1)S(1)} %pad_maximum_fusion.10.refs_8_), channel_id=1, source_target_pairs={{0,12},{4,8},{8,4},{12,0},{1,13},{5,9},{9,5},{13,1},{2,14},{6,10},... | collective-permute-start | bytes 688136 | tf_op jit(solution)/shard_map/ppermute | solution.py:49
  232.1 12.9 %collective-permute-start.40 = (bf16[2,256,224]{2,1,0:T(8,128)(2,1)S(1)}, bf16[2,256,224]{2,1,0:T(8,128)(2,1)S(1)}, u32[]{:S(2)}, u32[]{:S(2)}) collective-permute-start(bf16[2,256,224]{2,1,0:T(8,128)(2,1)S(1)} %pad_maximum_fusion.10.refs_8_), channel_id=1, source_target_pairs={{0,8},{4,12},{8,0},{12,4},{1,9},{5,13},{9,1},{13,5},{2,10},{6,14},... | collective-permute-start | bytes 688136 | tf_op jit(solution)/shard_map/ppermute | solution.py:49
  232.1 13.2 %collective-permute-start.39 = (bf16[2,256,224]{2,1,0:T(8,128)(2,1)S(1)}, bf16[2,256,224]{2,1,0:T(8,128)(2,1)}, u32[]{:S(2)}, u32[]{:S(2)}) collective-permute-start(bf16[2,256,224]{2,1,0:T(8,128)(2,1)S(1)} %pad_maximum_fusion.10.refs_8_), channel_id=1, source_target_pairs={{0,4},{4,0},{8,12},{12,8},{1,5},{5,1},{9,13},{13,9},{2,6},{6,2},{1... | collective-permute-start | bytes 688136 | tf_op jit(solution)/shard_map/ppermute | solution.py:49
  232.8 13.0 %collective-permute-start.23 = (bf16[2,256,224]{2,1,0:T(8,128)(2,1)S(1)}, bf16[2,256,224]{2,1,0:T(8,128)(2,1)S(1)}, u32[]{:S(2)}, u32[]{:S(2)}) collective-permute-start(bf16[2,256,224]{2,1,0:T(8,128)(2,1)S(1)} %collective-permute-done.19.refs_3_), channel_id=1, source_target_pairs={{0,1},{1,0},{2,3},{3,2},{4,5},{5,4},{6,7},{7,6},{8,9},{9,8},{10,11... | collective-permute-start | bytes 688136 | tf_op jit(solution)/shard_map/ppermute | solution.py:45
  233.9 14.6 %collective-permute-start.22 = (bf16[2,256,224]{2,1,0:T(8,128)(2,1)S(1)}, bf16[2,256,224]{2,1,0:T(8,128)(2,1)}, u32[]{:S(2)}, u32[]{:S(2)}) collective-permute-start(bf16[2,256,224]{2,1,0:T(8,128)(2,1)S(1)} %collective-permute-done.18.refs_2_), channel_id=1, source_target_pairs={{0,1},{1,0},{2,3},{3,2},{4,5},{5,4},{6,7},{7,6},{8,9},{9,8},{10,11... | collective-permute-start | bytes 688136 | tf_op jit(solution)/shard_map/ppermute | solution.py:45
  244.1 4.3 %collective-permute-start.21 = (bf16[2,256,224]{2,1,0:T(8,128)(2,1)S(1)}, bf16[2,256,224]{2,1,0:T(8,128)(2,1)}, u32[]{:S(2)}, u32[]{:S(2)}) collective-permute-start(bf16[2,256,224]{2,1,0:T(8,128)(2,1)S(1)} %collective-permute-done.17.refs_1_), channel_id=1, source_target_pairs={{0,1},{1,0},{2,3},{3,2},{4,5},{5,4},{6,7},{7,6},{8,9},{9,8},{10,11... | collective-permute-start | bytes 688136 | tf_op jit(solution)/shard_map/ppermute | solution.py:45
  (43 other events, 879.9 us)

commit v2 on v1

v2 whole, which is shorter than its diff:
```python
import itertools
import math

import jax
import jax.numpy as jnp
from jax import lax
from jax.experimental import pallas as pl
from jax.experimental.pallas import tpu as pltpu
from jax.sharding import Mesh
from jax.sharding import PartitionSpec as P

D = 3584
FF = 7168
TOK = 256
ITERS = 2
REPLICAS = 16
ROWS = 448
COLS = 224
WIDE = 896
PACKED = 784

inner_rate = 2.0
outer_rate = 0.7
momentum_decay = 0.9
epsilon = 1e-06

AXES = ("y", "b", "a", "x", "h", "c")
SIZES = (4, 2, 2, 4, 2, 2)
F32 = jnp.float32
BF16 = jnp.bfloat16


def flat(*where):
    index = 0
    for size, place in zip(SIZES, where):
        index = index * size + place
    return index


def devices():
    return itertools.product(*map(range, SIZES))


def swap(value, axis):
    return lax.ppermute(value, axis, [(0, 1), (1, 0)])


def ring(value, axis, mask):
    return lax.ppermute(value, axis, [(i, i ^ mask) for i in range(4)])


def line(value, mask):
    return lax.ppermute(value, ("b", "a"), [(i, i ^ mask) for i in range(4)])


def pick(array, index, axis=0):
    return lax.dynamic_index_in_dim(array, index, axis, keepdims=False)


def forward_kernel(rows_ref, weights_ref, out_ref):
    out_ref[0] = (
        jnp.dot(rows_ref[...], weights_ref[...], preferred_element_type=F32)
        * (1.0 / math.sqrt(FF))
    ).astype(BF16)


def forward(rows, weights):
    count = rows.shape[0]
    return pl.pallas_call(
        forward_kernel,
        grid=(4,),
        in_specs=[
            pl.BlockSpec((count, ROWS), lambda i: (0, 0)),
            pl.BlockSpec((ROWS, WIDE), lambda i: (0, i)),
        ],
        out_specs=pl.BlockSpec((1, count, WIDE), lambda i: (i, 0, 0)),
        out_shape=jax.ShapeDtypeStruct((4, count, WIDE), BF16),
        cost_estimate=pl.CostEstimate(
            flops=2 * count * ROWS * D, bytes_accessed=2 * ROWS * D, transcendentals=0
        ),
        compiler_params=pltpu.CompilerParams(vmem_limit_bytes=32 << 20),
        name="forward",
    )(rows, weights)


def after(value, *others):
    return lax.optimization_barrier((value, *others))[0]


def away_kernel(place, keep_ref, got_ref, extra_ref, first_ref, second_ref):
    x = place[0]
    for half, out, near in ((0, first_ref, 1), (1, second_ref, 3)):
        for j, mask in enumerate((near, 2)):
            for i in range(ITERS):
                rows = pl.ds(128 * i + 64 * half, 64)
                block = keep_ref[x ^ mask, rows].astype(F32) + got_ref[x ^ mask, rows].astype(F32)
                at = (j * ITERS + i) * WIDE
                out[:, at : at + WIDE] = block.astype(BF16)
        out[:, 2 * ITERS * WIDE :] = extra_ref[pl.ds(64 * half, 64)].astype(BF16)


def split_away(x, keep, got, extra):
    shape = jax.ShapeDtypeStruct((64, 2 * ITERS * WIDE + TOK), BF16)
    vmem = pl.BlockSpec(memory_space=pltpu.VMEM)
    return pl.pallas_call(
        away_kernel,
        in_specs=[pl.BlockSpec(memory_space=pltpu.SMEM)] + [vmem] * 3,
        out_specs=[vmem] * 2,
        out_shape=[shape, shape],
        compiler_params=pltpu.CompilerParams(vmem_limit_bytes=24 << 20),
        name="split_away",
    )(x.astype(jnp.int32).reshape(1), keep, got, extra)


def own_blocks(keep, got, extra, x, half, second):
    def block(step, index):
        rows = slice(128 * step + 64 * half, 128 * step + 64 * half + 64)
        return pick(keep, index)[rows].astype(F32) + pick(got, index)[rows].astype(F32)

    mine = [block(i, x) for i in range(ITERS)] + [block(i, x ^ second) for i in range(ITERS)]
    return jnp.concatenate(mine + [extra[64 * half : 64 * half + 64]], axis=1)


def turn(near, far, c):
    both = jnp.stack([near, far])
    both = jnp.swapaxes(both, 2, 3).reshape(2, 4, 2, 64, COLS)
    return pick(both, c, 2), pick(both, 1 - c, 2)


def features_in_order(own, got, h, c):
    first, low = c == 0, h == 0
    pairs = [jnp.where(first, own, got), jnp.where(first, got, own)]
    return jnp.concatenate(
        [jnp.where(low, p[0], p[1]) for p in pairs] + [jnp.where(low, p[1], p[0]) for p in pairs],
        axis=-1,
    )


def over_ring(value):
    return value + ring(value, "x", 1) + ring(value, "x", 2) + ring(value, "x", 3)


def sums_of(summed, target_now):
    return jnp.stack([jnp.sum(summed * summed, axis=1), jnp.sum(target_now * summed, axis=1)])


def normal_grad(summed, target_now, sums, token_mask):
    rms = jnp.sqrt(sums[0] / D + epsilon)
    along = sums[1] / D / rms
    rms, along = rms[:, None], along[:, None]
    return (token_mask * (target_now - summed / rms * along) / rms).astype(BF16)


def in_order(own, other, index, axis):
    first = index == 0
    return jnp.stack([jnp.where(first, own, other), jnp.where(first, other, own)], axis=axis)


def to_owners(chunks, b, h):
    parts = [[None, None], [None, None]]
    for m1, m2 in itertools.product(range(2), range(2)):
        pairs = [
            (flat(y, b_, a, x, h_, c), flat(x, b_ ^ m1, c, x ^ y, h_ ^ m2, a))
            for y, b_, a, x, h_, c in devices()
        ]
        part = lax.ppermute(pick(chunks, b ^ m1), AXES, pairs)
        parts[m1][m2] = part.reshape(ITERS, 2, 64, COLS)
    return [in_order(p, q, h, 1).reshape(ITERS, TOK, COLS) for p, q in parts]


def to_all(held):
    grads = []
    one = [ring(held[0], "x", 1), ring(held[1], "x", 3)]
    pairs = [jnp.stack([v, w]) for v, w in zip(held, one)]
    two = [ring(pairs[0], "x", 3), ring(pairs[1], "x", 1)]
    for i in range(2):
        grads += [pairs[i], two[i], swap(pairs[i], "c"), swap(two[i], "c")]
    return grads


def pack(block):
    top, rest = block[:, :128], block[:, 128:]
    last = rest[336:]
    groups = [
        jnp.concatenate([rest[112 * q : 112 * q + 112], last[:, 32 * q : 32 * q + 32]], axis=1)
        for q in range(3)
    ]
    return jnp.concatenate([top] + groups, axis=0)


def unpack(block):
    groups = [block[448 + 112 * q : 560 + 112 * q] for q in range(3)]
    last = jnp.concatenate([g[:, 96:] for g in groups], axis=1)
    rest = jnp.concatenate([g[:, :96] for g in groups] + [last], axis=0)
    return jnp.concatenate([block[:ROWS], rest], axis=1)


def outer_kernel(place, position, arrival, factors, slow_ref, held_ref, *refs):
    grads = refs[:8]
    rows = refs[8:16]
    out_ref, slow_out, held_out, g_ref, d_ref, s_ref, m_ref, sems = refs[16:]
    copies = []
    for part in range(2):
        for core in range(2):
            for far in range(2):
                source = grads[part * 4 + core * 2 + far]
                for i in range(2):
                    if part == 0:
                        mask = (0, 1)[i] ^ (3 * far)
                    else:
                        mask = (0, 3)[i] ^ far
                    copies.append(
                        pltpu.make_async_copy(
                            source.at[i], g_ref.at[core, mask, part], sems.at[len(copies)]
                        )
                    )
    for copy in copies:
        copy.start()
    s_ref[...] = pack(slow_ref[...])
    m_ref[...] = pack(held_ref[...])
    for copy in copies:
        copy.wait()
    scale = inner_rate / math.sqrt(FF)
    y, b, a, c = place[0], place[1], place[2], place[3]
    x = place[4]
    for ky in range(4):
        for kz in range(4):
            block = rows[(kz // 2) * 4 + ky].at[kz % 2]
            ry, rb, ra = y ^ ky, b ^ (kz // 2), a ^ (kz % 2)
            slot = ry ^ y ^ x
            total = jnp.dot(
                block[:, :TOK], g_ref[ra ^ c, slot, rb ^ b, 0], preferred_element_type=F32
            ) + jnp.dot(
                block[:, TOK:], g_ref[ra ^ c, slot, rb ^ b, 1], preferred_element_type=F32
            )
            d_ref[position[ry * 4 + rb * 2 + ra]] = pack(total * scale)

    def step(k, _):
        factor = factors[k]
        target = arrival[k]
        for at in range(0, PACKED, 112):
            here = pl.ds(at, 112)
            grad = d_ref[k, here] * factor
            held = momentum_decay * m_ref[here] + grad
            slow = s_ref[here] - outer_rate * (grad + momentum_decay * held)
            m_ref[here] = held
            s_ref[here] = slow
            out_ref[target, here] = slow.astype(BF16)
        return 0

    lax.fori_loop(0, REPLICAS, step, 0)
    slow_out[...] = unpack(s_ref[...])
    held_out[...] = unpack(m_ref[...])


def outer(place, position, arrival, factors, slow, held, grads, rows):
    smem = pl.BlockSpec(memory_space=pltpu.SMEM)
    vmem = pl.BlockSpec(memory_space=pltpu.VMEM)
    return pl.pallas_call(
        outer_kernel,
        in_specs=[smem] * 4 + [vmem] * 2 + [pl.BlockSpec(memory_space=pl.ANY)] * 8 + [vmem] * 8,
        out_specs=[vmem] * 3,
        out_shape=[
            jax.ShapeDtypeStruct((REPLICAS, PACKED, 128), BF16),
            jax.ShapeDtypeStruct((ROWS, COLS), F32),
            jax.ShapeDtypeStruct((ROWS, COLS), F32),
        ],
        scratch_shapes=[
            pltpu.VMEM((2, 4, 2, ITERS, TOK, COLS), BF16),
            pltpu.VMEM((REPLICAS, PACKED, 128), F32),
            pltpu.VMEM((PACKED, 128), F32),
            pltpu.VMEM((PACKED, 128), F32),
            pltpu.SemaphoreType.DMA((16,)),
        ],
        compiler_params=pltpu.CompilerParams(vmem_limit_bytes=56 << 20),
        name="outer",
    )(place, position, arrival, factors, slow, held, *grads, *rows)


def assemble_kernel(in_ref, out_ref):
    blocks = [unpack(in_ref[i].astype(F32)) for i in range(4)]
    out_ref[...] = jnp.concatenate(blocks, axis=1).astype(BF16)


def assemble(blocks):
    return pl.pallas_call(
        assemble_kernel,
        grid=(4,),
        in_specs=[pl.BlockSpec((4, PACKED, 128), lambda i: (i, 0, 0))],
        out_specs=pl.BlockSpec((ROWS, WIDE), lambda i: (0, i)),
        out_shape=jax.ShapeDtypeStruct((ROWS, D), BF16),
        compiler_params=pltpu.CompilerParams(vmem_limit_bytes=32 << 20),
        name="assemble",
    )(blocks)


def local(
    replica_weights, slow_weights, momentum, hidden, residual, target, arrival, staleness, live
):
    y, b, a, x, h, c = (lax.axis_index(name) for name in AXES)
    weights, features = replica_weights[0], hidden[0]

    by_core = features.reshape(ITERS, 2, 2, 64, ROWS)
    others = pick(by_core, 1 - c, 2).reshape(TOK, ROWS)
    mine = pick(by_core, c, 2).reshape(TOK, ROWS)
    send = forward(others, weights)
    got = swap(send, "c")
    keep = forward(after(mine, send), weights)

    by_h = [v.reshape(ITERS, COLS, 2, 128) for v in after((residual[0], target[0]), keep)]
    far = swap(jnp.concatenate([pick(v, 1 - h, 2) for v in by_h]), "h")

    turned = jnp.transpose(after(features, keep), (2, 0, 1)).reshape(ROWS, ITERS * TOK)
    one_z = line(turned, 1)

    cross = [
        (
            lax.dot_general(
                rows[128:], features[0], (((1,), (1,)), ((), ())), preferred_element_type=F32
            )
            * (inner_rate / FF)
        ).astype(BF16)
        for rows in (mine, others)
    ]
    extra = cross[0].astype(F32) + swap(cross[1], "c").astype(F32)
    away = split_away(x, keep, got, extra)
    steps = [ring(v, "x", k) for v, k in zip(away, (1, 3))]
    keep, got, extra = after((keep, got, extra), *away)
    owns = [
        own_blocks(keep, got, extra, x, half, second) for half, second in zip((0, 1), (3, 1))
    ]
    two_z = line(after(turned, *away), 2)

    steps, one_z, far = lax.optimization_barrier((steps, one_z, far))
    totals = [own + step.astype(F32) for own, step in zip(owns, steps)]
    cut = ITERS * WIDE
    away = [v[:, cut:].astype(BF16) for v in totals]
    steps = [ring(v, "x", k) for v, k in zip(away, (3, 1))]
    upper = jnp.stack([turned, after(one_z, *away)])
    upper_one, upper_two = ring(upper, "y", 1), ring(upper, "y", 3)
    near = jnp.concatenate([pick(v, h, 2) for v in after(by_h, *away)])
    near, give = turn(near, far, c)
    streams = features_in_order(near, swap(give, "c"), h, c).astype(F32)

    steps, two_z = lax.optimization_barrier((steps, two_z))
    totals = [
        jnp.concatenate([v[:, :cut], v[:, 2 * cut :]], axis=1) + step.astype(F32)
        for v, step in zip(totals, steps)
    ]
    low = h == 0
    away = jnp.where(low, totals[1], totals[0]).astype(BF16)
    last = swap(away, "h")
    three_z = line(after(turned, away), 3)
    last, upper_one, upper_two = lax.optimization_barrier((last, upper_one, upper_two))
    output = jnp.where(low, totals[0], totals[1]) + last.astype(F32)
    first_output, second_output = output[:, :WIDE], output[:, WIDE : 2 * WIDE]
    cross_rows = output[:, 2 * WIDE :].astype(BF16)

    slots = jnp.arange(REPLICAS, dtype=jnp.int32)
    live_count = jnp.sum(jnp.where(slots == y * 4 + b * 2 + a, live, 0))
    token = h * 128 + c * 64 + jnp.arange(64, dtype=jnp.int32)
    token_mask = (token < live_count).astype(F32)[:, None]

    summed = streams[0] + first_output
    sums = sums_of(summed, streams[2])
    total = over_ring(sums)
    upper_both = ring(after(upper_one, sums), "y", 3)
    total, three_z = lax.optimization_barrier((total, three_z))
    first_grad = normal_grad(summed, streams[2], total, token_mask)
    by_h = in_order(first_grad, swap(first_grad, "h"), h, 0)
    lower = jnp.stack(after([two_z, three_z], first_grad))
    lower_one, lower_two = ring(lower, "y", 3), ring(lower, "y", 1)
    all_first = in_order(by_h, swap(by_h, "c"), c, 1)
    change = jnp.dot(cross_rows, all_first.reshape(TOK, WIDE), preferred_element_type=F32)
    summed = streams[1] + (second_output - change)
    sums = sums_of(summed, streams[3])
    total = over_ring(sums)
    second_grad = normal_grad(summed, streams[3], total, token_mask)

    first_chunks = pick(after(all_first, sums), h, 0).reshape(2, 64, 2, 2, COLS)
    first_chunks = pick(first_chunks, c, 3)
    by_core = second_grad.reshape(64, 2, 2, COLS)
    second_chunks = in_order(pick(by_core, c, 2), swap(pick(by_core, 1 - c, 2), "c"), c, 0)
    chunks = jnp.stack([first_chunks, second_chunks]).reshape(ITERS, 128, 2, COLS)
    chunks = jnp.transpose(chunks, (2, 0, 1, 3))
    held = to_owners(chunks, b, h)
    held, lower_one, lower_two = lax.optimization_barrier((held, lower_one, lower_two))
    lower_both = ring(lower_one, "y", 1)
    grads = to_all(held)
    rows = [upper, upper_one, upper_both, upper_two, lower, lower_two, lower_both, lower_one]

    position = jnp.sum(jnp.where(arrival[None, :] == slots[:, None], slots[None, :], 0), axis=1)
    factors = 1.0 / (1.0 + staleness.astype(F32))
    place = jnp.stack([y, b, a, c, x]).astype(jnp.int32)
    results, slow_after, momentum_after = outer(
        place, position.astype(jnp.int32), arrival, factors, slow_weights, momentum, grads, rows
    )
    back = lax.all_to_all(results, ("y", "b", "a"), 0, 0, tiled=True)
    return (assemble(back)[None], slow_after, momentum_after)


def solution(mesh):
    rep, tp = AXES[:3], AXES[3:]
    fine = Mesh(mesh.devices.reshape(SIZES), AXES)
    return jax.shard_map(
        local,
        mesh=fine,
        in_specs=(
            P(rep, tp, None),
            P(tp, rep),
            P(tp, rep),
            P(rep, None, None, tp),
            P(rep, None, tp, None),
            P(rep, None, tp, None),
            P(),
            P(),
            P(),
        ),
        out_specs=(P(rep, tp, None), P(tp, rep), P(tp, rep)),
        check_vma=False,
    )
```

time: 347 us -> 280 us (0.81)
  starting transfers between devices: 129 us -> 72.7 us
  local copies, waits for them, and re-layouts: 29.5 us -> 17.8 us
  other arithmetic: 8.84 us -> 15.5 us
    ppermute x26 -> x20, starting transfers between devices: 61.3 us -> 27.8 us  [ring(): return lax.ppermute(value, axis, [(i, i ^ mask) for i in range(4)])]
    ppermute x18 -> x12, starting transfers between devices: 42.8 us -> 20.5 us  [swap(): return lax.ppermute(value, axis, [(0, 1), (1, 0)])]
    ppermute x8 -> x4, waiting for transfers between devices: 17.3 us -> 5.4 us  [to_owners(): part = lax.ppermute(pick(chunks, b ^ m1), AXES, pairs)]
    ppermute x18 -> x12, waiting for transfers between devices: 6.66 us -> 17.8 us  [swap(): return lax.ppermute(value, axis, [(0, 1), (1, 0)])]
    ppermute x6 -> x3, starting transfers between devices: 9.17 us -> 3.72 us  [line(): return lax.ppermute(value, ('b', 'a'), [(i, i ^ mask) for i in range(4)])]
    unnamed x70 -> x48, local copies, waits for them, and re-layouts: 10.8 us -> 5.89 us
    unnamed x0 -> x5, other arithmetic: none -> 4.9 us
    slice x11 -> x7, local copies, waits for them, and re-layouts: 7.3 us -> 2.48 us  [the longest x1 1.64 us: local(): rows[128:]]
  transfers between devices with their start and end apart: 58 -> 39, of which waited for: 21 -> 17; matrix products, arithmetic and copies ran while one was open for 10% -> 10% of each run, Pallas kernels for 2% -> 1%
where the time goes in v2:
time: 280 us; the launch traced here: 279 us
  blocking collectives  78.8 us (28%)
  starting transfers between devices  72.7 us (26%)
  waiting for transfers between devices  68.6 us (24%)
  Pallas kernels  21.7 us (8%)
  local copies, waits for them, and re-layouts  17.8 us (6%)
  other arithmetic  15.5 us (6%)
    all_to_all x1, blocking collectives, local(): back = lax.all_to_all(results, ('y', 'b', 'a'), 0, 0, tiled=True)  78.8 us
    ppermute x20, waiting for transfers between devices, ring(): return lax.ppermute(value, axis, [(i, i ^ mask) for i in range(4)])  31 us
    ppermute x20, starting transfers between devices, ring(): return lax.ppermute(value, axis, [(i, i ^ mask) for i in range(4)])  27.8 us
    ppermute x4, starting transfers between devices, to_owners(): part = lax.ppermute(pick(chunks, b ^ m1), AXES, pairs)  20.7 us
    ppermute x12, starting transfers between devices, swap(): return lax.ppermute(value, axis, [(0, 1), (1, 0)])  20.5 us
    ppermute x12, waiting for transfers between devices, swap(): return lax.ppermute(value, axis, [(0, 1), (1, 0)])  17.8 us
    ppermute x3, waiting for transfers between devices, line(): return lax.ppermute(value, ('b', 'a'), [(i, i ^ mask) for i in range(4)])  14.3 us
    pallas_call x1, Pallas kernels, outer(): pl.pallas_call(outer_kernel, in_specs=[smem] * 4 + [vmem] * 2 + [pl.Block...  12 us
  transfers between devices with their start and end apart: 39, of which 17 were waited for; matrix products, arithmetic and copies ran while one was open for 10% of the time, Pallas kernels for 1%

profile of v2, /device:TPU:1, one launch (start us, length us, event | category | flops | bytes accessed | tf_op | source)
XLA Modules:
  0.0 278.8 jit_solution(18356248748911122539)
XLA Ops:
  0.6 1.2 copy.33
  2.7 1.9 copy-done
  4.6 3.1 %forward.2 = bf16[4,256,896]{2,1,0:T(8,128)(2,1)} custom-call(bf16[256,448]{1,0:T(8,128)(2,1)S(1)} %bitcast.161, bf16[448,3584]{1,0:T(8,128)(2,1)S(1)} %bitcast.158), custom_call_target="tpu_custom_call" | custom-call | flops 822083584 | bytes 3211264 | tf_op jit(solution)/shard_map/forward/pallas_call | solution.py:69
  7.7 3.2 %collective-permute-start = (bf16[4,256,896]{2,1,0:T(8,128)(2,1)}, bf16[4,256,896]{2,1,0:T(8,128)(2,1)}, u32[]{:S(2)}, u32[]{:S(2)}) collective-permute-start(bf16[4,256,896]{2,1,0:T(8,128)(2,1)} %forward.2), channel_id=1, source_target_pairs={{0,1},{1,0},{2,3},{3,2},{4,5},{5,4},{6,7},{7,6},{8,9},{9,8},{10,11... | collective-permute-start | bytes 5505032 | tf_op jit(solution)/shard_map/ppermute | solution.py:45
  10.9 1.6 constant_dynamic-slice_fusion.1
  12.5 1.7 fusion.2
  14.3 2.1 forward.3.keep_ref
  16.4 1.2 copy-done.2
  20.9 5.2 %collective-permute-start.5 = (bf16[4,224,128]{2,1,0:T(8,128)(2,1)}, bf16[4,224,128]{2,1,0:T(8,128)(2,1)}, u32[]{:S(2)}, u32[]{:S(2)}) collective-permute-start(bf16[4,224,128]{2,1,0:T(8,128)(2,1)} %pad_maximum_fusion.7), channel_id=1, source_target_pairs={{0,2},{2,0},{1,3},{3,1},{4,6},{6,4},{5,7},{7,5},{8,10},{10,8},{9,1... | collective-permute-start | bytes 688136 | tf_op jit(solution)/shard_map/ppermute | solution.py:45
  27.7 1.2 copy.34
  28.9 1.3 stack_reshape.3
  30.5 1.7 split_away.1
  32.2 1.3 collective-permute-start.2
  33.5 1.8 collective-permute-start.3
  35.3 1.2 collective-permute-start.9
  41.5 14.3 %collective-permute-done.4 = bf16[448,512]{1,0:T(8,128)(2,1)} collective-permute-done((bf16[448,512]{1,0:T(8,128)(2,1)}, bf16[448,512]{1,0:T(8,128)(2,1)}, u32[]{:S(2)}, u32[]{:S(2)}) %collective-permute-start.4) | collective-permute-done | bytes 458784 | tf_op jit(solution)/shard_map/ppermute | solution.py:53
  57.3 1.8 maximum_bitcast_fusion
  59.0 1.2 copy.35
  60.3 1.4 collective-permute-start.6
  62.4 1.9 collective-permute-start.8
  64.2 2.4 collective-permute-start.7
  67.8 2.8 %collective-permute-start.12 = (bf16[2,448,512]{2,1,0:T(8,128)(2,1)S(1)}, bf16[2,448,512]{2,1,0:T(8,128)(2,1)S(1)}, u32[]{:S(2)}, u32[]{:S(2)}) collective-permute-start(bf16[2,448,512]{2,1,0:T(8,128)(2,1)S(1)} %pad_maximum_fusion.refs_8_), channel_id=1, source_target_pairs={{0,192},{64,128},{128,64},{192,0},{1,193},{65,129},{129,65},{193,1... | collective-permute-start | bytes 2752520 | tf_op jit(solution)/shard_map/ppermute | solution.py:49
  70.9 2.4 collective-permute-done.7
  73.9 1.8 collective-permute-start.16
  75.7 11.0 %collective-permute-done.10 = bf16[64,2048]{1,0:T(8,128)(2,1)S(1)} collective-permute-done((bf16[64,2048]{1,0:T(8,128)(2,1)S(1)}, bf16[64,2048]{1,0:T(8,128)(2,1)S(1)}, u32[]{:S(2)}, u32[]{:S(2)}) %collective-permute-start.10) | collective-permute-done | bytes 262176 | tf_op jit(solution)/shard_map/ppermute | solution.py:45
  86.7 3.8 %collective-permute-done.12.refs_11_ = bf16[2,448,512]{2,1,0:T(8,128)(2,1)S(1)} collective-permute-done((bf16[2,448,512]{2,1,0:T(8,128)(2,1)S(1)}, bf16[2,448,512]{2,1,0:T(8,128)(2,1)S(1)}, u32[]{:S(2)}, u32[]{:S(2)}) %collective-permute-start.12) | collective-permute-done | bytes 917536 | tf_op jit(solution)/shard_map/ppermute | solution.py:49
  92.4 1.8 collective-permute-start.14
  94.1 1.1 collective-permute-start.13
  97.1 2.0 collective-permute-start.17
  99.1 5.7 %collective-permute-done.17 = bf16[64,896]{1,0:T(8,128)(2,1)S(1)} collective-permute-done((bf16[64,896]{1,0:T(8,128)(2,1)S(1)}, bf16[64,896]{1,0:T(8,128)(2,1)S(1)}, u32[]{:S(2)}, u32[]{:S(2)}) %collective-permute-start.17) | collective-permute-done | bytes 114720 | tf_op jit(solution)/shard_map/ppermute | solution.py:45
  105.5 4.3 %collective-permute-start.18 = (bf16[2,64,896]{2,1,0:T(8,128)(2,1)}, bf16[2,64,896]{2,1,0:T(8,128)(2,1)}, u32[]{:S(2)}, u32[]{:S(2)}) collective-permute-start(bf16[2,64,896]{2,1,0:T(8,128)(2,1)} %pad_maximum_fusion.8), channel_id=1, source_target_pairs={{0,1},{1,0},{2,3},{3,2},{4,5},{5,4},{6,7},{7,6},{8,9},{9,8},{10,11... | collective-permute-start | bytes 688136 | tf_op jit(solution)/shard_map/ppermute | solution.py:45
  109.9 1.1 pad_maximum_fusion.1.refs_12_
  111.3 1.9 collective-permute-start.27
  114.7 1.8 collective-permute-start.20
  118.7 1.8 collective-permute-done.21
  121.2 1.7 collective-permute-start.22
  124.6 2.4 collective-permute-start.25
  127.0 12.8 %collective-permute-start.24 = (bf16[2,128,224]{2,1,0:T(8,128)(2,1)S(1)}, bf16[2,128,224]{2,1,0:T(8,128)(2,1)S(1)}, u32[]{:S(2)}, u32[]{:S(2)}) collective-permute-start(bf16[2,128,224]{2,1,0:T(8,128)(2,1)S(1)} %get-tuple-element.98), channel_id=1, source_target_pairs={{0,2},{1,18},{2,0},{3,16},{4,70},{5,86},{6,68},{7,84},{8,138},{9,1... | collective-permute-start | bytes 344072 | tf_op jit(solution)/shard_map/ppermute | solution.py:166
  139.8 4.8 %collective-permute-start.23 = (bf16[2,128,224]{2,1,0:T(8,128)(2,1)S(1)}, bf16[2,128,224]{2,1,0:T(8,128)(2,1)S(1)}, u32[]{:S(2)}, u32[]{:S(2)}) collective-permute-start(bf16[2,128,224]{2,1,0:T(8,128)(2,1)S(1)} %get-tuple-element.98), channel_id=1, source_target_pairs={{0,0},{1,16},{2,2},{3,18},{4,68},{5,84},{6,70},{7,86},{8,136},{9,1... | collective-permute-start | bytes 344072 | tf_op jit(solution)/shard_map/ppermute | solution.py:166
  144.8 5.4 %collective-permute-done.24 = bf16[2,128,224]{2,1,0:T(8,128)(2,1)S(1)} collective-permute-done((bf16[2,128,224]{2,1,0:T(8,128)(2,1)S(1)}, bf16[2,128,224]{2,1,0:T(8,128)(2,1)S(1)}, u32[]{:S(2)}, u32[]{:S(2)}) %collective-permute-start.24) | collective-permute-done | bytes 114720 | tf_op jit(solution)/shard_map/ppermute | solution.py:166
  150.3 7.1 %collective-permute-start.33 = (bf16[2,256,224]{2,1,0:T(8,128)(2,1)S(1)}, bf16[2,256,224]{2,1,0:T(8,128)(2,1)S(1)}, u32[]{:S(2)}, u32[]{:S(2)}) collective-permute-start(bf16[2,256,224]{2,1,0:T(8,128)(2,1)S(1)} %bitcast.170), channel_id=1, source_target_pairs={{0,12},{4,8},{8,4},{12,0},{1,13},{5,9},{9,5},{13,1},{2,14},{6,10},... | collective-permute-start | bytes 688136 | tf_op jit(solution)/shard_map/ppermute | solution.py:49
  158.3 5.6 %collective-permute-done.33 = bf16[2,256,224]{2,1,0:T(8,128)(2,1)S(1)} collective-permute-done((bf16[2,256,224]{2,1,0:T(8,128)(2,1)S(1)}, bf16[2,256,224]{2,1,0:T(8,128)(2,1)S(1)}, u32[]{:S(2)}, u32[]{:S(2)}) %collective-permute-start.33) | collective-permute-done | bytes 229408 | tf_op jit(solution)/shard_map/ppermute | solution.py:49
  164.1 2.0 collective-permute-done.29
  167.3 1.3 collective-permute-start.35
  168.6 12.4 %collective-permute-done.37.refs_10_ = bf16[2,448,512]{2,1,0:T(8,128)(2,1)S(1)} collective-permute-done((bf16[2,448,512]{2,1,0:T(8,128)(2,1)S(1)}, bf16[2,448,512]{2,1,0:T(8,128)(2,1)S(1)}, u32[]{:S(2)}, u32[]{:S(2)}) %collective-permute-start.37) | collective-permute-done | bytes 917536 | tf_op jit(solution)/shard_map/ppermute | solution.py:49
  185.1 12.0 %outer.1 = (bf16[16,784,128]{2,1,0:T(8,128)(2,1)}, f32[448,224]{1,0:T(8,128)}, f32[448,224]{1,0:T(8,128)}) custom-call(s32[5]{0:T(128)} %stack.129.place, s32[16]{0:T(128)} %select_reduce_fusion.position, s32[16]{0:T(128)} %arrival.1, f32[16]{0:T(128)} %add_divide_fusion.factors, f32[448,224]{1,0:T(8,128)} %slow_ref.1, f32[448,224]{1,0:T(8,128)} %held_ref.1, ...), custom_call_target="tpu_custom_call" | custom-call | tf_op jit(solution)/shard_map/outer/pallas_call | solution.py:259
  197.1 78.8 %all_to_all.5.in_ref = bf16[16,784,128]{2,1,0:T(8,128)(2,1)S(1)} all-to-all(bf16[16,784,128]{2,1,0:T(8,128)(2,1)} %get-tuple-element.74), channel_id=1, replica_groups=mesh['y'=4,'b'=2,'a'=2,'x'=4,'h'=2,'c'=2] {'y','b','a'}, dimensions={0} | all-to-all | bytes 6422528 | tf_op jit(solution)/shard_map/all_to_all | solution.py:398
  275.9 2.8 %assemble.1 = bf16[448,3584]{1,0:T(8,128)(2,1)} custom-call(bf16[16,784,128]{2,1,0:T(8,128)(2,1)S(1)} %all_to_all.5.in_ref), custom_call_target="tpu_custom_call" | custom-call | tf_op jit(solution)/shard_map/assemble/pallas_call | solution.py:286
  (159 shorter events, 32.0 us)
Async XLA Ops:
  4.6 9.7 %copy-start.1 = (bf16[1,448,3584]{2,1,0:T(8,128)(2,1)S(1)}, bf16[1,448,3584]{2,1,0:T(8,128)(2,1)}, u32[]{:S(2)}) copy-start(bf16[1,448,3584]{2,1,0:T(8,128)(2,1)} %param.9) | copy-start | bytes 9633796
  7.7 22.8 %collective-permute-start = (bf16[4,256,896]{2,1,0:T(8,128)(2,1)}, bf16[4,256,896]{2,1,0:T(8,128)(2,1)}, u32[]{:S(2)}, u32[]{:S(2)}) collective-permute-start(bf16[4,256,896]{2,1,0:T(8,128)(2,1)} %forward.2), channel_id=1, source_target_pairs={{0,1},{1,0},{2,3},{3,2},{4,5},{5,4},{6,7},{7,6},{8,9},{9,8},{10,11... | collective-permute-start | bytes 5505032 | tf_op jit(solution)/shard_map/ppermute | solution.py:45
  14.3 15.9 %collective-permute-start.1 = (bf16[128,256]{1,0:T(8,128)(2,1)}, bf16[128,256]{1,0:T(8,128)(2,1)S(1)}, u32[]{:S(2)}, u32[]{:S(2)}) collective-permute-start(bf16[128,256]{1,0:T(8,128)(2,1)} %fusion.2), channel_id=1, source_target_pairs={{0,1},{1,0},{2,3},{3,2},{4,5},{5,4},{6,7},{7,6},{8,9},{9,8},{10,11... | collective-permute-start | bytes 196616 | tf_op jit(solution)/shard_map/ppermute | solution.py:45
  20.2 10.1 %copy-start.17 = (bf16[1,2,1,64,448]{4,3,2,1,0:T(8,128)(2,1)S(1)}, bf16[1,2,1,64,448]{4,3,2,1,0:T(8,128)(2,1)}, u32[]{:S(2)}) copy-start(bf16[1,2,1,64,448]{4,3,2,1,0:T(8,128)(2,1)} %get-tuple-element.89) | copy-start | bytes 344068
  20.2 10.2 %copy-start.3 = (bf16[4,256,896]{2,1,0:T(8,128)(2,1)S(1)}, bf16[4,256,896]{2,1,0:T(8,128)(2,1)}, u32[]{:S(2)}) copy-start(bf16[4,256,896]{2,1,0:T(8,128)(2,1)} %copy-done.2) | copy-start | bytes 5505028
  20.9 20.5 %collective-permute-start.5 = (bf16[4,224,128]{2,1,0:T(8,128)(2,1)}, bf16[4,224,128]{2,1,0:T(8,128)(2,1)}, u32[]{:S(2)}, u32[]{:S(2)}) collective-permute-start(bf16[4,224,128]{2,1,0:T(8,128)(2,1)} %pad_maximum_fusion.7), channel_id=1, source_target_pairs={{0,2},{2,0},{1,3},{3,1},{4,6},{6,4},{5,7},{7,5},{8,10},{10,8},{9,1... | collective-permute-start | bytes 688136 | tf_op jit(solution)/shard_map/ppermute | solution.py:45
  26.9 28.8 %collective-permute-start.4 = (bf16[448,512]{1,0:T(8,128)(2,1)}, bf16[448,512]{1,0:T(8,128)(2,1)}, u32[]{:S(2)}, u32[]{:S(2)}) collective-permute-start(bf16[448,512]{1,0:T(8,128)(2,1)} %bitcast.78), channel_id=1, source_target_pairs={{0,16},{16,0},{32,48},{48,32},{1,17},{17,1},{33,49},{49,33},{2,18}... | collective-permute-start | bytes 1376264 | tf_op jit(solution)/shard_map/ppermute | solution.py:53
  32.2 23.5 %collective-permute-start.2 = (bf16[64,3840]{1,0:T(8,128)(2,1)S(1)}, bf16[64,3840]{1,0:T(8,128)(2,1)S(1)}, u32[]{:S(2)}, u32[]{:S(2)}) collective-permute-start(bf16[64,3840]{1,0:T(8,128)(2,1)S(1)} %get-tuple-element.43), channel_id=1, source_target_pairs={{0,4},{4,0},{8,12},{12,8},{1,5},{5,1},{9,13},{13,9},{2,6},{6,2},{1... | collective-permute-start | bytes 1474568 | tf_op jit(solution)/shard_map/ppermute | solution.py:49
  33.5 22.3 %collective-permute-start.3 = (bf16[64,3840]{1,0:T(8,128)(2,1)S(1)}, bf16[64,3840]{1,0:T(8,128)(2,1)S(1)}, u32[]{:S(2)}, u32[]{:S(2)}) collective-permute-start(bf16[64,3840]{1,0:T(8,128)(2,1)S(1)} %get-tuple-element.44), channel_id=1, source_target_pairs={{0,12},{4,8},{8,4},{12,0},{1,13},{5,9},{9,5},{13,1},{2,14},{6,10},... | collective-permute-start | bytes 1474568 | tf_op jit(solution)/shard_map/ppermute | solution.py:49
  35.3 35.4 %collective-permute-start.9 = (bf16[448,512]{1,0:T(8,128)(2,1)}, bf16[448,512]{1,0:T(8,128)(2,1)}, u32[]{:S(2)}, u32[]{:S(2)}) collective-permute-start(bf16[448,512]{1,0:T(8,128)(2,1)} %bitcast.78), channel_id=1, source_target_pairs={{0,32},{16,48},{32,0},{48,16},{1,33},{17,49},{33,1},{49,17},{2,34}... | collective-permute-start | bytes 1376264 | tf_op jit(solution)/shard_map/ppermute | solution.py:53
  60.3 10.3 %collective-permute-start.6 = (bf16[2,4,64,224]{3,2,1,0:T(8,128)(2,1)S(1)}, bf16[2,4,64,224]{3,2,1,0:T(8,128)(2,1)S(1)}, u32[]{:S(2)}, u32[]{:S(2)}) collective-permute-start(bf16[2,4,64,224]{3,2,1,0:T(8,128)(2,1)S(1)} %dynamic-slice_bitcast_fusion), channel_id=1, source_target_pairs={{0,1},{1,0},{2,3},{3,2},{4,5},{5,4},{6,7},{7,6},{8,9},{9,8},{10,11... | collective-permute-start | bytes 688136 | tf_op jit(solution)/shard_map/ppermute | solution.py:45
  62.4 8.5 %collective-permute-start.8 = (bf16[64,2048]{1,0:T(8,128)(2,1)S(1)}, bf16[64,2048]{1,0:T(8,128)(2,1)S(1)}, u32[]{:S(2)}, u32[]{:S(2)}) collective-permute-start(bf16[64,2048]{1,0:T(8,128)(2,1)S(1)} %slice.286), channel_id=1, source_target_pairs={{0,4},{4,0},{8,12},{12,8},{1,5},{5,1},{9,13},{13,9},{2,6},{6,2},{1... | collective-permute-start | bytes 786440 | tf_op jit(solution)/shard_map/ppermute | solution.py:49
  64.2 9.0 %collective-permute-start.7 = (bf16[64,2048]{1,0:T(8,128)(2,1)}, bf16[64,2048]{1,0:T(8,128)(2,1)S(1)}, u32[]{:S(2)}, u32[]{:S(2)}) collective-permute-start(bf16[64,2048]{1,0:T(8,128)(2,1)} %slice.287), channel_id=1, source_target_pairs={{0,12},{4,8},{8,4},{12,0},{1,13},{5,9},{9,5},{13,1},{2,14},{6,10},... | collective-permute-start | bytes 786440 | tf_op jit(solution)/shard_map/ppermute | solution.py:49
  67.8 22.7 %collective-permute-start.12 = (bf16[2,448,512]{2,1,0:T(8,128)(2,1)S(1)}, bf16[2,448,512]{2,1,0:T(8,128)(2,1)S(1)}, u32[]{:S(2)}, u32[]{:S(2)}) collective-permute-start(bf16[2,448,512]{2,1,0:T(8,128)(2,1)S(1)} %pad_maximum_fusion.refs_8_), channel_id=1, source_target_pairs={{0,192},{64,128},{128,64},{192,0},{1,193},{65,129},{129,65},{193,1... | collective-permute-start | bytes 2752520 | tf_op jit(solution)/shard_map/ppermute | solution.py:49
  70.6 21.0 %collective-permute-start.11 = (bf16[2,448,512]{2,1,0:T(8,128)(2,1)S(1)}, bf16[2,448,512]{2,1,0:T(8,128)(2,1)S(1)}, u32[]{:S(2)}, u32[]{:S(2)}) collective-permute-start(bf16[2,448,512]{2,1,0:T(8,128)(2,1)S(1)} %pad_maximum_fusion.refs_8_), channel_id=1, source_target_pairs={{0,64},{64,0},{128,192},{192,128},{1,65},{65,1},{129,193},{193,129... | collective-permute-start | bytes 2752520 | tf_op jit(solution)/shard_map/ppermute | solution.py:49
  73.4 13.4 %collective-permute-start.10 = (bf16[64,2048]{1,0:T(8,128)(2,1)S(1)}, bf16[64,2048]{1,0:T(8,128)(2,1)S(1)}, u32[]{:S(2)}, u32[]{:S(2)}) collective-permute-start(bf16[64,2048]{1,0:T(8,128)(2,1)S(1)} %select_convert_fusion), channel_id=1, source_target_pairs={{0,2},{2,0},{1,3},{3,1},{4,6},{6,4},{5,7},{7,5},{8,10},{10,8},{9,1... | collective-permute-start | bytes 786440 | tf_op jit(solution)/shard_map/ppermute | solution.py:45
  73.9 23.0 %collective-permute-start.16 = (bf16[448,512]{1,0:T(8,128)(2,1)}, bf16[448,512]{1,0:T(8,128)(2,1)S(1)}, u32[]{:S(2)}, u32[]{:S(2)}) collective-permute-start(bf16[448,512]{1,0:T(8,128)(2,1)} %bitcast.78), channel_id=1, source_target_pairs={{0,48},{16,32},{32,16},{48,0},{1,49},{17,33},{33,17},{49,1},{2,50}... | collective-permute-start | bytes 1376264 | tf_op jit(solution)/shard_map/ppermute | solution.py:53
  91.9 4.0 %collective-permute-start.15 = (f32[2,64]{1,0:T(2,128)S(1)}, f32[2,64]{1,0:T(2,128)S(1)}, u32[]{:S(2)}, u32[]{:S(2)}) collective-permute-start(f32[2,64]{1,0:T(2,128)S(1)} %pad_maximum_fusion.10), channel_id=1, source_target_pairs={{0,12},{4,8},{8,4},{12,0},{1,13},{5,9},{9,5},{13,1},{2,14},{6,10},... | collective-permute-start | bytes 1544 | tf_op jit(solution)/shard_map/ppermute | solution.py:49
  92.4 4.1 %collective-permute-start.14 = (f32[2,64]{1,0:T(2,128)S(1)}, f32[2,64]{1,0:T(2,128)S(1)}, u32[]{:S(2)}, u32[]{:S(2)}) collective-permute-start(f32[2,64]{1,0:T(2,128)S(1)} %pad_maximum_fusion.10), channel_id=1, source_target_pairs={{0,8},{4,12},{8,0},{12,4},{1,9},{5,13},{9,1},{13,5},{2,10},{6,14},... | collective-permute-start | bytes 1544 | tf_op jit(solution)/shard_map/ppermute | solution.py:49
  94.1 2.7 collective-permute-start.13
  97.1 7.7 %collective-permute-start.17 = (bf16[64,896]{1,0:T(8,128)(2,1)S(1)}, bf16[64,896]{1,0:T(8,128)(2,1)S(1)}, u32[]{:S(2)}, u32[]{:S(2)}) collective-permute-start(bf16[64,896]{1,0:T(8,128)(2,1)S(1)} %divide_convert_fusion.1), channel_id=1, source_target_pairs={{0,2},{2,0},{1,3},{3,1},{4,6},{6,4},{5,7},{7,5},{8,10},{10,8},{9,1... | collective-permute-start | bytes 344072 | tf_op jit(solution)/shard_map/ppermute | solution.py:45
  105.5 7.7 %collective-permute-start.18 = (bf16[2,64,896]{2,1,0:T(8,128)(2,1)}, bf16[2,64,896]{2,1,0:T(8,128)(2,1)}, u32[]{:S(2)}, u32[]{:S(2)}) collective-permute-start(bf16[2,64,896]{2,1,0:T(8,128)(2,1)} %pad_maximum_fusion.8), channel_id=1, source_target_pairs={{0,1},{1,0},{2,3},{3,2},{4,5},{5,4},{6,7},{7,6},{8,9},{9,8},{10,11... | collective-permute-start | bytes 688136 | tf_op jit(solution)/shard_map/ppermute | solution.py:45
  111.0 39.3 %collective-permute-start.28 = (bf16[2,448,512]{2,1,0:T(8,128)(2,1)S(1)}, bf16[2,448,512]{2,1,0:T(8,128)(2,1)S(1)}, u32[]{:S(2)}, u32[]{:S(2)}) collective-permute-start(bf16[2,448,512]{2,1,0:T(8,128)(2,1)S(1)} %pad_maximum_fusion.1.refs_12_), channel_id=1, source_target_pairs={{0,64},{64,0},{128,192},{192,128},{1,65},{65,1},{129,193},{193,129... | collective-permute-start | bytes 2752520 | tf_op jit(solution)/shard_map/ppermute | solution.py:49
  111.3 38.9 %collective-permute-start.27 = (bf16[2,448,512]{2,1,0:T(8,128)(2,1)S(1)}, bf16[2,448,512]{2,1,0:T(8,128)(2,1)}, u32[]{:S(2)}, u32[]{:S(2)}) collective-permute-start(bf16[2,448,512]{2,1,0:T(8,128)(2,1)S(1)} %pad_maximum_fusion.1.refs_12_), channel_id=1, source_target_pairs={{0,192},{64,128},{128,64},{192,0},{1,193},{65,129},{129,65},{193,1... | collective-permute-start | bytes 2752520 | tf_op jit(solution)/shard_map/ppermute | solution.py:49
  114.7 4.0 %collective-permute-start.20 = (f32[2,64]{1,0:T(2,128)S(1)}, f32[2,64]{1,0:T(2,128)S(1)}, u32[]{:S(2)}, u32[]{:S(2)}) collective-permute-start(f32[2,64]{1,0:T(2,128)S(1)} %pad_maximum_fusion.11), channel_id=1, source_target_pairs={{0,8},{4,12},{8,0},{12,4},{1,9},{5,13},{9,1},{13,5},{2,10},{6,14},... | collective-permute-start | bytes 1544 | tf_op jit(solution)/shard_map/ppermute | solution.py:49
  116.5 4.0 %collective-permute-start.21 = (f32[2,64]{1,0:T(2,128)S(1)}, f32[2,64]{1,0:T(2,128)S(1)}, u32[]{:S(2)}, u32[]{:S(2)}) collective-permute-start(f32[2,64]{1,0:T(2,128)S(1)} %pad_maximum_fusion.11), channel_id=1, source_target_pairs={{0,12},{4,8},{8,4},{12,0},{1,13},{5,9},{9,5},{13,1},{2,14},{6,10},... | collective-permute-start | bytes 1544 | tf_op jit(solution)/shard_map/ppermute | solution.py:49
  117.5 3.1 %collective-permute-start.19 = (f32[2,64]{1,0:T(2,128)S(1)}, f32[2,64]{1,0:T(2,128)S(1)}, u32[]{:S(2)}, u32[]{:S(2)}) collective-permute-start(f32[2,64]{1,0:T(2,128)S(1)} %pad_maximum_fusion.11), channel_id=1, source_target_pairs={{0,4},{4,0},{8,12},{12,8},{1,5},{5,1},{9,13},{13,9},{2,6},{6,2},{1... | collective-permute-start | bytes 1544 | tf_op jit(solution)/shard_map/ppermute | solution.py:49
  121.2 2.6 collective-permute-start.22
  123.2 34.2 %copy-start.12 = (bf16[2,448,512]{2,1,0:T(8,128)(2,1)S(1)}, bf16[2,448,512]{2,1,0:T(8,128)(2,1)}, u32[]{:S(2)}) copy-start(bf16[2,448,512]{2,1,0:T(8,128)(2,1)} %copy-done.11) | copy-start | bytes 2752516
  123.9 15.9 %collective-permute-start.26 = (bf16[2,128,224]{2,1,0:T(8,128)(2,1)S(1)}, bf16[2,128,224]{2,1,0:T(8,128)(2,1)S(1)}, u32[]{:S(2)}, u32[]{:S(2)}) collective-permute-start(bf16[2,128,224]{2,1,0:T(8,128)(2,1)S(1)} %get-tuple-element.97), channel_id=1, source_target_pairs={{0,34},{1,50},{2,32},{3,48},{4,102},{5,118},{6,100},{7,116},{8,170... | collective-permute-start | bytes 344072 | tf_op jit(solution)/shard_map/ppermute | solution.py:166
  124.6 20.1 %collective-permute-start.25 = (bf16[2,128,224]{2,1,0:T(8,128)(2,1)S(1)}, bf16[2,128,224]{2,1,0:T(8,128)(2,1)S(1)}, u32[]{:S(2)}, u32[]{:S(2)}) collective-permute-start(bf16[2,128,224]{2,1,0:T(8,128)(2,1)S(1)} %get-tuple-element.97), channel_id=1, source_target_pairs={{0,32},{1,48},{2,34},{3,50},{4,100},{5,116},{6,102},{7,118},{8,168... | collective-permute-start | bytes 344072 | tf_op jit(solution)/shard_map/ppermute | solution.py:166
  127.0 23.1 %collective-permute-start.24 = (bf16[2,128,224]{2,1,0:T(8,128)(2,1)S(1)}, bf16[2,128,224]{2,1,0:T(8,128)(2,1)S(1)}, u32[]{:S(2)}, u32[]{:S(2)}) collective-permute-start(bf16[2,128,224]{2,1,0:T(8,128)(2,1)S(1)} %get-tuple-element.98), channel_id=1, source_target_pairs={{0,2},{1,18},{2,0},{3,16},{4,70},{5,86},{6,68},{7,84},{8,138},{9,1... | collective-permute-start | bytes 344072 | tf_op jit(solution)/shard_map/ppermute | solution.py:166
  139.8 10.3 %collective-permute-start.23 = (bf16[2,128,224]{2,1,0:T(8,128)(2,1)S(1)}, bf16[2,128,224]{2,1,0:T(8,128)(2,1)S(1)}, u32[]{:S(2)}, u32[]{:S(2)}) collective-permute-start(bf16[2,128,224]{2,1,0:T(8,128)(2,1)S(1)} %get-tuple-element.98), channel_id=1, source_target_pairs={{0,0},{1,16},{2,2},{3,18},{4,68},{5,84},{6,70},{7,86},{8,136},{9,1... | collective-permute-start | bytes 344072 | tf_op jit(solution)/shard_map/ppermute | solution.py:166
  144.7 38.3 %copy-start.18 = (s32[16]{0:T(128)S(1)}, s32[16]{0:T(128)}, u32[]{:S(2)}) copy-start(s32[16]{0:T(128)} %arrival.1) | copy-start | bytes 196
  144.7 39.0 %copy-start.20 = (s32[16]{0:T(128)S(1)}, s32[16]{0:T(128)}, u32[]{:S(2)}) copy-start(s32[16]{0:T(128)} %param.16) | copy-start | bytes 196
  150.3 34.5 %copy-start.13 = (bf16[2,448,512]{2,1,0:T(8,128)(2,1)}, bf16[2,448,512]{2,1,0:T(8,128)(2,1)S(1)}, u32[]{:S(2)}) copy-start(bf16[2,448,512]{2,1,0:T(8,128)(2,1)S(1)} %collective-permute-done.28.refs_13_) | copy-start | bytes 2752516
  150.3 13.6 %collective-permute-start.33 = (bf16[2,256,224]{2,1,0:T(8,128)(2,1)S(1)}, bf16[2,256,224]{2,1,0:T(8,128)(2,1)S(1)}, u32[]{:S(2)}, u32[]{:S(2)}) collective-permute-start(bf16[2,256,224]{2,1,0:T(8,128)(2,1)S(1)} %bitcast.170), channel_id=1, source_target_pairs={{0,12},{4,8},{8,4},{12,0},{1,13},{5,9},{9,5},{13,1},{2,14},{6,10},... | collective-permute-start | bytes 688136 | tf_op jit(solution)/shard_map/ppermute | solution.py:49
  157.4 23.5 %collective-permute-start.37 = (bf16[2,448,512]{2,1,0:T(8,128)(2,1)S(1)}, bf16[2,448,512]{2,1,0:T(8,128)(2,1)S(1)}, u32[]{:S(2)}, u32[]{:S(2)}) collective-permute-start(bf16[2,448,512]{2,1,0:T(8,128)(2,1)S(1)} %copy-done.12), channel_id=1, source_target_pairs={{0,192},{64,128},{128,64},{192,0},{1,193},{65,129},{129,65},{193,1... | collective-permute-start | bytes 2752520 | tf_op jit(solution)/shard_map/ppermute | solution.py:49
  157.7 8.4 %collective-permute-start.29 = (bf16[2,256,224]{2,1,0:T(8,128)(2,1)S(1)}, bf16[2,256,224]{2,1,0:T(8,128)(2,1)S(1)}, u32[]{:S(2)}, u32[]{:S(2)}) collective-permute-start(bf16[2,256,224]{2,1,0:T(8,128)(2,1)S(1)} %bitcast.172), channel_id=1, source_target_pairs={{0,4},{4,0},{8,12},{12,8},{1,5},{5,1},{9,13},{13,9},{2,6},{6,2},{1... | collective-permute-start | bytes 688136 | tf_op jit(solution)/shard_map/ppermute | solution.py:49
  158.0 26.3 %collective-permute-start.38 = (bf16[2,448,512]{2,1,0:T(8,128)(2,1)}, bf16[2,448,512]{2,1,0:T(8,128)(2,1)}, u32[]{:S(2)}, u32[]{:S(2)}) collective-permute-start(bf16[2,448,512]{2,1,0:T(8,128)(2,1)} %collective-permute-done.27.refs_15_), channel_id=1, source_target_pairs={{0,64},{64,0},{128,192},{192,128},{1,65},{65,1},{129,193},{193,129... | collective-permute-start | bytes 2752520 | tf_op jit(solution)/shard_map/ppermute | solution.py:49
  164.0 20.8 %copy-start.8 = (bf16[2,2,256,224]{3,2,1,0:T(8,128)(2,1)}, bf16[2,2,256,224]{3,2,1,0:T(8,128)(2,1)S(1)}, u32[]{:S(2)}) copy-start(bf16[2,2,256,224]{3,2,1,0:T(8,128)(2,1)S(1)} %pad_maximum_fusion.3.refs_4_) | copy-start | bytes 1376260
  164.0 17.4 %collective-permute-start.34 = (bf16[2,2,256,224]{3,2,1,0:T(8,128)(2,1)S(1)}, bf16[2,2,256,224]{3,2,1,0:T(8,128)(2,1)S(1)}, u32[]{:S(2)}, u32[]{:S(2)}) collective-permute-start(bf16[2,2,256,224]{3,2,1,0:T(8,128)(2,1)S(1)} %pad_maximum_fusion.3.refs_4_), channel_id=1, source_target_pairs={{0,4},{4,0},{8,12},{12,8},{1,5},{5,1},{9,13},{13,9},{2,6},{6,2},{1... | collective-permute-start | bytes 1376264 | tf_op jit(solution)/shard_map/ppermute | solution.py:49
  166.2 18.6 %copy-start.9 = (bf16[2,2,256,224]{3,2,1,0:T(8,128)(2,1)}, bf16[2,2,256,224]{3,2,1,0:T(8,128)(2,1)S(1)}, u32[]{:S(2)}) copy-start(bf16[2,2,256,224]{3,2,1,0:T(8,128)(2,1)S(1)} %pad_maximum_fusion.2.refs_0_) | copy-start | bytes 1376260
  166.2 15.3 %collective-permute-start.30 = (bf16[2,2,256,224]{3,2,1,0:T(8,128)(2,1)S(1)}, bf16[2,2,256,224]{3,2,1,0:T(8,128)(2,1)}, u32[]{:S(2)}, u32[]{:S(2)}) collective-permute-start(bf16[2,2,256,224]{3,2,1,0:T(8,128)(2,1)S(1)} %pad_maximum_fusion.2.refs_0_), channel_id=1, source_target_pairs={{0,12},{4,8},{8,4},{12,0},{1,13},{5,9},{9,5},{13,1},{2,14},{6,10},... | collective-permute-start | bytes 1376264 | tf_op jit(solution)/shard_map/ppermute | solution.py:49
  167.3 17.0 %collective-permute-start.35 = (bf16[2,2,256,224]{3,2,1,0:T(8,128)(2,1)S(1)}, bf16[2,2,256,224]{3,2,1,0:T(8,128)(2,1)}, u32[]{:S(2)}, u32[]{:S(2)}) collective-permute-start(bf16[2,2,256,224]{3,2,1,0:T(8,128)(2,1)S(1)} %pad_maximum_fusion.3.refs_4_), channel_id=1, source_target_pairs={{0,1},{1,0},{2,3},{3,2},{4,5},{5,4},{6,7},{7,6},{8,9},{9,8},{10,11... | collective-permute-start | bytes 1376264 | tf_op jit(solution)/shard_map/ppermute | solution.py:45
  180.9 3.3 %collective-permute-start.31 = (bf16[2,2,256,224]{3,2,1,0:T(8,128)(2,1)S(1)}, bf16[2,2,256,224]{3,2,1,0:T(8,128)(2,1)S(1)}, u32[]{:S(2)}, u32[]{:S(2)}) collective-permute-start(bf16[2,2,256,224]{3,2,1,0:T(8,128)(2,1)S(1)} %pad_maximum_fusion.2.refs_0_), channel_id=1, source_target_pairs={{0,1},{1,0},{2,3},{3,2},{4,5},{5,4},{6,7},{7,6},{8,9},{9,8},{10,11... | collective-permute-start | bytes 1376264 | tf_op jit(solution)/shard_map/ppermute | solution.py:45
  181.4 2.9 %collective-permute-start.36 = (bf16[2,2,256,224]{3,2,1,0:T(8,128)(2,1)S(1)}, bf16[2,2,256,224]{3,2,1,0:T(8,128)(2,1)}, u32[]{:S(2)}, u32[]{:S(2)}) collective-permute-start(bf16[2,2,256,224]{3,2,1,0:T(8,128)(2,1)S(1)} %collective-permute-done.34.refs_5_), channel_id=1, source_target_pairs={{0,1},{1,0},{2,3},{3,2},{4,5},{5,4},{6,7},{7,6},{8,9},{9,8},{10,11... | collective-permute-start | bytes 1376264 | tf_op jit(solution)/shard_map/ppermute | solution.py:45
  181.9 2.9 %collective-permute-start.32 = (bf16[2,2,256,224]{3,2,1,0:T(8,128)(2,1)}, bf16[2,2,256,224]{3,2,1,0:T(8,128)(2,1)}, u32[]{:S(2)}, u32[]{:S(2)}) collective-permute-start(bf16[2,2,256,224]{3,2,1,0:T(8,128)(2,1)} %collective-permute-done.30.refs_1_), channel_id=1, source_target_pairs={{0,1},{1,0},{2,3},{3,2},{4,5},{5,4},{6,7},{7,6},{8,9},{9,8},{10,11... | collective-permute-start | bytes 1376264 | tf_op jit(solution)/shard_map/ppermute | solution.py:45
  (12 other events, 43.6 us)

commit v3 on v2

--- a/solution.py
+++ b/solution.py
@@ -57,30 +57,103 @@
     return lax.dynamic_index_in_dim(array, index, axis, keepdims=False)
 
 
-def forward_kernel(rows_ref, weights_ref, out_ref):
+def forward_kernel(which, rows_ref, features_ref, weights_ref, out_ref, cross_ref):
+    rows = rows_ref[...].reshape(TOK, ROWS)
     out_ref[0] = (
-        jnp.dot(rows_ref[...], weights_ref[...], preferred_element_type=F32)
-        * (1.0 / math.sqrt(FF))
+        jnp.dot(rows, weights_ref[...], preferred_element_type=F32) * (1.0 / math.sqrt(FF))
     ).astype(BF16)
 
-
-def forward(rows, weights):
-    count = rows.shape[0]
+    @pl.when(pl.program_id(0) == 3)
+    def _():
+        cross = lax.dot_general(
+            rows[128:],
+            features_ref[...].reshape(TOK, ROWS),
+            (((1,), (1,)), ((), ())),
+            preferred_element_type=F32,
+        )
+        cross_ref[...] = (cross * (inner_rate / FF)).astype(BF16)
+
+
+def forward(which, features, weights):
+    by_core = features.reshape(ITERS, 2, 2, 64, ROWS)
     return pl.pallas_call(
         forward_kernel,
-        grid=(4,),
-        in_specs=[
-            pl.BlockSpec((count, ROWS), lambda i: (0, 0)),
-            pl.BlockSpec((ROWS, WIDE), lambda i: (0, i)),
+        grid_spec=pltpu.PrefetchScalarGridSpec(
+            num_scalar_prefetch=1,
+            grid=(4,),
+            in_specs=[
+                pl.BlockSpec((ITERS, 2, 1, 64, ROWS), lambda i, which: (0, 0, which[0], 0, 0)),
+                pl.BlockSpec((1, 2, 2, 64, ROWS), lambda i, which: (0, 0, 0, 0, 0)),
+                pl.BlockSpec((ROWS, WIDE), lambda i, which: (0, i)),
+            ],
+            out_specs=[
+                pl.BlockSpec((1, TOK, WIDE), lambda i, which: (i, 0, 0)),
+                pl.BlockSpec((128, TOK), lambda i, which: (0, 0)),
+            ],
+        ),
+        out_shape=[
+            jax.ShapeDtypeStruct((4, TOK, WIDE), BF16),
+            jax.ShapeDtypeStruct((128, TOK), BF16),
         ],
-        out_specs=pl.BlockSpec((1, count, WIDE), lambda i: (i, 0, 0)),
-        out_shape=jax.ShapeDtypeStruct((4, count, WIDE), BF16),
-        cost_estimate=pl.CostEstimate(
-            flops=2 * count * ROWS * D, bytes_accessed=2 * ROWS * D, transcendentals=0
-        ),
         compiler_params=pltpu.CompilerParams(vmem_limit_bytes=32 << 20),
         name="forward",
-    )(rows, weights)
+    )(which.astype(jnp.int32).reshape(1), by_core, by_core, weights)
+
+
+def transpose_kernel(features_ref, out_ref):
+    for i in range(ITERS):
+        block = features_ref[i].astype(F32)
+        out_ref[:, TOK * i : TOK * i + TOK] = jnp.swapaxes(block, 0, 1).astype(BF16)
+
+
+def transpose_features(features):
+    return pl.pallas_call(
+        transpose_kernel,
+        out_shape=jax.ShapeDtypeStruct((ROWS, ITERS * TOK), BF16),
+        compiler_params=pltpu.CompilerParams(vmem_limit_bytes=16 << 20),
+        name="transpose_features",
+    )(features)
+
+
+def divide_kernel(place, residual_ref, target_ref, near_ref, far_ref):
+    for out, index in ((near_ref, place[0]), (far_ref, 1 - place[0])):
+        lanes = pl.ds(pl.multiple_of(128 * index, 128), 128)
+        for i in range(ITERS):
+            out[i] = residual_ref[i, :, lanes]
+            out[ITERS + i] = target_ref[i, :, lanes]
+
+
+def divide(h, residual, target):
+    vmem = pl.BlockSpec(memory_space=pltpu.VMEM)
+    return pl.pallas_call(
+        divide_kernel,
+        in_specs=[pl.BlockSpec(memory_space=pltpu.SMEM), vmem, vmem],
+        out_shape=[jax.ShapeDtypeStruct((2 * ITERS, COLS, 128), BF16)] * 2,
+        compiler_params=pltpu.CompilerParams(vmem_limit_bytes=16 << 20),
+        name="divide",
+    )(h.astype(jnp.int32).reshape(1), residual, target)
+
+
+def turn_kernel(place, near_ref, far_ref, own_ref, give_ref, turned_ref):
+    own = pl.ds(pl.multiple_of(64 * place[0], 64), 64)
+    give = pl.ds(pl.multiple_of(64 * (1 - place[0]), 64), 64)
+    for j, source in enumerate((near_ref, far_ref)):
+        for i in range(2 * ITERS):
+            turned_ref[...] = jnp.swapaxes(source[i].astype(F32), 0, 1)
+            own_ref[j, i] = turned_ref[own].astype(BF16)
+            give_ref[j, i] = turned_ref[give].astype(BF16)
+
+
+def turn(c, near, far):
+    vmem = pl.BlockSpec(memory_space=pltpu.VMEM)
+    return pl.pallas_call(
+        turn_kernel,
+        in_specs=[pl.BlockSpec(memory_space=pltpu.SMEM), vmem, vmem],
+        out_shape=[jax.ShapeDtypeStruct((2, 2 * ITERS, 64, COLS), BF16)] * 2,
+        scratch_shapes=[pltpu.VMEM((128, COLS), F32)],
+        compiler_params=pltpu.CompilerParams(vmem_limit_bytes=16 << 20),
+        name="turn",
+    )(c.astype(jnp.int32).reshape(1), near, far)
 
 
 def after(value, *others):
@@ -121,12 +194,6 @@
     return jnp.concatenate(mine + [extra[64 * half : 64 * half + 64]], axis=1)
 
 
-def turn(near, far, c):
-    both = jnp.stack([near, far])
-    both = jnp.swapaxes(both, 2, 3).reshape(2, 4, 2, 64, COLS)
-    return pick(both, c, 2), pick(both, 1 - c, 2)
-
-
 def features_in_order(own, got, h, c):
     first, low = c == 0, h == 0
     pairs = [jnp.where(first, own, got), jnp.where(first, got, own)]
@@ -196,69 +263,63 @@
 
 
 def outer_kernel(place, position, arrival, factors, slow_ref, held_ref, *refs):
+    rows, refs = refs[:8], refs[8:]
     grads = refs[:8]
-    rows = refs[8:16]
-    out_ref, slow_out, held_out, g_ref, d_ref, s_ref, m_ref, sems = refs[16:]
-    copies = []
-    for part in range(2):
-        for core in range(2):
-            for far in range(2):
-                source = grads[part * 4 + core * 2 + far]
-                for i in range(2):
-                    if part == 0:
-                        mask = (0, 1)[i] ^ (3 * far)
-                    else:
-                        mask = (0, 3)[i] ^ far
-                    copies.append(
-                        pltpu.make_async_copy(
-                            source.at[i], g_ref.at[core, mask, part], sems.at[len(copies)]
-                        )
-                    )
-    for copy in copies:
+    out_ref, slow_out, held_out, h_ref, g_ref, d_ref, s_ref, m_ref, h_sems, g_sems = refs[8:]
+    y, b, a, c, x = (place[i] for i in range(5))
+    grad_copies = []
+    for part, core, far, i in itertools.product(range(2), repeat=4):
+        mask = (0, 1)[i] ^ (3 * far) if part == 0 else (0, 3)[i] ^ far
+        source = grads[part * 4 + core * 2 + far].at[i]
+        target = g_ref.at[core, mask, part]
+        grad_copies.append(pltpu.make_async_copy(source, target, g_sems.at[len(grad_copies)]))
+    for copy in grad_copies:
+        copy.start()
+    order = list(itertools.product(range(2), range(4), range(2)))
+    row_copies = [
+        pltpu.make_async_copy(rows[4 * kb + ky].at[ka], h_ref.at[i], h_sems.at[i])
+        for i, (kb, ky, ka) in enumerate(order)
+    ]
+    for copy in row_copies:
         copy.start()
     s_ref[...] = pack(slow_ref[...])
     m_ref[...] = pack(held_ref[...])
-    for copy in copies:
+    for copy in grad_copies:
         copy.wait()
     scale = inner_rate / math.sqrt(FF)
-    y, b, a, c = place[0], place[1], place[2], place[3]
-    x = place[4]
-    for ky in range(4):
-        for kz in range(4):
-            block = rows[(kz // 2) * 4 + ky].at[kz % 2]
-            ry, rb, ra = y ^ ky, b ^ (kz // 2), a ^ (kz % 2)
-            slot = ry ^ y ^ x
+    for first in range(0, REPLICAS, 4):
+        for i in range(first, first + 4):
+            row_copies[i].wait()
+        for i in range(first, first + 4):
+            kb, ky, ka = order[i]
+            ry, ra = y ^ ky, a ^ ka
             total = jnp.dot(
-                block[:, :TOK], g_ref[ra ^ c, slot, rb ^ b, 0], preferred_element_type=F32
-            ) + jnp.dot(
-                block[:, TOK:], g_ref[ra ^ c, slot, rb ^ b, 1], preferred_element_type=F32
+                h_ref[i],
+                g_ref[ra ^ c, ky ^ x, kb].reshape(ITERS * TOK, COLS),
+                preferred_element_type=F32,
             )
-            d_ref[position[ry * 4 + rb * 2 + ra]] = pack(total * scale)
-
-    def step(k, _):
-        factor = factors[k]
-        target = arrival[k]
-        for at in range(0, PACKED, 112):
-            here = pl.ds(at, 112)
-            grad = d_ref[k, here] * factor
-            held = momentum_decay * m_ref[here] + grad
-            slow = s_ref[here] - outer_rate * (grad + momentum_decay * held)
-            m_ref[here] = held
-            s_ref[here] = slow
-            out_ref[target, here] = slow.astype(BF16)
-        return 0
-
-    lax.fori_loop(0, REPLICAS, step, 0)
+            d_ref[position[ry * 4 + (b ^ kb) * 2 + ra]] = pack(total)
+
+    for at in range(0, PACKED, 112):
+        here = pl.ds(at, 112)
+        slow, held = s_ref[here], m_ref[here]
+        for k in range(REPLICAS):
+            grad = d_ref[k, here] * (factors[k] * scale)
+            held = momentum_decay * held + grad
+            slow = slow - outer_rate * (grad + momentum_decay * held)
+            out_ref[arrival[k], here] = slow.astype(BF16)
+        s_ref[here] = slow
+        m_ref[here] = held
     slow_out[...] = unpack(s_ref[...])
     held_out[...] = unpack(m_ref[...])
 
 
-def outer(place, position, arrival, factors, slow, held, grads, rows):
+def outer(place, position, arrival, factors, slow, held, rows, grads):
     smem = pl.BlockSpec(memory_space=pltpu.SMEM)
     vmem = pl.BlockSpec(memory_space=pltpu.VMEM)
     return pl.pallas_call(
         outer_kernel,
-        in_specs=[smem] * 4 + [vmem] * 2 + [pl.BlockSpec(memory_space=pl.ANY)] * 8 + [vmem] * 8,
+        in_specs=[smem] * 4 + [vmem] * 2 + [pl.BlockSpec(memory_space=pl.ANY)] * 16,
         out_specs=[vmem] * 3,
         out_shape=[
             jax.ShapeDtypeStruct((REPLICAS, PACKED, 128), BF16),
@@ -266,15 +327,17 @@
             jax.ShapeDtypeStruct((ROWS, COLS), F32),
         ],
         scratch_shapes=[
+            pltpu.VMEM((REPLICAS, ROWS, ITERS * TOK), BF16),
             pltpu.VMEM((2, 4, 2, ITERS, TOK, COLS), BF16),
             pltpu.VMEM((REPLICAS, PACKED, 128), F32),
             pltpu.VMEM((PACKED, 128), F32),
             pltpu.VMEM((PACKED, 128), F32),
+            pltpu.SemaphoreType.DMA((REPLICAS,)),
             pltpu.SemaphoreType.DMA((16,)),
         ],
         compiler_params=pltpu.CompilerParams(vmem_limit_bytes=56 << 20),
         name="outer",
-    )(place, position, arrival, factors, slow, held, *grads, *rows)
+    )(place, position, arrival, factors, slow, held, *rows, *grads)
 
 
 def assemble_kernel(in_ref, out_ref):
@@ -300,49 +363,36 @@
     y, b, a, x, h, c = (lax.axis_index(name) for name in AXES)
     weights, features = replica_weights[0], hidden[0]
 
-    by_core = features.reshape(ITERS, 2, 2, 64, ROWS)
-    others = pick(by_core, 1 - c, 2).reshape(TOK, ROWS)
-    mine = pick(by_core, c, 2).reshape(TOK, ROWS)
-    send = forward(others, weights)
-    got = swap(send, "c")
-    keep = forward(after(mine, send), weights)
-
-    by_h = [v.reshape(ITERS, COLS, 2, 128) for v in after((residual[0], target[0]), keep)]
-    far = swap(jnp.concatenate([pick(v, 1 - h, 2) for v in by_h]), "h")
-
-    turned = jnp.transpose(after(features, keep), (2, 0, 1)).reshape(ROWS, ITERS * TOK)
+    turned = transpose_features(features)
     one_z = line(turned, 1)
 
-    cross = [
-        (
-            lax.dot_general(
-                rows[128:], features[0], (((1,), (1,)), ((), ())), preferred_element_type=F32
-            )
-            * (inner_rate / FF)
-        ).astype(BF16)
-        for rows in (mine, others)
-    ]
-    extra = cross[0].astype(F32) + swap(cross[1], "c").astype(F32)
+    send, cross_send = forward(after(1 - c, turned), features, weights)
+    got, cross_got = swap(send, "c"), swap(cross_send, "c")
+    keep, cross_keep = forward(after(c, send), features, weights)
+
+    extra = cross_keep.astype(F32) + cross_got.astype(F32)
     away = split_away(x, keep, got, extra)
     steps = [ring(v, "x", k) for v, k in zip(away, (1, 3))]
     keep, got, extra = after((keep, got, extra), *away)
+
     owns = [
         own_blocks(keep, got, extra, x, half, second) for half, second in zip((0, 1), (3, 1))
     ]
     two_z = line(after(turned, *away), 2)
 
-    steps, one_z, far = lax.optimization_barrier((steps, one_z, far))
+    near, far = divide(h, *after((residual[0], target[0]), owns[0]))
+    far = swap(far, "h")
+    steps, one_z = lax.optimization_barrier((steps, one_z))
     totals = [own + step.astype(F32) for own, step in zip(owns, steps)]
     cut = ITERS * WIDE
     away = [v[:, cut:].astype(BF16) for v in totals]
     steps = [ring(v, "x", k) for v, k in zip(away, (3, 1))]
     upper = jnp.stack([turned, after(one_z, *away)])
-    upper_one, upper_two = ring(upper, "y", 1), ring(upper, "y", 3)
-    near = jnp.concatenate([pick(v, h, 2) for v in after(by_h, *away)])
-    near, give = turn(near, far, c)
+    upper_one, upper_three = ring(upper, "y", 1), ring(upper, "y", 3)
+
+    steps, two_z = lax.optimization_barrier((steps, two_z))
+    near, give = turn(c, near, after(far, *away))
     streams = features_in_order(near, swap(give, "c"), h, c).astype(F32)
-
-    steps, two_z = lax.optimization_barrier((steps, two_z))
     totals = [
         jnp.concatenate([v[:, :cut], v[:, 2 * cut :]], axis=1) + step.astype(F32)
         for v, step in zip(totals, steps)
@@ -351,7 +401,7 @@
     away = jnp.where(low, totals[1], totals[0]).astype(BF16)
     last = swap(away, "h")
     three_z = line(after(turned, away), 3)
-    last, upper_one, upper_two = lax.optimization_barrier((last, upper_one, upper_two))
+    last, upper_one, upper_three = lax.optimization_barrier((last, upper_one, upper_three))
     output = jnp.where(low, totals[0], totals[1]) + last.astype(F32)
     first_output, second_output = output[:, :WIDE], output[:, WIDE : 2 * WIDE]
     cross_rows = output[:, 2 * WIDE :].astype(BF16)
@@ -364,12 +414,12 @@
     summed = streams[0] + first_output
     sums = sums_of(summed, streams[2])
     total = over_ring(sums)
-    upper_both = ring(after(upper_one, sums), "y", 3)
+    upper_two = ring(after(upper_one, sums), "y", 3)
     total, three_z = lax.optimization_barrier((total, three_z))
     first_grad = normal_grad(summed, streams[2], total, token_mask)
+    lower = jnp.stack(after([two_z, three_z], first_grad))
+    lower_three, lower_one = ring(lower, "y", 3), ring(lower, "y", 1)
     by_h = in_order(first_grad, swap(first_grad, "h"), h, 0)
-    lower = jnp.stack(after([two_z, three_z], first_grad))
-    lower_one, lower_two = ring(lower, "y", 3), ring(lower, "y", 1)
     all_first = in_order(by_h, swap(by_h, "c"), c, 1)
     change = jnp.dot(cross_rows, all_first.reshape(TOK, WIDE), preferred_element_type=F32)
     summed = streams[1] + (second_output - change)
@@ -384,16 +434,23 @@
     chunks = jnp.stack([first_chunks, second_chunks]).reshape(ITERS, 128, 2, COLS)
     chunks = jnp.transpose(chunks, (2, 0, 1, 3))
     held = to_owners(chunks, b, h)
-    held, lower_one, lower_two = lax.optimization_barrier((held, lower_one, lower_two))
-    lower_both = ring(lower_one, "y", 1)
+    held, lower_one, lower_three = lax.optimization_barrier((held, lower_one, lower_three))
+    lower_two = ring(lower_three, "y", 1)
     grads = to_all(held)
-    rows = [upper, upper_one, upper_both, upper_two, lower, lower_two, lower_both, lower_one]
-
+
+    slots = jnp.arange(REPLICAS, dtype=jnp.int32)
     position = jnp.sum(jnp.where(arrival[None, :] == slots[:, None], slots[None, :], 0), axis=1)
     factors = 1.0 / (1.0 + staleness.astype(F32))
     place = jnp.stack([y, b, a, c, x]).astype(jnp.int32)
     results, slow_after, momentum_after = outer(
-        place, position.astype(jnp.int32), arrival, factors, slow_weights, momentum, grads, rows
+        place,
+        position.astype(jnp.int32),
+        arrival,
+        factors,
+        slow_weights,
+        momentum,
+        [upper, upper_one, upper_two, upper_three, lower, lower_one, lower_two, lower_three],
+        grads,
     )
     back = lax.all_to_all(results, ("y", "b", "a"), 0, 0, tiled=True)
     return (assemble(back)[None], slow_after, momentum_after)

time: 280 us -> 261 us (0.932)
  other arithmetic: 15.5 us -> 6.65 us
  local copies, waits for them, and re-layouts: 17.8 us -> 11.4 us
  waiting for transfers between devices: 68.6 us -> 65.2 us
    ppermute x12, waiting for transfers between devices: 17.8 us -> 32.8 us  [swap(): return lax.ppermute(value, axis, [(0, 1), (1, 0)])]
    ppermute x3, waiting for transfers between devices: 14.3 us -> 0.01 us  [line(): return lax.ppermute(value, ('b', 'a'), [(i, i ^ mask) for i in range(4)])]
    unnamed x5, other arithmetic: 4.9 us -> 0.24 us
    ppermute x20, waiting for transfers between devices: 31 us -> 27.3 us  [ring(): return lax.ppermute(value, axis, [(i, i ^ mask) for i in range(4)])]
    unnamed x48 -> x46, local copies, waits for them, and re-layouts: 5.89 us -> 9.5 us
    reshape x3 -> x0, local copies, waits for them, and re-layouts: 2.85 us -> none  [the longest x2 2.05 us: local(): v.reshape(ITERS, COLS, 2, 128)]
    pallas_call x2 -> x5, Pallas kernels: 5.13 us -> 6.21 us  [the longest x2 5.67 us: forward(): pl.pallas_call(forward_kernel, grid_spec=pltpu.PrefetchScalarGridSpec(num...]
  transfers between devices with their start and end apart: 39 -> 39, of which waited for: 17 -> 19; matrix products, arithmetic and copies ran while one was open for 10% -> 3% of each run, Pallas kernels for 1% -> 1%
where the time goes in v3:
time: 261 us; the launch traced here: 260 us
  blocking collectives  80.4 us (31%)
  starting transfers between devices  73.3 us (28%)
  waiting for transfers between devices  65.2 us (25%)
  Pallas kernels  21.8 us (8%)
  local copies, waits for them, and re-layouts  11.4 us (4%)
  other arithmetic  6.65 us (3%)
    all_to_all x1, blocking collectives, local(): back = lax.all_to_all(results, ('y', 'b', 'a'), 0, 0, tiled=True)  80.4 us
    ppermute x12, waiting for transfers between devices, swap(): return lax.ppermute(value, axis, [(0, 1), (1, 0)])  32.8 us
    ppermute x20, waiting for transfers between devices, ring(): return lax.ppermute(value, axis, [(i, i ^ mask) for i in range(4)])  27.3 us
    ppermute x20, starting transfers between devices, ring(): return lax.ppermute(value, axis, [(i, i ^ mask) for i in range(4)])  27 us
    ppermute x12, starting transfers between devices, swap(): return lax.ppermute(value, axis, [(0, 1), (1, 0)])  22.5 us
    ppermute x4, starting transfers between devices, to_owners(): part = lax.ppermute(pick(chunks, b ^ m1), AXES, pairs)  20.2 us
    pallas_call x1, Pallas kernels, outer(): pl.pallas_call(outer_kernel, in_specs=[smem] * 4 + [vmem] * 2 + [pl.Block...  12.5 us
    unnamed x46, local copies, waits for them, and re-layouts  9.5 us
  transfers between devices with their start and end apart: 39, of which 19 were waited for; matrix products, arithmetic and copies ran while one was open for 3% of the time, Pallas kernels for 1%

profile of v3, /device:TPU:1, one launch (start us, length us, event | category | flops | bytes accessed | tf_op | source)
XLA Modules:
  0.0 260.5 jit_solution(4185467800805080674)
XLA Ops:
  0.6 1.2 copy.27
  2.1 1.9 copy-done
  4.0 3.3 %forward.2 = (bf16[4,256,896]{2,1,0:T(8,128)(2,1)}, bf16[128,256]{1,0:T(8,128)(2,1)S(1)}) custom-call(s32[1]{0:T(128)} %bitcast.7.which, bf16[2,2,2,64,448]{4,3,2,1,0:T(8,128)(2,1)S(1)} %bitcast.124, bf16[2,2,2,64,448]{4,3,2,1,0:T(8,128)(2,1)S(1)} %bitcast.125, bf16[448,3584]{1,0:T(8,128)(2,1)S(1)} %bitcast.128), custom_call_target="tpu_custom_call" | custom-call | tf_op jit(solution)/shard_map/forward/pallas_call | solution.py:79
  7.3 3.2 %collective-permute-start = (bf16[4,256,896]{2,1,0:T(8,128)(2,1)}, bf16[4,256,896]{2,1,0:T(8,128)(2,1)S(1)}, u32[]{:S(2)}, u32[]{:S(2)}) collective-permute-start(bf16[4,256,896]{2,1,0:T(8,128)(2,1)} %get-tuple-element.47), channel_id=1, source_target_pairs={{0,1},{1,0},{2,3},{3,2},{4,5},{5,4},{6,7},{7,6},{8,9},{9,8},{10,11... | collective-permute-start | bytes 5505032 | tf_op jit(solution)/shard_map/ppermute | solution.py:45
  10.6 1.9 copy-done.1
  12.5 2.3 forward.3
  14.8 1.2 copy-done.2
  16.1 1.5 copy-done.3
  17.8 1.2 collective-permute-start.2
  19.0 1.8 collective-permute-start.3
  20.8 3.0 %collective-permute-start.7 = (bf16[448,512]{1,0:T(8,128)(2,1)S(1)}, bf16[448,512]{1,0:T(8,128)(2,1)S(1)}, u32[]{:S(2)}, u32[]{:S(2)}) collective-permute-start(bf16[448,512]{1,0:T(8,128)(2,1)S(1)} %transpose_features.1), channel_id=1, source_target_pairs={{0,32},{16,48},{32,0},{48,16},{1,33},{17,49},{33,1},{49,17},{2,34}... | collective-permute-start | bytes 1376264 | tf_op jit(solution)/shard_map/ppermute | solution.py:53
  25.0 4.3 %collective-permute-start.11 = (bf16[4,224,128]{2,1,0:T(8,128)(2,1)S(1)}, bf16[4,224,128]{2,1,0:T(8,128)(2,1)S(1)}, u32[]{:S(2)}, u32[]{:S(2)}) collective-permute-start(bf16[4,224,128]{2,1,0:T(8,128)(2,1)S(1)} %get-tuple-element.68), channel_id=1, source_target_pairs={{0,2},{2,0},{1,3},{3,1},{4,6},{6,4},{5,7},{7,5},{8,10},{10,8},{9,1... | collective-permute-start | bytes 688136 | tf_op jit(solution)/shard_map/ppermute | solution.py:45
  30.0 1.9 collective-permute-done.3
  32.1 15.0 %collective-permute-done.11.far_ref = bf16[4,224,128]{2,1,0:T(8,128)(2,1)S(1)} collective-permute-done((bf16[4,224,128]{2,1,0:T(8,128)(2,1)S(1)}, bf16[4,224,128]{2,1,0:T(8,128)(2,1)S(1)}, u32[]{:S(2)}, u32[]{:S(2)}) %collective-permute-start.11) | collective-permute-done | bytes 229408 | tf_op jit(solution)/shard_map/ppermute | solution.py:45
  47.4 2.4 collective-permute-start.12
  51.7 1.1 pad_maximum_fusion.refs_0_
  52.9 2.8 %collective-permute-start.10 = (bf16[2,448,512]{2,1,0:T(8,128)(2,1)S(1)}, bf16[2,448,512]{2,1,0:T(8,128)(2,1)S(1)}, u32[]{:S(2)}, u32[]{:S(2)}) collective-permute-start(bf16[2,448,512]{2,1,0:T(8,128)(2,1)S(1)} %pad_maximum_fusion.refs_0_), channel_id=1, source_target_pairs={{0,192},{64,128},{128,64},{192,0},{1,193},{65,129},{129,65},{193,1... | collective-permute-start | bytes 2752520 | tf_op jit(solution)/shard_map/ppermute | solution.py:49
  55.8 2.5 collective-permute-done.6
  58.3 1.2 collective-permute-done.5
  59.7 1.2 collective-permute-start.8
  61.7 12.5 %collective-permute-done.8 = bf16[64,2048]{1,0:T(8,128)(2,1)S(1)} collective-permute-done((bf16[64,2048]{1,0:T(8,128)(2,1)S(1)}, bf16[64,2048]{1,0:T(8,128)(2,1)S(1)}, u32[]{:S(2)}, u32[]{:S(2)}) %collective-permute-start.8) | collective-permute-done | bytes 262176 | tf_op jit(solution)/shard_map/ppermute | solution.py:45
  74.2 1.5 collective-permute-done.10.refs_3_
  77.1 2.1 collective-permute-start.15
  81.1 1.7 collective-permute-done.16
  82.9 3.0 %collective-permute-start.18 = (bf16[64,896]{1,0:T(8,128)(2,1)S(1)}, bf16[64,896]{1,0:T(8,128)(2,1)S(1)}, u32[]{:S(2)}, u32[]{:S(2)}) collective-permute-start(bf16[64,896]{1,0:T(8,128)(2,1)S(1)} %divide_convert_fusion.1), channel_id=1, source_target_pairs={{0,2},{2,0},{1,3},{3,1},{4,6},{6,4},{5,7},{7,5},{8,10},{10,8},{9,1... | collective-permute-start | bytes 344072 | tf_op jit(solution)/shard_map/ppermute | solution.py:45
  86.0 4.7 %collective-permute-done.18 = bf16[64,896]{1,0:T(8,128)(2,1)S(1)} collective-permute-done((bf16[64,896]{1,0:T(8,128)(2,1)S(1)}, bf16[64,896]{1,0:T(8,128)(2,1)S(1)}, u32[]{:S(2)}, u32[]{:S(2)}) %collective-permute-start.18) | collective-permute-done | bytes 114720 | tf_op jit(solution)/shard_map/ppermute | solution.py:45
  90.8 4.3 %collective-permute-start.19 = (bf16[2,64,896]{2,1,0:T(8,128)(2,1)S(1)}, bf16[2,64,896]{2,1,0:T(8,128)(2,1)S(1)}, u32[]{:S(2)}, u32[]{:S(2)}) collective-permute-start(bf16[2,64,896]{2,1,0:T(8,128)(2,1)S(1)} %pad_maximum_fusion.7), channel_id=1, source_target_pairs={{0,1},{1,0},{2,3},{3,2},{4,5},{5,4},{6,7},{7,6},{8,9},{9,8},{10,11... | collective-permute-start | bytes 688136 | tf_op jit(solution)/shard_map/ppermute | solution.py:45
  95.1 1.1 pad_maximum_fusion.1.refs_4_
  96.2 1.4 collective-permute-start.29
  98.1 1.2 collective-permute-start.21
  102.1 1.2 collective-permute-done.22
  104.0 1.5 collective-permute-start.23
  106.5 1.7 collective-permute-start.27
  108.2 1.7 collective-permute-start.26
  109.9 11.8 %collective-permute-start.25 = (bf16[2,128,224]{2,1,0:T(8,128)(2,1)S(1)}, bf16[2,128,224]{2,1,0:T(8,128)(2,1)S(1)}, u32[]{:S(2)}, u32[]{:S(2)}) collective-permute-start(bf16[2,128,224]{2,1,0:T(8,128)(2,1)S(1)} %get-tuple-element.106), channel_id=1, source_target_pairs={{0,2},{1,18},{2,0},{3,16},{4,70},{5,86},{6,68},{7,84},{8,138},{9,1... | collective-permute-start | bytes 344072 | tf_op jit(solution)/shard_map/ppermute | solution.py:233
  121.7 5.1 %collective-permute-start.24 = (bf16[2,128,224]{2,1,0:T(8,128)(2,1)S(1)}, bf16[2,128,224]{2,1,0:T(8,128)(2,1)S(1)}, u32[]{:S(2)}, u32[]{:S(2)}) collective-permute-start(bf16[2,128,224]{2,1,0:T(8,128)(2,1)S(1)} %get-tuple-element.106), channel_id=1, source_target_pairs={{0,0},{1,16},{2,2},{3,18},{4,68},{5,84},{6,70},{7,86},{8,136},{9,1... | collective-permute-start | bytes 344072 | tf_op jit(solution)/shard_map/ppermute | solution.py:233
  126.9 5.1 %collective-permute-done.25 = bf16[2,128,224]{2,1,0:T(8,128)(2,1)S(1)} collective-permute-done((bf16[2,128,224]{2,1,0:T(8,128)(2,1)S(1)}, bf16[2,128,224]{2,1,0:T(8,128)(2,1)S(1)}, u32[]{:S(2)}, u32[]{:S(2)}) %collective-permute-start.25) | collective-permute-done | bytes 114720 | tf_op jit(solution)/shard_map/ppermute | solution.py:233
  132.1 5.6 %collective-permute-start.35 = (bf16[2,256,224]{2,1,0:T(8,128)(2,1)S(1)}, bf16[2,256,224]{2,1,0:T(8,128)(2,1)S(1)}, u32[]{:S(2)}, u32[]{:S(2)}) collective-permute-start(bf16[2,256,224]{2,1,0:T(8,128)(2,1)S(1)} %bitcast.135), channel_id=1, source_target_pairs={{0,12},{4,8},{8,4},{12,0},{1,13},{5,9},{9,5},{13,1},{2,14},{6,10},... | collective-permute-start | bytes 688136 | tf_op jit(solution)/shard_map/ppermute | solution.py:49
  138.6 1.1 collective-permute-start.31
  139.7 2.1 collective-permute-done.35
  142.0 2.8 %collective-permute-start.36 = (bf16[2,2,256,224]{3,2,1,0:T(8,128)(2,1)S(1)}, bf16[2,2,256,224]{3,2,1,0:T(8,128)(2,1)S(1)}, u32[]{:S(2)}, u32[]{:S(2)}) collective-permute-start(bf16[2,2,256,224]{3,2,1,0:T(8,128)(2,1)S(1)} %pad_maximum_fusion.3.refs_12_), channel_id=1, source_target_pairs={{0,4},{4,0},{8,12},{12,8},{1,5},{5,1},{9,13},{13,9},{2,6},{6,2},{1... | collective-permute-start | bytes 1376264 | tf_op jit(solution)/shard_map/ppermute | solution.py:49
  144.7 1.3 collective-permute-done.31
  146.2 2.5 collective-permute-start.32
  149.7 9.5 %collective-permute-done.13.refs_2_ = bf16[2,448,512]{2,1,0:T(8,128)(2,1)S(1)} collective-permute-done((bf16[2,448,512]{2,1,0:T(8,128)(2,1)S(1)}, bf16[2,448,512]{2,1,0:T(8,128)(2,1)S(1)}, u32[]{:S(2)}, u32[]{:S(2)}) %collective-permute-start.13) | collective-permute-done | bytes 917536 | tf_op jit(solution)/shard_map/ppermute | solution.py:49
  159.6 1.2 collective-permute-done.32.refs_9_
  164.7 12.5 %outer.1 = (bf16[16,784,128]{2,1,0:T(8,128)(2,1)}, f32[448,224]{1,0:T(8,128)}, f32[448,224]{1,0:T(8,128)}) custom-call(s32[5]{0:T(128)} %stack.123.place, s32[16]{0:T(128)} %select_reduce_fusion.position, s32[16]{0:T(128)} %arrival.1, f32[16]{0:T(128)} %add_divide_fusion.factors, f32[448,224]{1,0:T(8,128)} %slow_ref.1, f32[448,224]{1,0:T(8,128)} %held_ref.1, ...), custom_call_target="tpu_custom_call" | custom-call | tf_op jit(solution)/shard_map/outer/pallas_call | solution.py:320
  177.2 80.4 %all_to_all.5.in_ref = bf16[16,784,128]{2,1,0:T(8,128)(2,1)S(1)} all-to-all(bf16[16,784,128]{2,1,0:T(8,128)(2,1)} %get-tuple-element.86), channel_id=1, replica_groups=mesh['y'=4,'b'=2,'a'=2,'x'=4,'h'=2,'c'=2] {'y','b','a'}, dimensions={0} | all-to-all | bytes 6422528 | tf_op jit(solution)/shard_map/all_to_all | solution.py:455
  257.6 2.8 %assemble.1 = bf16[448,3584]{1,0:T(8,128)(2,1)} custom-call(bf16[16,784,128]{2,1,0:T(8,128)(2,1)S(1)} %all_to_all.5.in_ref), custom_call_target="tpu_custom_call" | custom-call | tf_op jit(solution)/shard_map/assemble/pallas_call | solution.py:349
  (143 shorter events, 20.5 us)
Async XLA Ops:
  7.3 8.8 %collective-permute-start = (bf16[4,256,896]{2,1,0:T(8,128)(2,1)}, bf16[4,256,896]{2,1,0:T(8,128)(2,1)S(1)}, u32[]{:S(2)}, u32[]{:S(2)}) collective-permute-start(bf16[4,256,896]{2,1,0:T(8,128)(2,1)} %get-tuple-element.47), channel_id=1, source_target_pairs={{0,1},{1,0},{2,3},{3,2},{4,5},{5,4},{6,7},{7,6},{8,9},{9,8},{10,11... | collective-permute-start | bytes 5505032 | tf_op jit(solution)/shard_map/ppermute | solution.py:45
  10.6 5.5 %collective-permute-start.1 = (bf16[128,256]{1,0:T(8,128)(2,1)S(1)}, bf16[128,256]{1,0:T(8,128)(2,1)S(1)}, u32[]{:S(2)}, u32[]{:S(2)}) collective-permute-start(bf16[128,256]{1,0:T(8,128)(2,1)S(1)} %get-tuple-element.51), channel_id=1, source_target_pairs={{0,1},{1,0},{2,3},{3,2},{4,5},{5,4},{6,7},{7,6},{8,9},{9,8},{10,11... | collective-permute-start | bytes 196616 | tf_op jit(solution)/shard_map/ppermute | solution.py:45
  10.6 18.7 %collective-permute-start.4 = (bf16[448,512]{1,0:T(8,128)(2,1)S(1)}, bf16[448,512]{1,0:T(8,128)(2,1)}, u32[]{:S(2)}, u32[]{:S(2)}) collective-permute-start(bf16[448,512]{1,0:T(8,128)(2,1)S(1)} %transpose_features.1), channel_id=1, source_target_pairs={{0,16},{16,0},{32,48},{48,32},{1,17},{17,1},{33,49},{49,33},{2,18}... | collective-permute-start | bytes 1376264 | tf_op jit(solution)/shard_map/ppermute | solution.py:53
  17.8 12.2 %collective-permute-start.2 = (bf16[64,3840]{1,0:T(8,128)(2,1)S(1)}, bf16[64,3840]{1,0:T(8,128)(2,1)S(1)}, u32[]{:S(2)}, u32[]{:S(2)}) collective-permute-start(bf16[64,3840]{1,0:T(8,128)(2,1)S(1)} %get-tuple-element.52), channel_id=1, source_target_pairs={{0,4},{4,0},{8,12},{12,8},{1,5},{5,1},{9,13},{13,9},{2,6},{6,2},{1... | collective-permute-start | bytes 1474568 | tf_op jit(solution)/shard_map/ppermute | solution.py:49
  19.0 12.9 %collective-permute-start.3 = (bf16[64,3840]{1,0:T(8,128)(2,1)S(1)}, bf16[64,3840]{1,0:T(8,128)(2,1)S(1)}, u32[]{:S(2)}, u32[]{:S(2)}) collective-permute-start(bf16[64,3840]{1,0:T(8,128)(2,1)S(1)} %get-tuple-element.53), channel_id=1, source_target_pairs={{0,12},{4,8},{8,4},{12,0},{1,13},{5,9},{9,5},{13,1},{2,14},{6,10},... | collective-permute-start | bytes 1474568 | tf_op jit(solution)/shard_map/ppermute | solution.py:49
  20.8 35.0 %collective-permute-start.7 = (bf16[448,512]{1,0:T(8,128)(2,1)S(1)}, bf16[448,512]{1,0:T(8,128)(2,1)S(1)}, u32[]{:S(2)}, u32[]{:S(2)}) collective-permute-start(bf16[448,512]{1,0:T(8,128)(2,1)S(1)} %transpose_features.1), channel_id=1, source_target_pairs={{0,32},{16,48},{32,0},{48,16},{1,33},{17,49},{33,1},{49,17},{2,34}... | collective-permute-start | bytes 1376264 | tf_op jit(solution)/shard_map/ppermute | solution.py:53
  25.0 22.2 %collective-permute-start.11 = (bf16[4,224,128]{2,1,0:T(8,128)(2,1)S(1)}, bf16[4,224,128]{2,1,0:T(8,128)(2,1)S(1)}, u32[]{:S(2)}, u32[]{:S(2)}) collective-permute-start(bf16[4,224,128]{2,1,0:T(8,128)(2,1)S(1)} %get-tuple-element.68), channel_id=1, source_target_pairs={{0,2},{2,0},{1,3},{3,1},{4,6},{6,4},{5,7},{7,5},{8,10},{10,8},{9,1... | collective-permute-start | bytes 688136 | tf_op jit(solution)/shard_map/ppermute | solution.py:45
  32.0 17.8 %copy-start.20 = (s32[16]{0:T(128)S(1)}, s32[16]{0:T(128)}, u32[]{:S(2)}) copy-start(s32[16]{0:T(128)} %param.17) | copy-start | bytes 196
  47.4 8.3 %collective-permute-start.12 = (bf16[2,4,64,224]{3,2,1,0:T(8,128)(2,1)S(1)}, bf16[2,4,64,224]{3,2,1,0:T(8,128)(2,1)S(1)}, u32[]{:S(2)}, u32[]{:S(2)}) collective-permute-start(bf16[2,4,64,224]{3,2,1,0:T(8,128)(2,1)S(1)} %get-tuple-element.71), channel_id=1, source_target_pairs={{0,1},{1,0},{2,3},{3,2},{4,5},{5,4},{6,7},{7,6},{8,9},{9,8},{10,11... | collective-permute-start | bytes 688136 | tf_op jit(solution)/shard_map/ppermute | solution.py:45
  50.4 7.9 %collective-permute-start.6 = (bf16[64,2048]{1,0:T(8,128)(2,1)S(1)}, bf16[64,2048]{1,0:T(8,128)(2,1)S(1)}, u32[]{:S(2)}, u32[]{:S(2)}) collective-permute-start(bf16[64,2048]{1,0:T(8,128)(2,1)S(1)} %slice.254), channel_id=1, source_target_pairs={{0,4},{4,0},{8,12},{12,8},{1,5},{5,1},{9,13},{13,9},{2,6},{6,2},{1... | collective-permute-start | bytes 786440 | tf_op jit(solution)/shard_map/ppermute | solution.py:49
  50.7 8.8 %collective-permute-start.5 = (bf16[64,2048]{1,0:T(8,128)(2,1)S(1)}, bf16[64,2048]{1,0:T(8,128)(2,1)S(1)}, u32[]{:S(2)}, u32[]{:S(2)}) collective-permute-start(bf16[64,2048]{1,0:T(8,128)(2,1)S(1)} %slice.255), channel_id=1, source_target_pairs={{0,12},{4,8},{8,4},{12,0},{1,13},{5,9},{9,5},{13,1},{2,14},{6,10},... | collective-permute-start | bytes 786440 | tf_op jit(solution)/shard_map/ppermute | solution.py:49
  52.8 6.8 %copy-start.6 = (bf16[2,448,512]{2,1,0:T(8,128)(2,1)}, bf16[2,448,512]{2,1,0:T(8,128)(2,1)S(1)}, u32[]{:S(2)}) copy-start(bf16[2,448,512]{2,1,0:T(8,128)(2,1)S(1)} %pad_maximum_fusion.refs_0_) | copy-start | bytes 2752516
  52.9 22.8 %collective-permute-start.10 = (bf16[2,448,512]{2,1,0:T(8,128)(2,1)S(1)}, bf16[2,448,512]{2,1,0:T(8,128)(2,1)S(1)}, u32[]{:S(2)}, u32[]{:S(2)}) collective-permute-start(bf16[2,448,512]{2,1,0:T(8,128)(2,1)S(1)} %pad_maximum_fusion.refs_0_), channel_id=1, source_target_pairs={{0,192},{64,128},{128,64},{192,0},{1,193},{65,129},{129,65},{193,1... | collective-permute-start | bytes 2752520 | tf_op jit(solution)/shard_map/ppermute | solution.py:49
  55.8 21.0 %collective-permute-start.9 = (bf16[2,448,512]{2,1,0:T(8,128)(2,1)S(1)}, bf16[2,448,512]{2,1,0:T(8,128)(2,1)S(1)}, u32[]{:S(2)}, u32[]{:S(2)}) collective-permute-start(bf16[2,448,512]{2,1,0:T(8,128)(2,1)S(1)} %pad_maximum_fusion.refs_0_), channel_id=1, source_target_pairs={{0,64},{64,0},{128,192},{192,128},{1,65},{65,1},{129,193},{193,129... | collective-permute-start | bytes 2752520 | tf_op jit(solution)/shard_map/ppermute | solution.py:49
  59.7 14.6 %collective-permute-start.8 = (bf16[64,2048]{1,0:T(8,128)(2,1)S(1)}, bf16[64,2048]{1,0:T(8,128)(2,1)S(1)}, u32[]{:S(2)}, u32[]{:S(2)}) collective-permute-start(bf16[64,2048]{1,0:T(8,128)(2,1)S(1)} %select_convert_fusion), channel_id=1, source_target_pairs={{0,2},{2,0},{1,3},{3,1},{4,6},{6,4},{5,7},{7,5},{8,10},{10,8},{9,1... | collective-permute-start | bytes 786440 | tf_op jit(solution)/shard_map/ppermute | solution.py:45
  61.2 21.6 %collective-permute-start.17 = (bf16[448,512]{1,0:T(8,128)(2,1)S(1)}, bf16[448,512]{1,0:T(8,128)(2,1)S(1)}, u32[]{:S(2)}, u32[]{:S(2)}) collective-permute-start(bf16[448,512]{1,0:T(8,128)(2,1)S(1)} %transpose_features.1), channel_id=1, source_target_pairs={{0,48},{16,32},{32,16},{48,0},{1,49},{17,33},{33,17},{49,1},{2,50}... | collective-permute-start | bytes 1376264 | tf_op jit(solution)/shard_map/ppermute | solution.py:53
  75.7 7.2 %copy-start.10 = (bf16[2,448,512]{2,1,0:T(8,128)(2,1)}, bf16[2,448,512]{2,1,0:T(8,128)(2,1)S(1)}, u32[]{:S(2)}) copy-start(bf16[2,448,512]{2,1,0:T(8,128)(2,1)S(1)} %collective-permute-done.10.refs_3_) | copy-start | bytes 2752516
  76.8 6.2 %copy-start.11 = (bf16[2,448,512]{2,1,0:T(8,128)(2,1)}, bf16[2,448,512]{2,1,0:T(8,128)(2,1)S(1)}, u32[]{:S(2)}) copy-start(bf16[2,448,512]{2,1,0:T(8,128)(2,1)S(1)} %collective-permute-done.9.refs_1_) | copy-start | bytes 2752516
  77.1 4.0 %collective-permute-start.15 = (f32[2,64]{1,0:T(2,128)S(1)}, f32[2,64]{1,0:T(2,128)S(1)}, u32[]{:S(2)}, u32[]{:S(2)}) collective-permute-start(f32[2,64]{1,0:T(2,128)S(1)} %pad_maximum_fusion.9), channel_id=1, source_target_pairs={{0,8},{4,12},{8,0},{12,4},{1,9},{5,13},{9,1},{13,5},{2,10},{6,14},... | collective-permute-start | bytes 1544 | tf_op jit(solution)/shard_map/ppermute | solution.py:49
  79.1 3.6 %collective-permute-start.16 = (f32[2,64]{1,0:T(2,128)S(1)}, f32[2,64]{1,0:T(2,128)S(1)}, u32[]{:S(2)}, u32[]{:S(2)}) collective-permute-start(f32[2,64]{1,0:T(2,128)S(1)} %pad_maximum_fusion.9), channel_id=1, source_target_pairs={{0,12},{4,8},{8,4},{12,0},{1,13},{5,9},{9,5},{13,1},{2,14},{6,10},... | collective-permute-start | bytes 1544 | tf_op jit(solution)/shard_map/ppermute | solution.py:49
  80.0 2.8 %collective-permute-start.14 = (f32[2,64]{1,0:T(2,128)S(1)}, f32[2,64]{1,0:T(2,128)S(1)}, u32[]{:S(2)}, u32[]{:S(2)}) collective-permute-start(f32[2,64]{1,0:T(2,128)S(1)} %pad_maximum_fusion.9), channel_id=1, source_target_pairs={{0,4},{4,0},{8,12},{12,8},{1,5},{5,1},{9,13},{13,9},{2,6},{6,2},{1... | collective-permute-start | bytes 1544 | tf_op jit(solution)/shard_map/ppermute | solution.py:49
  82.9 7.7 %collective-permute-start.18 = (bf16[64,896]{1,0:T(8,128)(2,1)S(1)}, bf16[64,896]{1,0:T(8,128)(2,1)S(1)}, u32[]{:S(2)}, u32[]{:S(2)}) collective-permute-start(bf16[64,896]{1,0:T(8,128)(2,1)S(1)} %divide_convert_fusion.1), channel_id=1, source_target_pairs={{0,2},{2,0},{1,3},{3,1},{4,6},{6,4},{5,7},{7,5},{8,10},{10,8},{9,1... | collective-permute-start | bytes 344072 | tf_op jit(solution)/shard_map/ppermute | solution.py:45
  90.8 6.8 %collective-permute-start.19 = (bf16[2,64,896]{2,1,0:T(8,128)(2,1)S(1)}, bf16[2,64,896]{2,1,0:T(8,128)(2,1)S(1)}, u32[]{:S(2)}, u32[]{:S(2)}) collective-permute-start(bf16[2,64,896]{2,1,0:T(8,128)(2,1)S(1)} %pad_maximum_fusion.7), channel_id=1, source_target_pairs={{0,1},{1,0},{2,3},{3,2},{4,5},{5,4},{6,7},{7,6},{8,9},{9,8},{10,11... | collective-permute-start | bytes 688136 | tf_op jit(solution)/shard_map/ppermute | solution.py:45
  96.2 35.9 %collective-permute-start.29 = (bf16[2,448,512]{2,1,0:T(8,128)(2,1)S(1)}, bf16[2,448,512]{2,1,0:T(8,128)(2,1)}, u32[]{:S(2)}, u32[]{:S(2)}) collective-permute-start(bf16[2,448,512]{2,1,0:T(8,128)(2,1)S(1)} %pad_maximum_fusion.1.refs_4_), channel_id=1, source_target_pairs={{0,192},{64,128},{128,64},{192,0},{1,193},{65,129},{129,65},{193,1... | collective-permute-start | bytes 2752520 | tf_op jit(solution)/shard_map/ppermute | solution.py:49
  97.6 34.5 %collective-permute-start.28 = (bf16[2,448,512]{2,1,0:T(8,128)(2,1)S(1)}, bf16[2,448,512]{2,1,0:T(8,128)(2,1)}, u32[]{:S(2)}, u32[]{:S(2)}) collective-permute-start(bf16[2,448,512]{2,1,0:T(8,128)(2,1)S(1)} %pad_maximum_fusion.1.refs_4_), channel_id=1, source_target_pairs={{0,64},{64,0},{128,192},{192,128},{1,65},{65,1},{129,193},{193,129... | collective-permute-start | bytes 2752520 | tf_op jit(solution)/shard_map/ppermute | solution.py:49
  98.1 4.0 %collective-permute-start.21 = (f32[2,64]{1,0:T(2,128)S(1)}, f32[2,64]{1,0:T(2,128)S(1)}, u32[]{:S(2)}, u32[]{:S(2)}) collective-permute-start(f32[2,64]{1,0:T(2,128)S(1)} %pad_maximum_fusion.10), channel_id=1, source_target_pairs={{0,8},{4,12},{8,0},{12,4},{1,9},{5,13},{9,1},{13,5},{2,10},{6,14},... | collective-permute-start | bytes 1544 | tf_op jit(solution)/shard_map/ppermute | solution.py:49
  99.3 4.0 %collective-permute-start.22 = (f32[2,64]{1,0:T(2,128)S(1)}, f32[2,64]{1,0:T(2,128)S(1)}, u32[]{:S(2)}, u32[]{:S(2)}) collective-permute-start(f32[2,64]{1,0:T(2,128)S(1)} %pad_maximum_fusion.10), channel_id=1, source_target_pairs={{0,12},{4,8},{8,4},{12,0},{1,13},{5,9},{9,5},{13,1},{2,14},{6,10},... | collective-permute-start | bytes 1544 | tf_op jit(solution)/shard_map/ppermute | solution.py:49
  100.3 3.0 %collective-permute-start.20 = (f32[2,64]{1,0:T(2,128)S(1)}, f32[2,64]{1,0:T(2,128)S(1)}, u32[]{:S(2)}, u32[]{:S(2)}) collective-permute-start(f32[2,64]{1,0:T(2,128)S(1)} %pad_maximum_fusion.10), channel_id=1, source_target_pairs={{0,4},{4,0},{8,12},{12,8},{1,5},{5,1},{9,13},{13,9},{2,6},{6,2},{1... | collective-permute-start | bytes 1544 | tf_op jit(solution)/shard_map/ppermute | solution.py:49
  104.0 2.5 collective-permute-start.23
  105.8 31.9 %copy-start.12 = (bf16[2,448,512]{2,1,0:T(8,128)(2,1)S(1)}, bf16[2,448,512]{2,1,0:T(8,128)(2,1)}, u32[]{:S(2)}) copy-start(bf16[2,448,512]{2,1,0:T(8,128)(2,1)} %copy-done.11) | copy-start | bytes 2752516
  106.5 15.2 %collective-permute-start.27 = (bf16[2,128,224]{2,1,0:T(8,128)(2,1)S(1)}, bf16[2,128,224]{2,1,0:T(8,128)(2,1)S(1)}, u32[]{:S(2)}, u32[]{:S(2)}) collective-permute-start(bf16[2,128,224]{2,1,0:T(8,128)(2,1)S(1)} %get-tuple-element.105), channel_id=1, source_target_pairs={{0,34},{1,50},{2,32},{3,48},{4,102},{5,118},{6,100},{7,116},{8,170... | collective-permute-start | bytes 344072 | tf_op jit(solution)/shard_map/ppermute | solution.py:233
  108.2 18.6 %collective-permute-start.26 = (bf16[2,128,224]{2,1,0:T(8,128)(2,1)S(1)}, bf16[2,128,224]{2,1,0:T(8,128)(2,1)S(1)}, u32[]{:S(2)}, u32[]{:S(2)}) collective-permute-start(bf16[2,128,224]{2,1,0:T(8,128)(2,1)S(1)} %get-tuple-element.105), channel_id=1, source_target_pairs={{0,32},{1,48},{2,34},{3,50},{4,100},{5,116},{6,102},{7,118},{8,168... | collective-permute-start | bytes 344072 | tf_op jit(solution)/shard_map/ppermute | solution.py:233
  109.9 22.1 %collective-permute-start.25 = (bf16[2,128,224]{2,1,0:T(8,128)(2,1)S(1)}, bf16[2,128,224]{2,1,0:T(8,128)(2,1)S(1)}, u32[]{:S(2)}, u32[]{:S(2)}) collective-permute-start(bf16[2,128,224]{2,1,0:T(8,128)(2,1)S(1)} %get-tuple-element.106), channel_id=1, source_target_pairs={{0,2},{1,18},{2,0},{3,16},{4,70},{5,86},{6,68},{7,84},{8,138},{9,1... | collective-permute-start | bytes 344072 | tf_op jit(solution)/shard_map/ppermute | solution.py:233
  121.7 10.3 %collective-permute-start.24 = (bf16[2,128,224]{2,1,0:T(8,128)(2,1)S(1)}, bf16[2,128,224]{2,1,0:T(8,128)(2,1)S(1)}, u32[]{:S(2)}, u32[]{:S(2)}) collective-permute-start(bf16[2,128,224]{2,1,0:T(8,128)(2,1)S(1)} %get-tuple-element.106), channel_id=1, source_target_pairs={{0,0},{1,16},{2,2},{3,18},{4,68},{5,84},{6,70},{7,86},{8,136},{9,1... | collective-permute-start | bytes 344072 | tf_op jit(solution)/shard_map/ppermute | solution.py:233
  126.8 35.7 %copy-start.19 = (s32[16]{0:T(128)S(1)}, s32[16]{0:T(128)}, u32[]{:S(2)}) copy-start(s32[16]{0:T(128)} %arrival.1) | copy-start | bytes 196
  126.9 36.3 %copy-start.21 = (s32[16]{0:T(128)S(1)}, s32[16]{0:T(128)}, u32[]{:S(2)}) copy-start(s32[16]{0:T(128)} %param.16) | copy-start | bytes 196
  132.1 9.7 %collective-permute-start.35 = (bf16[2,256,224]{2,1,0:T(8,128)(2,1)S(1)}, bf16[2,256,224]{2,1,0:T(8,128)(2,1)S(1)}, u32[]{:S(2)}, u32[]{:S(2)}) collective-permute-start(bf16[2,256,224]{2,1,0:T(8,128)(2,1)S(1)} %bitcast.135), channel_id=1, source_target_pairs={{0,12},{4,8},{8,4},{12,0},{1,13},{5,9},{9,5},{13,1},{2,14},{6,10},... | collective-permute-start | bytes 688136 | tf_op jit(solution)/shard_map/ppermute | solution.py:49
  137.7 21.4 %collective-permute-start.13 = (bf16[2,448,512]{2,1,0:T(8,128)(2,1)S(1)}, bf16[2,448,512]{2,1,0:T(8,128)(2,1)S(1)}, u32[]{:S(2)}, u32[]{:S(2)}) collective-permute-start(bf16[2,448,512]{2,1,0:T(8,128)(2,1)S(1)} %copy-done.12), channel_id=1, source_target_pairs={{0,192},{64,128},{128,64},{192,0},{1,193},{65,129},{129,65},{193,1... | collective-permute-start | bytes 2752520 | tf_op jit(solution)/shard_map/ppermute | solution.py:49
  138.6 7.5 %collective-permute-start.31 = (bf16[2,256,224]{2,1,0:T(8,128)(2,1)S(1)}, bf16[2,256,224]{2,1,0:T(8,128)(2,1)S(1)}, u32[]{:S(2)}, u32[]{:S(2)}) collective-permute-start(bf16[2,256,224]{2,1,0:T(8,128)(2,1)S(1)} %bitcast.137), channel_id=1, source_target_pairs={{0,4},{4,0},{8,12},{12,8},{1,5},{5,1},{9,13},{13,9},{2,6},{6,2},{1... | collective-permute-start | bytes 688136 | tf_op jit(solution)/shard_map/ppermute | solution.py:49
  139.7 24.0 %collective-permute-start.30 = (bf16[2,448,512]{2,1,0:T(8,128)(2,1)}, bf16[2,448,512]{2,1,0:T(8,128)(2,1)}, u32[]{:S(2)}, u32[]{:S(2)}) collective-permute-start(bf16[2,448,512]{2,1,0:T(8,128)(2,1)} %collective-permute-done.29.refs_7_), channel_id=1, source_target_pairs={{0,64},{64,0},{128,192},{192,128},{1,65},{65,1},{129,193},{193,129... | collective-permute-start | bytes 2752520 | tf_op jit(solution)/shard_map/ppermute | solution.py:49
  141.9 21.8 %copy-start.8 = (bf16[2,2,256,224]{3,2,1,0:T(8,128)(2,1)}, bf16[2,2,256,224]{3,2,1,0:T(8,128)(2,1)S(1)}, u32[]{:S(2)}) copy-start(bf16[2,2,256,224]{3,2,1,0:T(8,128)(2,1)S(1)} %pad_maximum_fusion.3.refs_12_) | copy-start | bytes 1376260
  142.0 17.2 %collective-permute-start.36 = (bf16[2,2,256,224]{3,2,1,0:T(8,128)(2,1)S(1)}, bf16[2,2,256,224]{3,2,1,0:T(8,128)(2,1)S(1)}, u32[]{:S(2)}, u32[]{:S(2)}) collective-permute-start(bf16[2,2,256,224]{3,2,1,0:T(8,128)(2,1)S(1)} %pad_maximum_fusion.3.refs_12_), channel_id=1, source_target_pairs={{0,4},{4,0},{8,12},{12,8},{1,5},{5,1},{9,13},{13,9},{2,6},{6,2},{1... | collective-permute-start | bytes 1376264 | tf_op jit(solution)/shard_map/ppermute | solution.py:49
  146.2 17.6 %copy-start.9 = (bf16[2,2,256,224]{3,2,1,0:T(8,128)(2,1)}, bf16[2,2,256,224]{3,2,1,0:T(8,128)(2,1)S(1)}, u32[]{:S(2)}) copy-start(bf16[2,2,256,224]{3,2,1,0:T(8,128)(2,1)S(1)} %pad_maximum_fusion.2.refs_8_) | copy-start | bytes 1376260
  146.2 14.7 %collective-permute-start.32 = (bf16[2,2,256,224]{3,2,1,0:T(8,128)(2,1)S(1)}, bf16[2,2,256,224]{3,2,1,0:T(8,128)(2,1)S(1)}, u32[]{:S(2)}, u32[]{:S(2)}) collective-permute-start(bf16[2,2,256,224]{3,2,1,0:T(8,128)(2,1)S(1)} %pad_maximum_fusion.2.refs_8_), channel_id=1, source_target_pairs={{0,12},{4,8},{8,4},{12,0},{1,13},{5,9},{9,5},{13,1},{2,14},{6,10},... | collective-permute-start | bytes 1376264 | tf_op jit(solution)/shard_map/ppermute | solution.py:49
  148.7 15.0 %collective-permute-start.37 = (bf16[2,2,256,224]{3,2,1,0:T(8,128)(2,1)S(1)}, bf16[2,2,256,224]{3,2,1,0:T(8,128)(2,1)}, u32[]{:S(2)}, u32[]{:S(2)}) collective-permute-start(bf16[2,2,256,224]{3,2,1,0:T(8,128)(2,1)S(1)} %pad_maximum_fusion.3.refs_12_), channel_id=1, source_target_pairs={{0,1},{1,0},{2,3},{3,2},{4,5},{5,4},{6,7},{7,6},{8,9},{9,8},{10,11... | collective-permute-start | bytes 1376264 | tf_op jit(solution)/shard_map/ppermute | solution.py:45
  159.1 4.6 %collective-permute-start.33 = (bf16[2,2,256,224]{3,2,1,0:T(8,128)(2,1)S(1)}, bf16[2,2,256,224]{3,2,1,0:T(8,128)(2,1)S(1)}, u32[]{:S(2)}, u32[]{:S(2)}) collective-permute-start(bf16[2,2,256,224]{3,2,1,0:T(8,128)(2,1)S(1)} %pad_maximum_fusion.2.refs_8_), channel_id=1, source_target_pairs={{0,1},{1,0},{2,3},{3,2},{4,5},{5,4},{6,7},{7,6},{8,9},{9,8},{10,11... | collective-permute-start | bytes 1376264 | tf_op jit(solution)/shard_map/ppermute | solution.py:45
  159.1 4.6 %collective-permute-start.38 = (bf16[2,2,256,224]{3,2,1,0:T(8,128)(2,1)S(1)}, bf16[2,2,256,224]{3,2,1,0:T(8,128)(2,1)S(1)}, u32[]{:S(2)}, u32[]{:S(2)}) collective-permute-start(bf16[2,2,256,224]{3,2,1,0:T(8,128)(2,1)S(1)} %collective-permute-done.36.refs_13_), channel_id=1, source_target_pairs={{0,1},{1,0},{2,3},{3,2},{4,5},{5,4},{6,7},{7,6},{8,9},{9,8},{10,11... | collective-permute-start | bytes 1376264 | tf_op jit(solution)/shard_map/ppermute | solution.py:45
  160.9 2.9 %collective-permute-start.34 = (bf16[2,2,256,224]{3,2,1,0:T(8,128)(2,1)S(1)}, bf16[2,2,256,224]{3,2,1,0:T(8,128)(2,1)}, u32[]{:S(2)}, u32[]{:S(2)}) collective-permute-start(bf16[2,2,256,224]{3,2,1,0:T(8,128)(2,1)S(1)} %collective-permute-done.32.refs_9_), channel_id=1, source_target_pairs={{0,1},{1,0},{2,3},{3,2},{4,5},{5,4},{6,7},{7,6},{8,9},{9,8},{10,11... | collective-permute-start | bytes 1376264 | tf_op jit(solution)/shard_map/ppermute | solution.py:45
  (13 other events, 24.7 us)
